TPU v7x, 256 devices: a whole 4x4x8 slice. The times are simulated.
256 devices in a mesh: seq: 32 (over z, x), tp: 8 (over y, core).
Axes of the slice: x: 4, y: 4, z: 8, core: 2. Of those that a mesh axis runs over, the one named last changes fastest.
Arguments:
- x_in: bfloat16 [8192, 16384], P('seq', 'tp'), may hold values from -6 to 6
- bc_in: bfloat16 [8192, 8, 512], P('seq', 'tp'), may hold values from -6 to 6
- gate_in: bfloat16 [8192, 16384], P('seq', 'tp'), may hold values from -6 to 6
- dt_raw: float32 [8192, 256], P('seq', 'tp'), may hold values from -5 to 2
- decay_rate: float32 [256], P('tp'), may hold values from 0 to 2, as said below
- skip_gain: float32 [256], P('tp'), may hold values from 0.5 to 1.5
- conv_x: float32 [4, 16384], P(None, 'tp'), may hold values from -3 to 3
- conv_bc: float32 [4, 8, 512], P(None, 'tp'), may hold values from -3 to 3
- norm_gain: float32 [16384], P('tp'), may hold values from 0.1 to 1.9
- out_weight: bfloat16 [16384, 4096], P('tp', 'seq'), may hold values from -0.09375 to 0.09375
- lengths: int32 [4], replicated, may hold values from 1 to 4096, as said below
Outputs:
- mixed: bfloat16 [8192, 4096], P('seq', 'tp')
Inputs may be any that keep to these rules, and one draw needn't show every extreme that they name: The lengths sum to 8192; the second is exactly 4096 and the first is more than 256 and at most 2048. `decay_rate`: positive.
All inputs are finite; a program needn't handle non-finite values.
Results may differ from a plain program's by a relative error of at most 0.02.
Values may be sent and summed in bfloat16 or wider, within the bound.
No kernel may reach another device: no remote copies, remote signals or barrier semaphores. Data moves between devices by JAX's collectives and lax.ppermute only.
A program may use at most 192 MiB of HBM per device.

v0:
```python
import jax
import jax.numpy as jnp
from jax import lax
from jax.sharding import PartitionSpec as P

SPAN = 256


def from_behind(x, axis, by):
    peers = lax.axis_size(axis)
    pairs = [(i, i + by) for i in range(peers) if 0 <= i + by < peers]
    return lax.ppermute(x, axis, pairs)


def prefix(x, axis, combine, identity):
    peers, index = (lax.axis_size(axis), lax.axis_index(axis))
    everything = jax.tree.map(
        lambda part, kind: lax.all_gather(part.astype(kind), axis), x, (jnp.bfloat16, jnp.bfloat16)
    )
    start = jax.tree.map(
        lambda part, zero: jnp.broadcast_to(jnp.asarray(zero, part.dtype), part.shape), x, identity
    )

    def turn(k, before):
        reached = k < index
        new = combine(
            before, jax.tree.map(lambda part, own: part[k].astype(own.dtype), everything, x)
        )
        return jax.tree.map(lambda a, b: jnp.where(reached, a, b), new, before)

    return lax.fori_loop(0, peers, turn, start)


def on_device(
    x_in,
    bc_in,
    gate_in,
    dt_raw,
    decay_rate,
    skip_gain,
    conv_x,
    conv_bc,
    norm_gain,
    out_weight,
    lengths,
):
    rows, inner_loc = x_in.shape
    groups_loc = bc_in.shape[1]
    state = bc_in.shape[2] // 2
    heads_loc = dt_raw.shape[1]
    head_dim = inner_loc // heads_loc
    per_group = heads_loc // groups_loc
    kernel = conv_x.shape[0]
    blocks = rows // SPAN
    row_start = lax.axis_index("seq") * rows
    places = row_start + jnp.arange(rows, dtype=jnp.int32)
    starts = jnp.cumsum(lengths) - lengths
    first = jnp.max(jnp.where(starts[None, :] <= places[:, None], starts[None, :], 0), axis=1)
    tail_x, tail_bc = from_behind((x_in[rows - kernel + 1 :], bc_in[rows - kernel + 1 :]), "seq", 1)
    ext_x = jnp.concatenate([tail_x, x_in], axis=0)
    ext_bc = jnp.concatenate([tail_bc, bc_in], axis=0)
    acc_x = jnp.zeros((rows, inner_loc), jnp.float32)
    acc_bc = jnp.zeros(bc_in.shape, jnp.float32)
    for offset in range(kernel):
        usable = places - kernel + 1 + offset >= first
        acc_x = acc_x + jnp.where(
            usable[:, None],
            conv_x[offset][None, :] * ext_x[offset : offset + rows].astype(jnp.float32),
            0.0,
        )
        acc_bc = acc_bc + jnp.where(
            usable[:, None, None],
            conv_bc[offset][None] * ext_bc[offset : offset + rows].astype(jnp.float32),
            0.0,
        )
    conv_out = jax.nn.silu(acc_x).astype(jnp.bfloat16)
    bc_out = jax.nn.silu(acc_bc).astype(jnp.bfloat16)
    step_size = jax.nn.softplus(dt_raw)
    rate = -decay_rate[None, :] * step_size
    xheads = conv_out.reshape(blocks, SPAN, groups_loc, per_group, head_dim)
    keys_b = bc_out[:, :, :state].reshape(blocks, SPAN, groups_loc, state)
    query_c = bc_out[:, :, state:].reshape(blocks, SPAN, groups_loc, state)
    logdec = jnp.cumsum(rate.reshape(blocks, SPAN, heads_loc), axis=1)
    step_blocks = step_size.reshape(blocks, SPAN, heads_loc)
    place_b = places.reshape(blocks, SPAN)
    first_b = first.reshape(blocks, SPAN)
    intersection = jnp.einsum(
        "bqgn,bsgn->bgqs", query_c, keys_b, preferred_element_type=jnp.float32
    )
    causal = (place_b[:, None, :] <= place_b[:, :, None]) & (
        place_b[:, None, :] >= first_b[:, :, None]
    )
    log_t = jnp.swapaxes(logdec, 1, 2)
    spread = jnp.exp(
        jnp.where(causal[:, None], log_t[:, :, :, None] - log_t[:, :, None, :], -jnp.inf)
    )
    spread = spread * jnp.swapaxes(step_blocks, 1, 2)[:, :, None, :]
    mixing = (
        intersection[:, :, None] * spread.reshape(blocks, groups_loc, per_group, SPAN, SPAN)
    ).astype(jnp.bfloat16)
    within = jnp.einsum("bgjqs,bsgjp->bqgjp", mixing, xheads, preferred_element_type=jnp.float32)
    log_end = logdec[:, -1, :]
    first_end = first_b[:, -1]
    keep = place_b >= first_end[:, None]
    weight_u = jnp.where(keep[:, :, None], jnp.exp(log_end[:, None, :] - logdec) * step_blocks, 0.0)
    inputs_u = (weight_u.reshape(blocks, SPAN, groups_loc, per_group)[..., None] * xheads).astype(
        jnp.bfloat16
    )
    local_states = jnp.einsum(
        "bqgjp,bqgn->bgjpn", inputs_u, keys_b, preferred_element_type=jnp.float32
    )
    carried = jnp.exp(log_end) * (first_end <= place_b[:, 0] - 1).astype(jnp.float32)[:, None]
    carried = carried.reshape(blocks, groups_loc, per_group)
    prior = jnp.zeros(local_states.shape[1:], jnp.float32)
    total = jnp.ones(carried.shape[1:], jnp.float32)
    befores = [prior]
    factors = [total]
    prior = carried[0][..., None, None] * prior + local_states[0]
    total = carried[0] * total

    def combine(earlier, later):
        return (earlier[0] * later[0], later[0][..., None, None] * earlier[1] + later[1])

    enter_decay, enter_state = prefix(
        (total, prior), "seq", combine, (jnp.ones_like(total), jnp.zeros_like(prior))
    )
    before = jnp.stack(befores) + jnp.stack(factors)[..., None, None] * enter_state[None]
    reach = jnp.exp(logdec) * (first_b <= place_b[:, :1] - 1).astype(jnp.float32)[:, :, None]
    across = jnp.einsum(
        "bqgn,bgjpn->bqgjp", query_c.astype(jnp.float32), before, precision=lax.Precision.HIGHEST
    )
    across = across * reach.reshape(blocks, SPAN, groups_loc, per_group)[..., None]
    output = (
        within + across + skip_gain.reshape(groups_loc, per_group)[None, None, :, :, None] * xheads
    )
    gated = output.reshape(rows, inner_loc) * jax.nn.silu(gate_in.astype(jnp.float32))
    grouped = gated.reshape(rows, groups_loc, inner_loc // groups_loc)
    scale = lax.rsqrt(jnp.mean(grouped * grouped, axis=-1, keepdims=True) + 1e-05)
    normed = ((grouped * scale).reshape(rows, inner_loc) * norm_gain[None, :]).astype(jnp.bfloat16)
    terms = jnp.dot(
        normed,
        lax.all_gather(out_weight, "seq", axis=1, tiled=True),
        preferred_element_type=jnp.float32,
    )
    mixed = lax.psum_scatter(terms.astype(jnp.bfloat16), "tp", scatter_dimension=1, tiled=True)
    return mixed


def solution(mesh):
    in_specs = (
        P("seq", "tp"),
        P("seq", "tp", None),
        P("seq", "tp"),
        P("seq", "tp"),
        P("tp"),
        P("tp"),
        P(None, "tp"),
        P(None, "tp", None),
        P("tp"),
        P("tp", "seq"),
        P(),
    )
    out_specs = P("seq", "tp")
    return jax.shard_map(
        on_device, mesh=mesh, in_specs=in_specs, out_specs=out_specs, check_vma=False
    )
```

profile of v0, /device:TPU:8, one launch (start us, length us, event | category | flops | bytes accessed | tf_op | source)
XLA Modules:
  0.0 467.1 jit_solution(7035890431279881747)
XLA Ops:
  7.4 1.1 copy.68
  8.5 3.4 collective-permute-start
  12.6 3.4 collective-permute-start.1
  22.1 0.9 fusion.39
  24.6 1.9 multiply_convert_fusion.7
  26.6 3.8 fusion.16
  30.4 1.5 add_convert_fusion
  34.1 1.5 copy.85
  35.6 42.4 %all_gather.13 = bf16[32,1,32]{2,1,0:T(2,128)(2,1)S(1)} all-gather(bf16[1,1,32]{2,1,0:T(2,128)(2,1)S(1)} %get-tuple-element.167), channel_id=1, replica_groups=mesh['seq'=32,'tp'=8] {'seq'}, dimensions={0}, use_global_device_ids=true | all-gather | bytes 2112 | tf_op jit(solution)/shard_map/all_gather | solution.py:18
  80.5 188.2 %all-gather.6.cloned.1.call-done = bf16[1024,64,256]{2,1,0:T(8,128)(2,1)} async-done(((bf16[32,64,256]{2,1,0:T(8,128)(2,1)}), bf16[1024,64,256]{2,1,0:T(8,128)(2,1)}) %all-gather.6.cloned.1.call-update) | async-done | bytes 33554448 | tf_op jit(solution)/shard_map/all_gather | solution.py:18
  268.6 73.0 %while.14 = (s32[]{:T(128)}, f32[1,32,64,256]{3,2,1,0:T(8,128)S(1)}, s32[]{:T(128)}, bf16[32,1,32]{2,1,0:T(2,128)(2,1)S(1)}, bf16[32,1,32,64,256]{4,3,2,1,0:T(8,128)(2,1)}, /*index=5*/s32[]{:T(128)}, s32[]{:T(128)}) while((s32[]{:T(128)}, f32[1,32,64,256]{3,2,1,0:T(8,128)S(1)}, s32[]{:T(128)}, bf16[32,1,32]{2,1,0:T(2,128)(2,1)S(1)}, ...), condition=%wide.region_5.6_spmd.clone, body=%wide.region_4.5_spmd.clone.sunk | while | flops 2621476 | bytes 5243305 | solution.py:31
  268.6 2.2 fusion.45
  270.9 2.2 fusion.45
  273.2 2.2 fusion.45
  275.4 2.2 fusion.45
  277.7 2.2 fusion.45
  280.0 2.3 fusion.45
  282.3 2.3 fusion.45
  284.6 2.2 fusion.45
  286.9 2.2 fusion.45
  289.2 2.3 fusion.45
  291.5 2.2 fusion.45
  293.7 2.2 fusion.45
  296.0 2.3 fusion.45
  298.3 2.2 fusion.45
  300.6 2.2 fusion.45
  302.9 2.2 fusion.45
  305.1 2.2 fusion.45
  307.4 2.2 fusion.45
  309.7 2.2 fusion.45
  312.0 2.2 fusion.45
  314.2 2.2 fusion.45
  316.5 2.2 fusion.45
  318.8 2.2 fusion.45
  321.1 2.2 fusion.45
  323.3 2.2 fusion.45
  325.6 2.2 fusion.45
  327.9 2.3 fusion.45
  330.2 2.3 fusion.45
  332.5 2.2 fusion.45
  334.8 2.2 fusion.45
  337.1 2.2 fusion.45
  339.4 2.2 fusion.45
  341.7 1.1 fusion.14
  342.9 2.5 fusion.13
  346.2 72.7 %all-gather.4.cloned.1.call-done = bf16[2048,4096]{1,0:T(8,128)(2,1)} async-done(((bf16[2048,128]{1,0:T(8,128)(2,1)}), bf16[2048,4096]{1,0:T(8,128)(2,1)}) %all-gather.4.cloned.1.call-update) | async-done | bytes 16777232 | tf_op jit(solution)/shard_map/all_gather | solution.py:142
  418.9 11.7 %convolution_convert_fusion = bf16[256,4096]{1,0:T(8,128)(2,1)} fusion(bf16[2048,4096]{1,0:T(8,128)(2,1)} %all-gather.4.cloned.1.call-done, f32[256,2048]{0,1:T(8,128)S(1)} %get-tuple-element.159, f32[2048]{0:T(1024)S(1)} %copy-done.3, f32[256]{0:T(256)S(1)} %add_rsqrt_fusion), kind=kOutput, calls=%fused_computation.4 | convolution fusion | flops 4297588736 | bytes 20980736 | tf_op jit(solution)/shard_map/dot_general | solution.py:140
  430.6 29.9 %reduce-scatter.2.cloned.1.call-done = bf16[256,512]{1,0:T(8,128)(2,1)} async-done(((bf16[256,4096]{1,0:T(8,128)(2,1)}), bf16[256,512]{1,0:T(8,128)(2,1)}) %reduce-scatter.2.cloned.1.call-update) | async-done | bytes 262160 | tf_op jit(solution)/shard_map/reduce_scatter | solution.py:145
  (98 shorter events, 14.4 us)
Async XLA Ops:
  6.5 17.5 %copy-start = (bf16[256,2048]{1,0:T(8,128)(2,1)S(1)}, bf16[256,2048]{1,0:T(8,128)(2,1)}, u32[]{:S(2)}) copy-start(bf16[256,2048]{1,0:T(8,128)(2,1)} %param.13) | copy-start | bytes 3145732
  6.5 262.1 %all-gather.6.cloned.1.call-start = ((), (), s32[]{:S(2)}) async-start(), calls=%async_computation.3 | async-start | bytes 34603008 | tf_op jit(solution)/shard_map/all_gather | solution.py:18
  8.5 18.1 %collective-permute-start = (bf16[3,2048]{0,1:T(8,128)(2,1)}, bf16[3,2048]{0,1:T(8,128)(2,1)S(1)}, u32[]{:S(2)}, u32[]{:S(2)}) collective-permute-start(bf16[3,2048]{0,1:T(8,128)(2,1)} %copy.68), channel_id=1, source_target_pairs={{0,8},{8,16},{16,24},{24,32},{32,40},{40,48},{48,56},{56,64},{64,7... | collective-permute-start | bytes 36872 | tf_op jit(solution)/shard_map/ppermute | solution.py:12
  12.6 12.0 %collective-permute-start.1 = (bf16[3,1,512]{2,0,1:T(4,128)(2,1)S(1)}, bf16[3,1,512]{2,0,1:T(4,128)(2,1)S(1)}, u32[]{:S(2)}, u32[]{:S(2)}) collective-permute-start(bf16[3,1,512]{2,0,1:T(4,128)(2,1)S(1)} %slice.79), channel_id=1, source_target_pairs={{0,8},{8,16},{16,24},{24,32},{32,40},{40,48},{48,56},{56,64},{64,7... | collective-permute-start | bytes 9224 | tf_op jit(solution)/shard_map/ppermute | solution.py:12
  18.4 5.3 %copy-start.8 = (s32[256]{0:T(256)}, s32[256]{0:T(256)S(1)}, u32[]{:S(2)}) copy-start(s32[256]{0:T(256)S(1)} %iota_add_fusion) | copy-start | bytes 3076
  20.2 3.6 copy-start.7
  31.8 387.0 %all-gather.4.cloned.1.call-start = ((), (), s32[]{:S(2)}) async-start(), calls=%async_computation.1 | async-start | bytes 17301504 | tf_op jit(solution)/shard_map/all_gather | solution.py:142
  32.6 428.0 %reduce-scatter.2.cloned.1.call-start = ((), (), s32[]{:S(2)}) async-start(), calls=%async_computation.2 | async-start | bytes 2359296 | tf_op jit(solution)/shard_map/reduce_scatter | solution.py:145
  341.6 1.2 copy-start.1
  341.6 1.3 copy-start.2
  341.6 1.2 copy-start.4
  341.6 1.2 copy-start.5
  341.6 1.2 copy-start.6
  341.7 1.2 copy-start.9
  345.4 73.5 %copy-start.3 = (f32[2048]{0:T(1024)S(1)}, f32[2048]{0:T(1024)}, u32[]{:S(2)}) copy-start(f32[2048]{0:T(1024)} %param.21) | copy-start | bytes 24580
Sparse Core Ops, SparseCore 0:
  32.0 236.6 all-gather.5
  271.1 147.7 all-gather.3
  430.8 29.7 reduce-scatter.1
where the time goes:
time: 472 us; the launch traced here: 467 us
  waiting for transfers between devices  292 us (62%)
  other arithmetic  83.7 us (18%)
  blocking collectives  42.4 us (9%)
  matrix products  17.8 us (4%)
  between operations  14 us (3%)
  local copies, waits for them, and re-layouts  9.78 us (2%)
  starting transfers between devices  6.85 us (1%)
    all_gather x1, waiting for transfers between devices, prefix(): lax.all_gather(part.astype(kind), axis)  188 us
    all_gather x1, waiting for transfers between devices, on_device(): lax.all_gather(out_weight, 'seq', axis=1, tiled=True)  72.7 us
    select_n x32, other arithmetic, turn(): return jax.tree.map(lambda a, b: jnp.where(reached, a, b), new, before)  71.6 us
    all_gather x1, blocking collectives, prefix(): lax.all_gather(part.astype(kind), axis)  42.4 us
    reduce_scatter x1, waiting for transfers between devices, on_device(): lax.psum_scatter(terms.astype(jnp.bfloat16), 'tp', scatter_dimension=1, t...  29.9 us
    dot_general x1, matrix products, on_device(): jnp.dot(normed, lax.all_gather(out_weight, 'seq', axis=1, tiled=True), pr...  11.7 us
  transfers between devices with their start and end apart: 5, of which 3 were waited for; matrix products, arithmetic and copies ran while one was open for 20% of the time, Pallas kernels for 0%

commit v1 on v0

v1 whole, which is shorter than its diff:
```python
import functools

import jax
import jax.numpy as jnp
from jax import lax
from jax.experimental import pallas as pl
from jax.experimental.pallas import tpu as pltpu
from jax.sharding import Mesh, PartitionSpec as P

SPAN = 256
NX = 4
NY = 4
HEADS = 8
HEAD_DIM = 64
WIDTH = HEADS * HEAD_DIM
STATE = 256
BC = 2 * STATE
PAY = WIDTH + BC + 128
F32 = jnp.float32
BF16 = jnp.bfloat16
VMEM = pl.BlockSpec(memory_space=pltpu.VMEM)
SMEM = pl.BlockSpec(memory_space=pltpu.SMEM)
PARAMS = pltpu.CompilerParams(vmem_limit_bytes=48 * 1024 * 1024)


def call(kernel, scalars, args, outs, scratch=(), flops=0, nbytes=0):
    return pl.pallas_call(
        kernel,
        in_specs=[SMEM] + [VMEM] * len(args),
        out_specs=tuple(VMEM for _ in outs),
        out_shape=tuple(jax.ShapeDtypeStruct(s, d) for s, d in outs),
        scratch_shapes=list(scratch),
        compiler_params=PARAMS,
        cost_estimate=pl.CostEstimate(flops=flops, bytes_accessed=nbytes, transcendentals=0),
    )(scalars, *args)


def shift(v, axis, by):
    n = lax.axis_size(axis)
    return lax.ppermute(v, axis, [(i, (i + by) % n) for i in range(n)])


def around(v, by):
    return lax.rem(v + by, 4)


def sigmoid(v):
    return 0.5 * jnp.tanh(0.5 * v) + 0.5


def lanes(q, width):
    return pl.ds(pl.multiple_of(q * width, width), width)


def pack_kernel(sc, x_ref, bc_ref, dt_ref, own, to_next, to_prev, to_far, h0, h1, h2, h3, dts):
    x = sc[0]
    dts[...] = jnp.zeros_like(dts)
    dts[:, : 4 * HEADS] = dt_ref[...]
    raw = dts[...]
    lane = lax.broadcasted_iota(jnp.int32, raw.shape, 1)
    for by, out in ((0, own), (1, to_next), (3, to_prev), (2, to_far)):
        q = around(x, by)
        out[:, :WIDTH] = x_ref[:, lanes(q, WIDTH)]
        out[:, WIDTH : WIDTH + BC] = bc_ref[...]
        mine = pltpu.roll(raw, lax.rem(128 - HEADS * q, 128), 1)
        mine = jnp.where(lane < HEADS, mine, 0.0)
        hi = mine.astype(BF16).astype(F32)
        mid = (mine - hi).astype(BF16).astype(F32)
        low = (mine - hi - mid).astype(BF16).astype(F32)
        out[:, WIDTH + BC :] = (
            hi + pltpu.roll(mid, HEADS, 1) + pltpu.roll(low, 2 * HEADS, 1)
        ).astype(BF16)
    for q, out in enumerate((h0, h1, h2, h3)):
        out[:, :WIDTH] = x_ref[SPAN - 16 :, q * WIDTH : (q + 1) * WIDTH]
        out[:, WIDTH:] = bc_ref[SPAN - 16 :, :]


def split_kernel(sc, g_ref, own, to_next, to_prev, to_far):
    x = sc[0]
    for by, out in ((0, own), (1, to_next), (3, to_prev), (2, to_far)):
        out[...] = g_ref[:, lanes(around(x, by), WIDTH)]


def block_kernel(
    sc, own, prev, nxt, far, h0, h1, h2, h3, cw_ref, cbw_ref, skip_ref, decay_ref,
    y_out, c_out, re_out, t_out,
    pay, ext, conv, gram, carry, weighted,
):
    x = sc[0]
    base = sc[1] * (NX * SPAN)
    s1, s2, s3 = sc[4], sc[5], sc[6]
    pay[x] = own[...]
    pay[around(x, 3)] = prev[...]
    pay[around(x, 1)] = nxt[...]
    pay[around(x, 2)] = far[...]
    ext[0:8] = (
        h0[8:16].astype(F32) + h1[8:16].astype(F32) + h2[8:16].astype(F32) + h3[8:16].astype(F32)
    )
    carry[...] = jnp.zeros_like(carry)
    taps_x = cw_ref[:, lanes(x, WIDTH)]
    taps_bc = cbw_ref[...]
    decay = decay_ref[...]

    def first_of(t):
        return jnp.where(t >= s3, s3, jnp.where(t >= s2, s2, jnp.where(t >= s1, s1, 0)))

    def turn(j, before):
        start = base + j * SPAN

        @pl.when(j > 0)
        def _():
            ext[0:8] = ext[SPAN : SPAN + 8]

        ext[8:] = pay[j][:, : WIDTH + BC].astype(F32)
        row = lax.broadcasted_iota(jnp.int32, (SPAN, 128), 0)
        lane = lax.broadcasted_iota(jnp.int32, (SPAN, 128), 1)
        lane1 = lax.broadcasted_iota(jnp.int32, (1, 128), 1)
        place = start + row
        first = first_of(place)
        pos = place - first
        for part in range((WIDTH + BC) // 128):
            cols = slice(part * 128, part * 128 + 128)
            taps, at = (taps_x, part * 128) if part * 128 < WIDTH else (taps_bc, part * 128 - WIDTH)
            acc = taps[3:4, at : at + 128] * ext[8 : 8 + SPAN, cols]
            for back in (1, 2, 3):
                term = taps[3 - back : 4 - back, at : at + 128] * ext[8 - back : 8 - back + SPAN, cols]
                acc = acc + jnp.where(pos >= back, term, 0.0)
            conv[:, cols] = (acc * sigmoid(acc)).astype(BF16)
        keys = conv[:, WIDTH : WIDTH + STATE]
        query = conv[:, WIDTH + STATE :]
        packed = pay[j][:, WIDTH + BC :].astype(F32)
        raw = packed + pltpu.roll(packed, 128 - HEADS, 1) + pltpu.roll(packed, 128 - 2 * HEADS, 1)
        step = jnp.maximum(raw, 0.0) + jnp.log1p(jnp.exp(-jnp.abs(raw)))
        rate = jnp.where(lane < HEADS, -decay * step, 0.0)
        hi = rate.astype(BF16).astype(F32)
        mid = (rate - hi).astype(BF16).astype(F32)
        low = (rate - hi - mid).astype(BF16).astype(F32)
        three = (hi + pltpu.roll(mid, HEADS, 1) + pltpu.roll(low, 2 * HEADS, 1)).astype(BF16)
        wide_t = lax.broadcasted_iota(jnp.int32, (SPAN, SPAN), 0)
        wide_s = lax.broadcasted_iota(jnp.int32, (SPAN, SPAN), 1)
        lower = jnp.where(wide_s <= wide_t, 1.0, 0.0).astype(BF16)
        sums = jnp.dot(lower, three, preferred_element_type=F32)
        logd = sums + pltpu.roll(sums, 128 - HEADS, 1) + pltpu.roll(sums, 128 - 2 * HEADS, 1)
        logd = jnp.where(lane < HEADS, logd, 0.0)
        turned = jnp.transpose(jnp.where(lane < HEADS, logd, pltpu.roll(step, HEADS, 1)))
        dots = lax.dot_general(query, keys, (((1,), (1,)), ((), ())), preferred_element_type=F32)
        wide_first = first_of(start + wide_t)
        gram[...] = jnp.where(
            (wide_s <= wide_t) & (start + wide_s >= wide_first), dots, 0.0
        )
        first_end = first_of(start + SPAN - 1)
        keep = place >= first_end
        entered = first < start
        carried = jnp.where(first_end < start, 1.0, 0.0)
        end = logd[SPAN - 1 : SPAN, :]
        re_out[j] = jnp.where(first < base, jnp.exp(logd + before), 0.0)
        across = jnp.dot(query, carry[...].astype(BF16), preferred_element_type=F32)
        c_out[j] = query
        half = SPAN // 2
        left = lane < HEAD_DIM
        left1 = lane1 < HEAD_DIM
        decays = []
        for pair in range(HEADS // 2):
            cols = slice(pair * 128, pair * 128 + 128)
            xs = conv[:, cols]
            tops, bottoms = [], []
            for h in (2 * pair, 2 * pair + 1):
                column = logd[:, h : h + 1]
                across_row = turned[h : h + 1, :]
                weight = turned[HEADS + h : HEADS + h + 1, :]
                top = jnp.exp(jnp.minimum(column[:half] - across_row[:, :half], 0.0)) * (
                    gram[:half, :half] * weight[:, :half]
                )
                bottom = jnp.exp(jnp.minimum(column[half:] - across_row, 0.0)) * (
                    gram[half:, :] * weight
                )
                tops.append(jnp.dot(top.astype(BF16), xs[:half], preferred_element_type=F32))
                bottoms.append(jnp.dot(bottom.astype(BF16), xs, preferred_element_type=F32))
            within = jnp.concatenate(
                [
                    jnp.where(left[:half], tops[0], tops[1]),
                    jnp.where(left[half:], bottoms[0], bottoms[1]),
                ],
                axis=0,
            )
            h = 2 * pair
            log2 = jnp.where(left, logd[:, h : h + 1], logd[:, h + 1 : h + 2])
            step2 = jnp.where(left, step[:, h : h + 1], step[:, h + 1 : h + 2])
            end2 = jnp.where(left1, end[:, h : h + 1], end[:, h + 1 : h + 2])
            xf = xs.astype(F32)
            inputs = jnp.where(keep, jnp.exp(end2 - log2) * step2, 0.0) * xf
            weighted[:, cols] = inputs.astype(BF16)
            reach = jnp.where(entered, jnp.exp(log2), 0.0)
            y_out[j, :, cols] = within + reach * across[:, cols] + skip_ref[:, cols] * xf
            decays.append(jnp.exp(end2) * carried)
        states = lax.dot_general(
            keys, weighted[...], (((0,), (0,)), ((), ())), preferred_element_type=F32
        )
        carry[...] = jnp.concatenate(decays, axis=1) * carry[...] + states
        return before + end

    total = lax.fori_loop(0, NX, turn, jnp.zeros((1, 128), F32))
    last = first_of(base + NX * SPAN - 1)
    lane1 = lax.broadcasted_iota(jnp.int32, (1, 128), 1)
    whole = jnp.where(last < base, jnp.exp(total), 0.0)
    spread = jnp.concatenate(
        [
            jnp.where(lane1 < HEAD_DIM, whole[:, h : h + 1], whole[:, h + 1 : h + 2])
            for h in range(0, HEADS, 2)
        ],
        axis=1,
    )
    hi = spread.astype(BF16).astype(F32)
    low = spread - hi
    which = lax.broadcasted_iota(jnp.int32, (16, WIDTH), 0)
    marks = jnp.where(which == 0, hi, jnp.where(which == 1, low, 0.0)).astype(BF16)
    parts = t_out.shape[0]
    rows = STATE // parts
    for k in range(parts):
        t_out[k, :rows] = carry[k * rows : (k + 1) * rows].astype(BF16)
        t_out[k, rows:] = marks


def scan_kernel(sc, t_ref, e_out):
    parts, rows, _ = e_out.shape
    state = jnp.zeros(e_out.shape[1:], F32)
    for k in range(parts):
        e_out[k] = state.astype(BF16)
        if k < parts - 1:
            marks = t_ref[k, rows:].astype(F32)
            state = (marks[0:1] + marks[1:2]) * state + t_ref[k, :rows].astype(F32)


def gate_kernel(sc, own, prev, nxt, far, y_ref, c_ref, re_ref, e_ref, gain_ref, v0, v1, v2, v3, sq, gate):
    x = sc[0]
    gate[x] = own[...]
    gate[around(x, 3)] = prev[...]
    gate[around(x, 1)] = nxt[...]
    gate[around(x, 2)] = far[...]
    gain = gain_ref[...]
    left = lax.broadcasted_iota(jnp.int32, (SPAN, 128), 1) < HEAD_DIM
    for j, out in enumerate((v0, v1, v2, v3)):
        across = jnp.dot(c_ref[j], e_ref[...], preferred_element_type=F32)
        reach = re_ref[j]
        total = jnp.zeros((SPAN, 128), F32)
        for pair in range(HEADS // 2):
            cols = slice(pair * 128, pair * 128 + 128)
            h = 2 * pair
            reach2 = jnp.where(left, reach[:, h : h + 1], reach[:, h + 1 : h + 2])
            g = gate[j, :, cols].astype(F32)
            v = (y_ref[j, :, cols] + reach2 * across[:, cols]) * (g * sigmoid(g))
            total = total + v * v
            out[:, cols] = (v * gain[:, cols]).astype(BF16)
        summed = jnp.broadcast_to(jnp.sum(total, axis=1, keepdims=True), (SPAN, 128))
        sq[:, j * SPAN : (j + 1) * SPAN] = jnp.transpose(summed)[:8]


def product_kernel(chunk, sc, *refs):
    blocks = (refs[0:4], refs[4:8])
    squares = refs[8:12]
    w_ref = refs[12]
    send, kept = refs[13:15]
    x, c = sc[0], sc[3]
    order = (x, around(x, 3), around(x, 1), around(x, 2))
    total = squares[0][...] + squares[1][...] + squares[2][...] + squares[3][...]
    for b in range(2):
        at = (2 * chunk + b) * SPAN
        row = jnp.broadcast_to(total[0:1, at : at + SPAN], (128, SPAN))
        mean = jnp.transpose(row) * (1.0 / (NX * WIDTH))
        scale = lax.rsqrt(mean + 1e-05)
        scale = jnp.concatenate([scale, scale], axis=1)
        for core, out in ((1 - c, send), (c, kept)):
            for yy in range(0, NY, 2):
                acc = jnp.zeros((SPAN, 256), F32)
                for part, q in zip(blocks[b], order):
                    rows = pl.ds(pl.multiple_of(q * WIDTH, WIDTH), WIDTH)
                    w = jnp.concatenate(
                        [w_ref[2 * yy + core, rows, :], w_ref[2 * yy + 2 + core, rows, :]], axis=1
                    )
                    acc = acc + jnp.dot(part[...], w, preferred_element_type=F32)
                acc = (acc * scale).astype(out.dtype)
                out[yy, b * SPAN : (b + 1) * SPAN, :] = acc[:, :128]
                out[yy + 1, b * SPAN : (b + 1) * SPAN, :] = acc[:, 128:]


def cores_kernel(sc, kept, got, to_next, to_prev, to_far, mine):
    y = sc[2]
    for by, out in ((1, to_next), (3, to_prev), (2, to_far), (0, mine)):
        q = around(y, by)
        out[...] = (kept[q] + got[q].astype(F32)).astype(out.dtype)


def rows_kernel(sc, a0, a1, a2, a3, b0, b1, b2, b3, own, to_next, to_prev, to_far, whole):
    x = sc[0]
    first = a0[...] + a1[...].astype(F32) + a2[...].astype(F32) + a3[...].astype(F32)
    second = b0[...] + b1[...].astype(F32) + b2[...].astype(F32) + b3[...].astype(F32)
    whole[0] = first[:SPAN]
    whole[1] = first[SPAN:]
    whole[2] = second[:SPAN]
    whole[3] = second[SPAN:]
    for by, out in ((0, own), (1, to_next), (3, to_prev), (2, to_far)):
        out[...] = whole[around(x, by)].astype(BF16)


def place_kernel(sc, own, prev, nxt, far, out):
    x = sc[0]
    for by, got in ((0, own), (3, prev), (1, nxt), (2, far)):
        out[:, lanes(around(x, by), 128)] = got[...]


def on_device(
    x_in, bc_in, gate_in, dt_raw, decay_rate, skip_gain, conv_x, conv_bc, norm_gain, out_weight, lengths
):
    xi, zi = lax.axis_index("x"), lax.axis_index("z")
    nz = lax.axis_size("z")
    ends = jnp.cumsum(lengths)
    sc = jnp.stack(
        [xi, zi, lax.axis_index("y"), lax.axis_index("c"), ends[0], ends[1], ends[2], ends[2]]
    ).astype(jnp.int32)
    bc = bc_in.reshape(SPAN, BC)
    w_all = lax.all_gather(out_weight, "z", axis=0)

    piece = ((SPAN, PAY), BF16)
    edge = ((16, WIDTH + BC), BF16)
    own, to_next, to_prev, to_far, *edges = call(
        pack_kernel, sc, (x_in, bc, dt_raw), [piece] * 4 + [edge] * 4,
        [pltpu.VMEM((SPAN, 128), F32)], nbytes=6 << 20,
    )
    prev, nxt, far = shift(to_next, "x", 1), shift(to_prev, "x", -1), shift(to_far, "x", 2)
    halo = [
        lax.ppermute(e, ("z", "x"), [((z - 1) * NX + NX - 1, z * NX + k) for z in range(1, nz)])
        for k, e in enumerate(edges)
    ]
    quarter = ((SPAN, WIDTH), BF16)
    g_own, g_next, g_prev, g_far = call(
        split_kernel, sc, (gate_in,), [quarter] * 4, nbytes=2 << 20
    )
    gates = (g_own, shift(g_next, "x", 1), shift(g_prev, "x", -1), shift(g_far, "x", 2))

    skip = jnp.repeat(lax.dynamic_slice(skip_gain, (xi * HEADS,), (HEADS,)), HEAD_DIM)[None, :]
    decay = jnp.pad(lax.dynamic_slice(decay_rate, (xi * HEADS,), (HEADS,)), (0, 128 - HEADS))[None, :]
    gain = lax.dynamic_slice(norm_gain, (xi * WIDTH,), (WIDTH,))[None, :]
    rows = STATE // nz
    y_loc, query, reach, sums = call(
        block_kernel, sc,
        (own, prev, nxt, far, *halo, conv_x, conv_bc.reshape(4, BC), skip, decay),
        [
            ((NX, SPAN, WIDTH), F32),
            ((NX, SPAN, STATE), BF16),
            ((NX, SPAN, 128), F32),
            ((nz, rows + 16, WIDTH), BF16),
        ],
        [
            pltpu.VMEM((NX, SPAN, PAY), BF16),
            pltpu.VMEM((SPAN + 8, WIDTH + BC), F32),
            pltpu.VMEM((SPAN, WIDTH + BC), BF16),
            pltpu.VMEM((SPAN, SPAN), F32),
            pltpu.VMEM((STATE, WIDTH), F32),
            pltpu.VMEM((SPAN, WIDTH), BF16),
        ],
        flops=4 << 30, nbytes=8 << 20,
    )
    spread = lax.all_to_all(sums, "z", 0, 0, tiled=True)
    (enter,) = call(scan_kernel, sc, (spread,), [((nz, rows, WIDTH), BF16)], nbytes=1 << 20)
    enter = lax.all_to_all(enter, "z", 0, 0, tiled=True).reshape(STATE, WIDTH)
    *v, sq = call(
        gate_kernel, sc, (*gates, y_loc, query, reach, enter, gain),
        [quarter] * 4 + [((8, NX * SPAN), F32)],
        [pltpu.VMEM((NX, SPAN, WIDTH), BF16)],
        flops=2 << 30, nbytes=6 << 20,
    )
    squares = (sq, shift(sq, "x", 1), shift(sq, "x", -1), shift(sq, "x", 2))
    parts = []
    for j, own_v in enumerate(v):
        a, b = shift(own_v, "x", 1), shift(own_v, "x", -1)
        parts.append((own_v, a, b, shift(a, "x", 1) if j % 2 == 0 else shift(b, "x", -1)))

    halves = []
    for chunk in range(2):
        send, kept = call(
            functools.partial(product_kernel, chunk), sc,
            (*parts[2 * chunk], *parts[2 * chunk + 1], *squares, w_all),
            [((NY, 2 * SPAN, 128), BF16), ((NY, 2 * SPAN, 128), F32)],
            flops=4 << 30, nbytes=8 << 20,
        )
        got = shift(send, "c", 1)
        part = ((2 * SPAN, 128), BF16)
        y_next, y_prev, y_far, mine = call(
            cores_kernel, sc, (kept, got), [part] * 3 + [((2 * SPAN, 128), F32)], nbytes=2 << 20
        )
        halves += [mine, shift(y_next, "y", 1), shift(y_prev, "y", -1), shift(y_far, "y", 2)]
    tile = ((SPAN, 128), BF16)
    own, to_next, to_prev, to_far = call(
        rows_kernel, sc, halves, [tile] * 4, [pltpu.VMEM((NX, SPAN, 128), F32)], nbytes=2 << 20
    )
    (mixed,) = call(
        place_kernel, sc,
        (own, shift(to_next, "x", 1), shift(to_prev, "x", -1), shift(to_far, "x", 2)),
        [((SPAN, NX * 128), BF16)], nbytes=1 << 20,
    )
    return mixed


def solution(mesh):
    seq, tp = ("z", "x"), ("y", "c")
    fine = Mesh(mesh.devices.reshape(mesh.devices.shape[0] // NX, NX, NY, 2), seq + tp)
    in_specs = (
        P(seq, tp),
        P(seq, tp, None),
        P(seq, tp),
        P(seq, tp),
        P(tp),
        P(tp),
        P(None, tp),
        P(None, tp, None),
        P(tp),
        P(tp, seq),
        P(),
    )
    return jax.shard_map(
        on_device, mesh=fine, in_specs=in_specs, out_specs=P(seq, tp), check_vma=False
    )
```

time: 472 us -> 193 us (0.41)
  waiting for transfers between devices: 292 us -> 59 us
  other arithmetic: 83.7 us -> 0.83 us
  starting transfers between devices: 6.85 us -> 47.1 us
  Pallas kernels: 0 us -> 30.5 us
  blocking collectives: 42.4 us -> 22.1 us
  matrix products: 17.8 us -> 0 us
  local copies, waits for them, and re-layouts: 9.78 us -> 19.3 us
    all_gather x2 -> x1, waiting for transfers between devices: 261 us -> 0.01 us  [on_device(): w_all = lax.all_gather(out_weight, 'z', axis=0)]
    select_n x32 -> x0, other arithmetic: 71.6 us -> none  [turn(): return jax.tree.map(lambda a, b: jnp.where(reached, a, b), new, before)]
    ppermute x2 -> x36, waiting for transfers between devices: 0.01 us -> 58.3 us  [the longest x32 58.3 us: shift(): return lax.ppermute(v, axis, [(i, (i + by) % n) for i in range(n)])]
    all_gather x1 -> x0, blocking collectives: 42.4 us -> none  [prefix(): lax.all_gather(part.astype(kind), axis)]
    ppermute x2 -> x36, starting transfers between devices: 6.77 us -> 43.7 us  [the longest x32 41.1 us: shift(): return lax.ppermute(v, axis, [(i, (i + by) % n) for i in range(n)])]
    pallas_call x0 -> x11, Pallas kernels: none -> 30.5 us  [call(): pl.pallas_call(kernel, in_specs=[SMEM] + [VMEM] * len(args), out_specs=tu...]
    reduce_scatter x1 -> x0, waiting for transfers between devices: 29.9 us -> none  [on_device(): lax.psum_scatter(terms.astype(jnp.bfloat16), 'tp', scatter_dimension=1, t...]
    all_to_all x0 -> x1, blocking collectives: none -> 22.1 us  [on_device(): spread = lax.all_to_all(sums, 'z', 0, 0, tiled=True)]
  transfers between devices with their start and end apart: 5 -> 38, of which waited for: 3 -> 17; matrix products, arithmetic and copies ran while one was open for 20% -> 4% of each run, Pallas kernels for 0% -> 15%
where the time goes in v1:
time: 193 us; the launch traced here: 192 us
  waiting for transfers between devices  59 us (31%)
  starting transfers between devices  47.1 us (24%)
  Pallas kernels  30.5 us (16%)
  blocking collectives  22.1 us (11%)
  local copies, waits for them, and re-layouts  19.3 us (10%)
  between operations  13.6 us (7%)
    ppermute x32, waiting for transfers between devices, shift(): return lax.ppermute(v, axis, [(i, (i + by) % n) for i in range(n)])  58.3 us
    ppermute x32, starting transfers between devices, shift(): return lax.ppermute(v, axis, [(i, (i + by) % n) for i in range(n)])  41.1 us
    pallas_call x11, Pallas kernels, call(): pl.pallas_call(kernel, in_specs=[SMEM] + [VMEM] * len(args), out_specs=tu...  30.5 us
    all_to_all x1, blocking collectives, on_device(): spread = lax.all_to_all(sums, 'z', 0, 0, tiled=True)  22.1 us
    unnamed x30, local copies, waits for them, and re-layouts  13.6 us
  transfers between devices with their start and end apart: 38, of which 17 were waited for; matrix products, arithmetic and copies ran while one was open for 4% of the time, Pallas kernels for 15%

profile of v1, /device:TPU:8, one launch (start us, length us, event | category | flops | bytes accessed | tf_op | source)
XLA Modules:
  0.0 192.5 jit_solution(17934135080086425974)
XLA Ops:
  9.6 2.6 %stack.19.sc = s32[8]{0:T(128)S(1)} concatenate(s32[1]{0:T(128)} %bitcast, s32[1]{0:T(128)} %bitcast.1, s32[1]{0:T(128)} %bitcast.2, s32[1]{0:T(128)} %bitcast.3, s32[1]{0:T(128)} %bitcast.5, s32[1]{0:T(128)} %bitcast.6, s32[1]{0:T(128)} %bitcast.7, s32[1]{0:T(128)} %bitcast.7), dimensions={0} | concatenate | bytes 64 | tf_op jit(solution)/shard_map/stack | solution.py:317
  12.2 1.2 copy-done
  14.4 2.2 %shard_map.110 = (bf16[256,1152]{1,0:T(8,128)(2,1)S(1)}, bf16[256,1152]{1,0:T(8,128)(2,1)}, bf16[256,1152]{1,0:T(8,128)(2,1)}, bf16[256,1152]{1,0:T(8,128)(2,1)S...) custom-call(s32[8]{0:T(128)S(1)} %stack.19.sc, ...), custom_call_target="tpu_custom_call" | custom-call | bytes 6291456 | tf_op jit(solution)/shard_map/pallas_call | solution.py:27
  16.5 1.5 collective-permute-start.3
  18.0 1.7 collective-permute-start.4
  19.8 1.8 collective-permute-start.5
  26.6 6.6 %collective-permute-done.3.prev = bf16[256,1152]{1,0:T(8,128)(2,1)S(1)} collective-permute-done((bf16[256,1152]{1,0:T(8,128)(2,1)}, bf16[256,1152]{1,0:T(8,128)(2,1)S(1)}, u32[]{:S(2)}, u32[]{:S(2)}) %collective-permute-start.3) | collective-permute-done | bytes 589856 | tf_op jit(solution)/shard_map/ppermute | solution.py:40
  33.2 11.9 %collective-permute-done.4.nxt = bf16[256,1152]{1,0:T(8,128)(2,1)S(1)} collective-permute-done((bf16[256,1152]{1,0:T(8,128)(2,1)}, bf16[256,1152]{1,0:T(8,128)(2,1)S(1)}, u32[]{:S(2)}, u32[]{:S(2)}) %collective-permute-start.4) | collective-permute-done | bytes 589856 | tf_op jit(solution)/shard_map/ppermute | solution.py:40
  45.1 1.7 collective-permute-done.5.far
  47.5 11.4 %shard_map.111 = (f32[4,256,512]{2,1,0:T(8,128)S(1)}, bf16[4,256,256]{2,1,0:T(8,128)(2,1)S(1)}, f32[4,256,128]{2,1,0:T(8,128)S(1)}, bf16[8,48,512]{2,1,0:T(8,128)(2,1)S(1)}) custom-call(s32[8]{0:T(128)S(1)} %stack.19.sc, bf16[256,1152]{1,0:T(8,128)(2,1)S(1)} %get-tuple-element.46.own, bf16[256,1152]{1,0:T(8,128)(2,1)S(1)} %collective-permute-done.3.prev, ...), custom_call_target="tpu_custom_call" | custom-call | flops 4294967296 | bytes 8388608 | tf_op jit(solution)/shard_map/pallas_call | solution.py:27
  58.9 1.4 copy-done.8
  61.1 22.1 %all_to_all.10.t_ref = bf16[8,48,512]{2,1,0:T(8,128)(2,1)S(1)} all-to-all(bf16[8,48,512]{2,1,0:T(8,128)(2,1)S(1)} %get-tuple-element.57), channel_id=1, replica_groups=mesh['z'=8,'x'=4,'y'=4,'c'=2] {'z'}, dimensions={0} | all-to-all | bytes 786432 | tf_op jit(solution)/shard_map/all_to_all | solution.py:363
  83.1 1.3 shard_map.112
  84.4 3.4 %all-to-all-start.1 = ((bf16[8,32,512]{2,1,0:T(8,128)(2,1)}), bf16[8,32,512]{2,1,0:T(8,128)(2,1)S(1)}, u32[]{:S(2)}, u32[]{:S(2)}) async-start(bf16[8,32,512]{2,1,0:T(8,128)(2,1)} %shard_map.112), calls=%async_computation.1 | async-start | bytes 524288 | tf_op jit(solution)/shard_map/all_to_all | solution.py:365
  88.5 2.3 %collective-permute-start = (bf16[256,512]{1,0:T(8,128)(2,1)S(1)}, bf16[256,512]{1,0:T(8,128)(2,1)S(1)}, u32[]{:S(2)}, u32[]{:S(2)}) collective-permute-start(bf16[256,512]{1,0:T(8,128)(2,1)S(1)} %get-tuple-element.43), channel_id=1, source_target_pairs={{0,8},{8,16},{16,24},{24,0},{1,9},{9,17},{17,25},{25,1},{2,10},{10... | collective-permute-start | bytes 786440 | tf_op jit(solution)/shard_map/ppermute | solution.py:40
  90.8 1.0 collective-permute-start.1
  91.8 1.2 collective-permute-start.2
  93.7 7.5 %collective-permute-done.prev = bf16[256,512]{1,0:T(8,128)(2,1)S(1)} collective-permute-done((bf16[256,512]{1,0:T(8,128)(2,1)S(1)}, bf16[256,512]{1,0:T(8,128)(2,1)S(1)}, u32[]{:S(2)}, u32[]{:S(2)}) %collective-permute-start) | collective-permute-done | bytes 262176 | tf_op jit(solution)/shard_map/ppermute | solution.py:40
  101.3 1.6 copy-done.9
  102.9 1.0 copy-done.11
  103.9 1.0 copy-done.13
  105.0 2.4 %shard_map.113 = (bf16[256,512]{1,0:T(8,128)(2,1)S(1)}, bf16[256,512]{1,0:T(8,128)(2,1)S(1)}, bf16[256,512]{1,0:T(8,128)(2,1)S(1)}, bf16[256,512]{1,0:T(8,128)(2,1)S(1)}, f32[8,1024]{1,0:T(8,128)S(1)}) custom-call(s32[8]{0:T(128)S(1)} %stack.19.sc, bf16[256,512]{1,0:T(8,128)(2,1)S(1)} %get-tuple-element.42.own, ...), custom_call_target="tpu_custom_call" | custom-call | flops 2147483648 | bytes 6291456 | tf_op jit(solution)/shard_map/pallas_call | solution.py:27
  108.0 2.7 %collective-permute-start.27 = (bf16[256,512]{1,0:T(8,128)(2,1)S(1)}, bf16[256,512]{1,0:T(8,128)(2,1)S(1)}, u32[]{:S(2)}, u32[]{:S(2)}) collective-permute-start(bf16[256,512]{1,0:T(8,128)(2,1)S(1)} %get-tuple-element.68.refs_4_), channel_id=1, source_target_pairs={{0,24},{8,0},{16,8},{24,16},{1,25},{9,1},{17,9},{25,17},{2,26},{10... | collective-permute-start | bytes 786440 | tf_op jit(solution)/shard_map/ppermute | solution.py:40
  110.7 1.5 collective-permute-start.24
  112.7 2.8 %collective-permute-start.17 = (f32[8,1024]{1,0:T(8,128)S(1)}, f32[8,1024]{1,0:T(8,128)S(1)}, u32[]{:S(2)}, u32[]{:S(2)}) collective-permute-start(f32[8,1024]{1,0:T(8,128)S(1)} %get-tuple-element.60.refs_8_), channel_id=1, source_target_pairs={{0,24},{8,0},{16,8},{24,16},{1,25},{9,1},{17,9},{25,17},{2,26},{10... | collective-permute-start | bytes 98312 | tf_op jit(solution)/shard_map/ppermute | solution.py:40
  115.5 1.9 collective-permute-done.16.refs_9_
  117.3 3.3 %collective-permute-done.17.refs_10_ = f32[8,1024]{1,0:T(8,128)S(1)} collective-permute-done((f32[8,1024]{1,0:T(8,128)S(1)}, f32[8,1024]{1,0:T(8,128)S(1)}, u32[]{:S(2)}, u32[]{:S(2)}) %collective-permute-start.17) | collective-permute-done | bytes 32800 | tf_op jit(solution)/shard_map/ppermute | solution.py:40
  120.7 2.5 %collective-permute-done.18.refs_11_ = f32[8,1024]{1,0:T(8,128)S(1)} collective-permute-done((f32[8,1024]{1,0:T(8,128)S(1)}, f32[8,1024]{1,0:T(8,128)S(1)}, u32[]{:S(2)}, u32[]{:S(2)}) %collective-permute-start.18) | collective-permute-done | bytes 32800 | tf_op jit(solution)/shard_map/ppermute | solution.py:40
  123.2 3.2 %collective-permute-start.14 = (bf16[256,512]{1,0:T(8,128)(2,1)S(1)}, bf16[256,512]{1,0:T(8,128)(2,1)S(1)}, u32[]{:S(2)}, u32[]{:S(2)}) collective-permute-start(bf16[256,512]{1,0:T(8,128)(2,1)S(1)} %get-tuple-element.59.refs_4_), channel_id=1, source_target_pairs={{0,24},{8,0},{16,8},{24,16},{1,25},{9,1},{17,9},{25,17},{2,26},{10... | collective-permute-start | bytes 786440 | tf_op jit(solution)/shard_map/ppermute | solution.py:40
  126.4 3.2 %collective-permute-start.28 = (bf16[256,512]{1,0:T(8,128)(2,1)S(1)}, bf16[256,512]{1,0:T(8,128)(2,1)S(1)}, u32[]{:S(2)}, u32[]{:S(2)}) collective-permute-start(bf16[256,512]{1,0:T(8,128)(2,1)S(1)} %collective-permute-done.27.refs_6_), channel_id=1, source_target_pairs={{0,24},{8,0},{16,8},{24,16},{1,25},{9,1},{17,9},{25,17},{2,26},{10... | collective-permute-start | bytes 786440 | tf_op jit(solution)/shard_map/ppermute | solution.py:40
  129.7 1.9 %collective-permute-done.26.refs_5_ = bf16[256,512]{1,0:T(8,128)(2,1)S(1)} collective-permute-done((bf16[256,512]{1,0:T(8,128)(2,1)S(1)}, bf16[256,512]{1,0:T(8,128)(2,1)S(1)}, u32[]{:S(2)}, u32[]{:S(2)}) %collective-permute-start.26) | collective-permute-done | bytes 262176 | tf_op jit(solution)/shard_map/ppermute | solution.py:40
  131.6 2.0 %collective-permute-start.11 = (bf16[256,512]{1,0:T(8,128)(2,1)S(1)}, bf16[256,512]{1,0:T(8,128)(2,1)S(1)}, u32[]{:S(2)}, u32[]{:S(2)}) collective-permute-start(bf16[256,512]{1,0:T(8,128)(2,1)S(1)} %get-tuple-element.58.refs_0_), channel_id=1, source_target_pairs={{0,24},{8,0},{16,8},{24,16},{1,25},{9,1},{17,9},{25,17},{2,26},{10... | collective-permute-start | bytes 786440 | tf_op jit(solution)/shard_map/ppermute | solution.py:40
  133.6 3.6 %collective-permute-done.10.refs_1_ = bf16[256,512]{1,0:T(8,128)(2,1)S(1)} collective-permute-done((bf16[256,512]{1,0:T(8,128)(2,1)S(1)}, bf16[256,512]{1,0:T(8,128)(2,1)S(1)}, u32[]{:S(2)}, u32[]{:S(2)}) %collective-permute-start.10) | collective-permute-done | bytes 262176 | tf_op jit(solution)/shard_map/ppermute | solution.py:40
  138.2 4.3 %collective-permute-done.25.refs_3_ = bf16[256,512]{1,0:T(8,128)(2,1)S(1)} collective-permute-done((bf16[256,512]{1,0:T(8,128)(2,1)S(1)}, bf16[256,512]{1,0:T(8,128)(2,1)S(1)}, u32[]{:S(2)}, u32[]{:S(2)}) %collective-permute-start.25) | collective-permute-done | bytes 262176 | tf_op jit(solution)/shard_map/ppermute | solution.py:40
  143.2 1.7 collective-permute-start.15
  147.6 4.6 %shard_map.116 = (bf16[4,512,128]{2,1,0:T(8,128)(2,1)S(1)}, f32[4,512,128]{2,1,0:T(8,128)S(1)}) custom-call(s32[8]{0:T(128)S(1)} %stack.19.sc, bf16[256,512]{1,0:T(8,128)(2,1)S(1)} %get-tuple-element.67.refs_0_, bf16[256,512]{1,0:T(8,128)(2,1)S(1)} %collective-permute-done.23.refs_1_, bf16[256,512]{1,0:T(8,128)(2,1)S(1)} %collective-permute-done.24.refs_2_, ...), custom_call_target="tpu_custom_call" | custom-call | flops 4294967296 | bytes 8388608 | tf_op jit(solution)/shard_map/pallas_call | solution.py:27
  152.6 4.8 %shard_map.114 = (bf16[4,512,128]{2,1,0:T(8,128)(2,1)S(1)}, f32[4,512,128]{2,1,0:T(8,128)S(1)}) custom-call(s32[8]{0:T(128)S(1)} %stack.19.sc, bf16[256,512]{1,0:T(8,128)(2,1)S(1)} %get-tuple-element.58.refs_0_, bf16[256,512]{1,0:T(8,128)(2,1)S(1)} %collective-permute-done.10.refs_1_, bf16[256,512]{1,0:T(8,128)(2,1)S(1)} %collective-permute-done.11.refs_2_, ...), custom_call_target="tpu_custom_call" | custom-call | flops 4294967296 | bytes 8388608 | tf_op jit(solution)/shard_map/pallas_call | solution.py:27
  158.6 1.7 collective-permute-start.30
  160.7 2.3 %collective-permute-start.32 = (bf16[512,128]{1,0:T(8,128)(2,1)S(1)}, bf16[512,128]{1,0:T(8,128)(2,1)S(1)}, u32[]{:S(2)}, u32[]{:S(2)}) collective-permute-start(bf16[512,128]{1,0:T(8,128)(2,1)S(1)} %get-tuple-element.74), channel_id=1, source_target_pairs={{0,4},{2,6},{4,0},{6,2},{1,5},{3,7},{5,1},{7,3},{8,12},{10,14},{12... | collective-permute-start | bytes 393224 | tf_op jit(solution)/shard_map/ppermute | solution.py:40
  164.5 1.2 collective-permute-start.21
  165.7 1.6 collective-permute-start.22
  167.3 2.8 %collective-permute-done.32.b3 = bf16[512,128]{1,0:T(8,128)(2,1)S(1)} collective-permute-done((bf16[512,128]{1,0:T(8,128)(2,1)S(1)}, bf16[512,128]{1,0:T(8,128)(2,1)S(1)}, u32[]{:S(2)}, u32[]{:S(2)}) %collective-permute-start.32) | collective-permute-done | bytes 131104 | tf_op jit(solution)/shard_map/ppermute | solution.py:40
  170.1 1.2 collective-permute-done.20.a1
  171.8 2.7 %collective-permute-done.22.a3 = bf16[512,128]{1,0:T(8,128)(2,1)S(1)} collective-permute-done((bf16[512,128]{1,0:T(8,128)(2,1)S(1)}, bf16[512,128]{1,0:T(8,128)(2,1)S(1)}, u32[]{:S(2)}, u32[]{:S(2)}) %collective-permute-start.22) | collective-permute-done | bytes 131104 | tf_op jit(solution)/shard_map/ppermute | solution.py:40
  175.6 3.0 %collective-permute-start.34 = (bf16[256,128]{1,0:T(8,128)(2,1)S(1)}, bf16[256,128]{1,0:T(8,128)(2,1)S(1)}, u32[]{:S(2)}, u32[]{:S(2)}) collective-permute-start(bf16[256,128]{1,0:T(8,128)(2,1)S(1)} %get-tuple-element.77), channel_id=1, source_target_pairs={{0,24},{8,0},{16,8},{24,16},{1,25},{9,1},{17,9},{25,17},{2,26},{10... | collective-permute-start | bytes 196616 | tf_op jit(solution)/shard_map/ppermute | solution.py:40
  178.5 2.2 %collective-permute-done.33.prev = bf16[256,128]{1,0:T(8,128)(2,1)S(1)} collective-permute-done((bf16[256,128]{1,0:T(8,128)(2,1)S(1)}, bf16[256,128]{1,0:T(8,128)(2,1)S(1)}, u32[]{:S(2)}, u32[]{:S(2)}) %collective-permute-start.33) | collective-permute-done | bytes 65568 | tf_op jit(solution)/shard_map/ppermute | solution.py:40
  181.1 3.3 %collective-permute-done.35.far = bf16[256,128]{1,0:T(8,128)(2,1)S(1)} collective-permute-done((bf16[256,128]{1,0:T(8,128)(2,1)S(1)}, bf16[256,128]{1,0:T(8,128)(2,1)S(1)}, u32[]{:S(2)}, u32[]{:S(2)}) %collective-permute-start.35) | collective-permute-done | bytes 65568 | tf_op jit(solution)/shard_map/ppermute | solution.py:40
  184.3 1.3 shard_map.119
  (80 shorter events, 22.6 us)
Async XLA Ops:
  6.5 139.1 %all-gather.3.cloned.1.call-start = ((), (), s32[]{:S(2)}) async-start(), calls=%async_computation.2 | async-start | bytes 4718592 | tf_op jit(solution)/shard_map/all_gather | solution.py:321
  12.2 1.2 copy-start
  13.4 0.9 copy-start.2
  16.5 16.6 %collective-permute-start.3 = (bf16[256,1152]{1,0:T(8,128)(2,1)}, bf16[256,1152]{1,0:T(8,128)(2,1)S(1)}, u32[]{:S(2)}, u32[]{:S(2)}) collective-permute-start(bf16[256,1152]{1,0:T(8,128)(2,1)} %get-tuple-element.47), channel_id=1, source_target_pairs={{0,8},{8,16},{16,24},{24,0},{1,9},{9,17},{17,25},{25,1},{2,10},{10... | collective-permute-start | bytes 1769480 | tf_op jit(solution)/shard_map/ppermute | solution.py:40
  18.0 27.0 %collective-permute-start.4 = (bf16[256,1152]{1,0:T(8,128)(2,1)}, bf16[256,1152]{1,0:T(8,128)(2,1)S(1)}, u32[]{:S(2)}, u32[]{:S(2)}) collective-permute-start(bf16[256,1152]{1,0:T(8,128)(2,1)} %get-tuple-element.48), channel_id=1, source_target_pairs={{0,24},{8,0},{16,8},{24,16},{1,25},{9,1},{17,9},{25,17},{2,26},{10... | collective-permute-start | bytes 1769480 | tf_op jit(solution)/shard_map/ppermute | solution.py:40
  19.8 27.0 %collective-permute-start.5 = (bf16[256,1152]{1,0:T(8,128)(2,1)S(1)}, bf16[256,1152]{1,0:T(8,128)(2,1)}, u32[]{:S(2)}, u32[]{:S(2)}) collective-permute-start(bf16[256,1152]{1,0:T(8,128)(2,1)S(1)} %get-tuple-element.49), channel_id=1, source_target_pairs={{0,16},{8,24},{16,0},{24,8},{1,17},{9,25},{17,1},{25,9},{2,18},{10... | collective-permute-start | bytes 1769480 | tf_op jit(solution)/shard_map/ppermute | solution.py:40
  21.6 2.1 %collective-permute-start.6 = (bf16[16,1024]{1,0:T(8,128)(2,1)S(1)}, bf16[16,1024]{1,0:T(8,128)(2,1)S(1)}, u32[]{:S(2)}, u32[]{:S(2)}) collective-permute-start(bf16[16,1024]{1,0:T(8,128)(2,1)S(1)} %get-tuple-element.50), channel_id=1, source_target_pairs={{24,32},{56,64},{88,96},{120,128},{152,160},{184,192},{216,224},{2... | collective-permute-start | bytes 98312 | tf_op jit(solution)/shard_map/ppermute | solution.py:331
  22.3 2.1 %collective-permute-start.7 = (bf16[16,1024]{1,0:T(8,128)(2,1)S(1)}, bf16[16,1024]{1,0:T(8,128)(2,1)S(1)}, u32[]{:S(2)}, u32[]{:S(2)}) collective-permute-start(bf16[16,1024]{1,0:T(8,128)(2,1)S(1)} %get-tuple-element.51), channel_id=1, source_target_pairs={{24,40},{56,72},{88,104},{120,136},{152,168},{184,200},{216,232},{... | collective-permute-start | bytes 98312 | tf_op jit(solution)/shard_map/ppermute | solution.py:331
  23.7 2.9 %collective-permute-start.8 = (bf16[16,1024]{1,0:T(8,128)(2,1)S(1)}, bf16[16,1024]{1,0:T(8,128)(2,1)S(1)}, u32[]{:S(2)}, u32[]{:S(2)}) collective-permute-start(bf16[16,1024]{1,0:T(8,128)(2,1)S(1)} %get-tuple-element.52), channel_id=1, source_target_pairs={{24,48},{56,80},{88,112},{120,144},{152,176},{184,208},{216,240},{... | collective-permute-start | bytes 98312 | tf_op jit(solution)/shard_map/ppermute | solution.py:331
  24.3 2.3 %collective-permute-start.9 = (bf16[16,1024]{1,0:T(8,128)(2,1)S(1)}, bf16[16,1024]{1,0:T(8,128)(2,1)S(1)}, u32[]{:S(2)}, u32[]{:S(2)}) collective-permute-start(bf16[16,1024]{1,0:T(8,128)(2,1)S(1)} %get-tuple-element.53), channel_id=1, source_target_pairs={{24,56},{56,88},{88,120},{120,152},{152,184},{184,216},{216,248},{... | collective-permute-start | bytes 98312 | tf_op jit(solution)/shard_map/ppermute | solution.py:331
  47.5 40.3 %copy-start.1 = (bf16[256,2048]{1,0:T(8,128)(2,1)S(1)}, bf16[256,2048]{1,0:T(8,128)(2,1)}, u32[]{:S(2)}) copy-start(bf16[256,2048]{1,0:T(8,128)(2,1)} %g_ref.1) | copy-start | bytes 3145732
  58.9 1.4 copy-start.8
  61.1 22.1 %copy-start.10 = (bf16[4,256,256]{2,1,0:T(8,128)(2,1)}, bf16[4,256,256]{2,1,0:T(8,128)(2,1)S(1)}, u32[]{:S(2)}) copy-start(bf16[4,256,256]{2,1,0:T(8,128)(2,1)S(1)} %get-tuple-element.55.c_ref) | copy-start | bytes 1572868
  84.4 16.8 %all-to-all-start.1 = ((bf16[8,32,512]{2,1,0:T(8,128)(2,1)}), bf16[8,32,512]{2,1,0:T(8,128)(2,1)S(1)}, u32[]{:S(2)}, u32[]{:S(2)}) async-start(bf16[8,32,512]{2,1,0:T(8,128)(2,1)} %shard_map.112), calls=%async_computation.1 | async-start | bytes 524288 | tf_op jit(solution)/shard_map/all_to_all | solution.py:365
  88.5 12.8 %collective-permute-start = (bf16[256,512]{1,0:T(8,128)(2,1)S(1)}, bf16[256,512]{1,0:T(8,128)(2,1)S(1)}, u32[]{:S(2)}, u32[]{:S(2)}) collective-permute-start(bf16[256,512]{1,0:T(8,128)(2,1)S(1)} %get-tuple-element.43), channel_id=1, source_target_pairs={{0,8},{8,16},{16,24},{24,0},{1,9},{9,17},{17,25},{25,1},{2,10},{10... | collective-permute-start | bytes 786440 | tf_op jit(solution)/shard_map/ppermute | solution.py:40
  90.8 10.5 %collective-permute-start.1 = (bf16[256,512]{1,0:T(8,128)(2,1)S(1)}, bf16[256,512]{1,0:T(8,128)(2,1)S(1)}, u32[]{:S(2)}, u32[]{:S(2)}) collective-permute-start(bf16[256,512]{1,0:T(8,128)(2,1)S(1)} %get-tuple-element.44), channel_id=1, source_target_pairs={{0,24},{8,0},{16,8},{24,16},{1,25},{9,1},{17,9},{25,17},{2,26},{10... | collective-permute-start | bytes 786440 | tf_op jit(solution)/shard_map/ppermute | solution.py:40
  91.8 9.5 %collective-permute-start.2 = (bf16[256,512]{1,0:T(8,128)(2,1)S(1)}, bf16[256,512]{1,0:T(8,128)(2,1)S(1)}, u32[]{:S(2)}, u32[]{:S(2)}) collective-permute-start(bf16[256,512]{1,0:T(8,128)(2,1)S(1)} %get-tuple-element.45), channel_id=1, source_target_pairs={{0,16},{8,24},{16,0},{24,8},{1,17},{9,25},{17,1},{25,9},{2,18},{10... | collective-permute-start | bytes 786440 | tf_op jit(solution)/shard_map/ppermute | solution.py:40
  101.3 1.6 copy-start.9
  102.9 1.0 copy-start.11
  103.9 1.0 copy-start.13
  107.4 15.8 %collective-permute-start.23 = (bf16[256,512]{1,0:T(8,128)(2,1)S(1)}, bf16[256,512]{1,0:T(8,128)(2,1)S(1)}, u32[]{:S(2)}, u32[]{:S(2)}) collective-permute-start(bf16[256,512]{1,0:T(8,128)(2,1)S(1)} %get-tuple-element.67.refs_0_), channel_id=1, source_target_pairs={{0,8},{8,16},{16,24},{24,0},{1,9},{9,17},{17,25},{25,1},{2,10},{10... | collective-permute-start | bytes 786440 | tf_op jit(solution)/shard_map/ppermute | solution.py:40
  108.0 18.4 %collective-permute-start.27 = (bf16[256,512]{1,0:T(8,128)(2,1)S(1)}, bf16[256,512]{1,0:T(8,128)(2,1)S(1)}, u32[]{:S(2)}, u32[]{:S(2)}) collective-permute-start(bf16[256,512]{1,0:T(8,128)(2,1)S(1)} %get-tuple-element.68.refs_4_), channel_id=1, source_target_pairs={{0,24},{8,0},{16,8},{24,16},{1,25},{9,1},{17,9},{25,17},{2,26},{10... | collective-permute-start | bytes 786440 | tf_op jit(solution)/shard_map/ppermute | solution.py:40
  110.7 15.8 %collective-permute-start.24 = (bf16[256,512]{1,0:T(8,128)(2,1)S(1)}, bf16[256,512]{1,0:T(8,128)(2,1)S(1)}, u32[]{:S(2)}, u32[]{:S(2)}) collective-permute-start(bf16[256,512]{1,0:T(8,128)(2,1)S(1)} %get-tuple-element.67.refs_0_), channel_id=1, source_target_pairs={{0,24},{8,0},{16,8},{24,16},{1,25},{9,1},{17,9},{25,17},{2,26},{10... | collective-permute-start | bytes 786440 | tf_op jit(solution)/shard_map/ppermute | solution.py:40
  112.2 5.1 %collective-permute-start.16 = (f32[8,1024]{1,0:T(8,128)S(1)}, f32[8,1024]{1,0:T(8,128)S(1)}, u32[]{:S(2)}, u32[]{:S(2)}) collective-permute-start(f32[8,1024]{1,0:T(8,128)S(1)} %get-tuple-element.60.refs_8_), channel_id=1, source_target_pairs={{0,8},{8,16},{16,24},{24,0},{1,9},{9,17},{17,25},{25,1},{2,10},{10... | collective-permute-start | bytes 98312 | tf_op jit(solution)/shard_map/ppermute | solution.py:40
  112.7 8.0 %collective-permute-start.17 = (f32[8,1024]{1,0:T(8,128)S(1)}, f32[8,1024]{1,0:T(8,128)S(1)}, u32[]{:S(2)}, u32[]{:S(2)}) collective-permute-start(f32[8,1024]{1,0:T(8,128)S(1)} %get-tuple-element.60.refs_8_), channel_id=1, source_target_pairs={{0,24},{8,0},{16,8},{24,16},{1,25},{9,1},{17,9},{25,17},{2,26},{10... | collective-permute-start | bytes 98312 | tf_op jit(solution)/shard_map/ppermute | solution.py:40
  117.3 5.8 %collective-permute-start.18 = (f32[8,1024]{1,0:T(8,128)S(1)}, f32[8,1024]{1,0:T(8,128)S(1)}, u32[]{:S(2)}, u32[]{:S(2)}) collective-permute-start(f32[8,1024]{1,0:T(8,128)S(1)} %get-tuple-element.60.refs_8_), channel_id=1, source_target_pairs={{0,16},{8,24},{16,0},{24,8},{1,17},{9,25},{17,1},{25,9},{2,18},{10... | collective-permute-start | bytes 98312 | tf_op jit(solution)/shard_map/ppermute | solution.py:40
  120.7 10.9 %collective-permute-start.26 = (bf16[256,512]{1,0:T(8,128)(2,1)S(1)}, bf16[256,512]{1,0:T(8,128)(2,1)S(1)}, u32[]{:S(2)}, u32[]{:S(2)}) collective-permute-start(bf16[256,512]{1,0:T(8,128)(2,1)S(1)} %get-tuple-element.68.refs_4_), channel_id=1, source_target_pairs={{0,8},{8,16},{16,24},{24,0},{1,9},{9,17},{17,25},{25,1},{2,10},{10... | collective-permute-start | bytes 786440 | tf_op jit(solution)/shard_map/ppermute | solution.py:40
  123.2 14.0 %collective-permute-start.10 = (bf16[256,512]{1,0:T(8,128)(2,1)S(1)}, bf16[256,512]{1,0:T(8,128)(2,1)S(1)}, u32[]{:S(2)}, u32[]{:S(2)}) collective-permute-start(bf16[256,512]{1,0:T(8,128)(2,1)S(1)} %get-tuple-element.58.refs_0_), channel_id=1, source_target_pairs={{0,8},{8,16},{16,24},{24,0},{1,9},{9,17},{17,25},{25,1},{2,10},{10... | collective-permute-start | bytes 786440 | tf_op jit(solution)/shard_map/ppermute | solution.py:40
  123.2 14.0 %collective-permute-start.14 = (bf16[256,512]{1,0:T(8,128)(2,1)S(1)}, bf16[256,512]{1,0:T(8,128)(2,1)S(1)}, u32[]{:S(2)}, u32[]{:S(2)}) collective-permute-start(bf16[256,512]{1,0:T(8,128)(2,1)S(1)} %get-tuple-element.59.refs_4_), channel_id=1, source_target_pairs={{0,24},{8,0},{16,8},{24,16},{1,25},{9,1},{17,9},{25,17},{2,26},{10... | collective-permute-start | bytes 786440 | tf_op jit(solution)/shard_map/ppermute | solution.py:40
  126.4 16.1 %collective-permute-start.25 = (bf16[256,512]{1,0:T(8,128)(2,1)S(1)}, bf16[256,512]{1,0:T(8,128)(2,1)S(1)}, u32[]{:S(2)}, u32[]{:S(2)}) collective-permute-start(bf16[256,512]{1,0:T(8,128)(2,1)S(1)} %collective-permute-done.23.refs_1_), channel_id=1, source_target_pairs={{0,8},{8,16},{16,24},{24,0},{1,9},{9,17},{17,25},{25,1},{2,10},{10... | collective-permute-start | bytes 786440 | tf_op jit(solution)/shard_map/ppermute | solution.py:40
  126.4 18.5 %collective-permute-start.28 = (bf16[256,512]{1,0:T(8,128)(2,1)S(1)}, bf16[256,512]{1,0:T(8,128)(2,1)S(1)}, u32[]{:S(2)}, u32[]{:S(2)}) collective-permute-start(bf16[256,512]{1,0:T(8,128)(2,1)S(1)} %collective-permute-done.27.refs_6_), channel_id=1, source_target_pairs={{0,24},{8,0},{16,8},{24,16},{1,25},{9,1},{17,9},{25,17},{2,26},{10... | collective-permute-start | bytes 786440 | tf_op jit(solution)/shard_map/ppermute | solution.py:40
  131.6 20.9 %collective-permute-start.11 = (bf16[256,512]{1,0:T(8,128)(2,1)S(1)}, bf16[256,512]{1,0:T(8,128)(2,1)S(1)}, u32[]{:S(2)}, u32[]{:S(2)}) collective-permute-start(bf16[256,512]{1,0:T(8,128)(2,1)S(1)} %get-tuple-element.58.refs_0_), channel_id=1, source_target_pairs={{0,24},{8,0},{16,8},{24,16},{1,25},{9,1},{17,9},{25,17},{2,26},{10... | collective-permute-start | bytes 786440 | tf_op jit(solution)/shard_map/ppermute | solution.py:40
  137.2 15.3 %collective-permute-start.13 = (bf16[256,512]{1,0:T(8,128)(2,1)S(1)}, bf16[256,512]{1,0:T(8,128)(2,1)S(1)}, u32[]{:S(2)}, u32[]{:S(2)}) collective-permute-start(bf16[256,512]{1,0:T(8,128)(2,1)S(1)} %get-tuple-element.59.refs_4_), channel_id=1, source_target_pairs={{0,8},{8,16},{16,24},{24,0},{1,9},{9,17},{17,25},{25,1},{2,10},{10... | collective-permute-start | bytes 786440 | tf_op jit(solution)/shard_map/ppermute | solution.py:40
  137.2 15.3 %collective-permute-start.12 = (bf16[256,512]{1,0:T(8,128)(2,1)S(1)}, bf16[256,512]{1,0:T(8,128)(2,1)}, u32[]{:S(2)}, u32[]{:S(2)}) collective-permute-start(bf16[256,512]{1,0:T(8,128)(2,1)S(1)} %collective-permute-done.10.refs_1_), channel_id=1, source_target_pairs={{0,8},{8,16},{16,24},{24,0},{1,9},{9,17},{17,25},{25,1},{2,10},{10... | collective-permute-start | bytes 786440 | tf_op jit(solution)/shard_map/ppermute | solution.py:40
  143.2 9.3 %collective-permute-start.15 = (bf16[256,512]{1,0:T(8,128)(2,1)S(1)}, bf16[256,512]{1,0:T(8,128)(2,1)}, u32[]{:S(2)}, u32[]{:S(2)}) collective-permute-start(bf16[256,512]{1,0:T(8,128)(2,1)S(1)} %collective-permute-done.14.refs_6_), channel_id=1, source_target_pairs={{0,24},{8,0},{16,8},{24,16},{1,25},{9,1},{17,9},{25,17},{2,26},{10... | collective-permute-start | bytes 786440 | tf_op jit(solution)/shard_map/ppermute | solution.py:40
  145.7 1.0 copy-start.4
  146.6 0.9 copy-start.6
  152.2 5.7 %collective-permute-start.29 = (bf16[4,512,128]{2,1,0:T(8,128)(2,1)S(1)}, bf16[4,512,128]{2,1,0:T(8,128)(2,1)S(1)}, u32[]{:S(2)}, u32[]{:S(2)}) collective-permute-start(bf16[4,512,128]{2,1,0:T(8,128)(2,1)S(1)} %get-tuple-element.70), channel_id=1, source_target_pairs={{0,1},{1,0},{2,3},{3,2},{4,5},{5,4},{6,7},{7,6},{8,9},{9,8},{10,11... | collective-permute-start | bytes 1572872 | tf_op jit(solution)/shard_map/ppermute | solution.py:40
  157.4 5.6 %collective-permute-start.19 = (bf16[4,512,128]{2,1,0:T(8,128)(2,1)S(1)}, bf16[4,512,128]{2,1,0:T(8,128)(2,1)S(1)}, u32[]{:S(2)}, u32[]{:S(2)}) collective-permute-start(bf16[4,512,128]{2,1,0:T(8,128)(2,1)S(1)} %get-tuple-element.62), channel_id=1, source_target_pairs={{0,1},{1,0},{2,3},{3,2},{4,5},{5,4},{6,7},{7,6},{8,9},{9,8},{10,11... | collective-permute-start | bytes 1572872 | tf_op jit(solution)/shard_map/ppermute | solution.py:40
  158.6 7.1 %collective-permute-start.30 = (bf16[512,128]{1,0:T(8,128)(2,1)S(1)}, bf16[512,128]{1,0:T(8,128)(2,1)S(1)}, u32[]{:S(2)}, u32[]{:S(2)}) collective-permute-start(bf16[512,128]{1,0:T(8,128)(2,1)S(1)} %get-tuple-element.72), channel_id=1, source_target_pairs={{0,2},{2,4},{4,6},{6,0},{1,3},{3,5},{5,7},{7,1},{8,10},{10,12},{12... | collective-permute-start | bytes 393224 | tf_op jit(solution)/shard_map/ppermute | solution.py:40
  160.2 7.1 %collective-permute-start.31 = (bf16[512,128]{1,0:T(8,128)(2,1)S(1)}, bf16[512,128]{1,0:T(8,128)(2,1)S(1)}, u32[]{:S(2)}, u32[]{:S(2)}) collective-permute-start(bf16[512,128]{1,0:T(8,128)(2,1)S(1)} %get-tuple-element.73), channel_id=1, source_target_pairs={{0,6},{2,0},{4,2},{6,4},{1,7},{3,1},{5,3},{7,5},{8,14},{10,8},{12,... | collective-permute-start | bytes 393224 | tf_op jit(solution)/shard_map/ppermute | solution.py:40
  160.7 9.5 %collective-permute-start.32 = (bf16[512,128]{1,0:T(8,128)(2,1)S(1)}, bf16[512,128]{1,0:T(8,128)(2,1)S(1)}, u32[]{:S(2)}, u32[]{:S(2)}) collective-permute-start(bf16[512,128]{1,0:T(8,128)(2,1)S(1)} %get-tuple-element.74), channel_id=1, source_target_pairs={{0,4},{2,6},{4,0},{6,2},{1,5},{3,7},{5,1},{7,3},{8,12},{10,14},{12... | collective-permute-start | bytes 393224 | tf_op jit(solution)/shard_map/ppermute | solution.py:40
  163.6 7.8 %collective-permute-start.20 = (bf16[512,128]{1,0:T(8,128)(2,1)S(1)}, bf16[512,128]{1,0:T(8,128)(2,1)S(1)}, u32[]{:S(2)}, u32[]{:S(2)}) collective-permute-start(bf16[512,128]{1,0:T(8,128)(2,1)S(1)} %get-tuple-element.64), channel_id=1, source_target_pairs={{0,2},{2,4},{4,6},{6,0},{1,3},{3,5},{5,7},{7,1},{8,10},{10,12},{12... | collective-permute-start | bytes 393224 | tf_op jit(solution)/shard_map/ppermute | solution.py:40
  164.5 7.2 %collective-permute-start.21 = (bf16[512,128]{1,0:T(8,128)(2,1)S(1)}, bf16[512,128]{1,0:T(8,128)(2,1)S(1)}, u32[]{:S(2)}, u32[]{:S(2)}) collective-permute-start(bf16[512,128]{1,0:T(8,128)(2,1)S(1)} %get-tuple-element.65), channel_id=1, source_target_pairs={{0,6},{2,0},{4,2},{6,4},{1,7},{3,1},{5,3},{7,5},{8,14},{10,8},{12,... | collective-permute-start | bytes 393224 | tf_op jit(solution)/shard_map/ppermute | solution.py:40
  165.7 8.8 %collective-permute-start.22 = (bf16[512,128]{1,0:T(8,128)(2,1)S(1)}, bf16[512,128]{1,0:T(8,128)(2,1)S(1)}, u32[]{:S(2)}, u32[]{:S(2)}) collective-permute-start(bf16[512,128]{1,0:T(8,128)(2,1)S(1)} %get-tuple-element.66), channel_id=1, source_target_pairs={{0,4},{2,6},{4,0},{6,2},{1,5},{3,7},{5,1},{7,3},{8,12},{10,14},{12... | collective-permute-start | bytes 393224 | tf_op jit(solution)/shard_map/ppermute | solution.py:40
  175.2 5.6 %collective-permute-start.33 = (bf16[256,128]{1,0:T(8,128)(2,1)S(1)}, bf16[256,128]{1,0:T(8,128)(2,1)S(1)}, u32[]{:S(2)}, u32[]{:S(2)}) collective-permute-start(bf16[256,128]{1,0:T(8,128)(2,1)S(1)} %get-tuple-element.76), channel_id=1, source_target_pairs={{0,8},{8,16},{16,24},{24,0},{1,9},{9,17},{17,25},{25,1},{2,10},{10... | collective-permute-start | bytes 196616 | tf_op jit(solution)/shard_map/ppermute | solution.py:40
  175.6 5.5 %collective-permute-start.34 = (bf16[256,128]{1,0:T(8,128)(2,1)S(1)}, bf16[256,128]{1,0:T(8,128)(2,1)S(1)}, u32[]{:S(2)}, u32[]{:S(2)}) collective-permute-start(bf16[256,128]{1,0:T(8,128)(2,1)S(1)} %get-tuple-element.77), channel_id=1, source_target_pairs={{0,24},{8,0},{16,8},{24,16},{1,25},{9,1},{17,9},{25,17},{2,26},{10... | collective-permute-start | bytes 196616 | tf_op jit(solution)/shard_map/ppermute | solution.py:40
  178.5 5.8 %collective-permute-start.35 = (bf16[256,128]{1,0:T(8,128)(2,1)S(1)}, bf16[256,128]{1,0:T(8,128)(2,1)S(1)}, u32[]{:S(2)}, u32[]{:S(2)}) collective-permute-start(bf16[256,128]{1,0:T(8,128)(2,1)S(1)} %get-tuple-element.78), channel_id=1, source_target_pairs={{0,16},{8,24},{16,0},{24,8},{1,17},{9,25},{17,1},{25,9},{2,18},{10... | collective-permute-start | bytes 196616 | tf_op jit(solution)/shard_map/ppermute | solution.py:40
  (4 other events, 3.0 us)
Sparse Core Ops, SparseCore 0:
  9.1 57.6 all-gather.2

commit v2 on v1

v2 whole, which is shorter than its diff:
```python
import jax
import jax.numpy as jnp
from jax import lax
from jax.experimental import pallas as pl
from jax.experimental.pallas import tpu as pltpu
from jax.sharding import Mesh, PartitionSpec as P

SPAN = 256
NX = 4
NY = 4
HEADS = 8
HEAD_DIM = 64
WIDTH = HEADS * HEAD_DIM
STATE = 256
BC = 2 * STATE
WIDE = WIDTH + BC
F32 = jnp.float32
BF16 = jnp.bfloat16
LARGE = 48 * 1024 * 1024
SMALL = 20 * 1024 * 1024
SPECS = {
    "v": pl.BlockSpec(memory_space=pltpu.VMEM),
    "s": pl.BlockSpec(memory_space=pltpu.SMEM),
    "a": pl.BlockSpec(memory_space=pl.ANY),
    "h": pl.BlockSpec(memory_space=pl.ANY),
}


def call(kernel, spaces, args, outs, scratch=(), flops=0, nbytes=0, places=None, vmem=LARGE):
    return pl.pallas_call(
        kernel,
        in_specs=[SPECS[s] for s in spaces],
        out_specs=tuple(SPECS[s] for s in places or "v" * len(outs)),
        out_shape=tuple(jax.ShapeDtypeStruct(s, d) for s, d in outs),
        scratch_shapes=list(scratch),
        compiler_params=pltpu.CompilerParams(vmem_limit_bytes=vmem),
        cost_estimate=pl.CostEstimate(flops=flops, bytes_accessed=nbytes, transcendentals=0),
    )(*args)


def shift(v, axis, by):
    n = lax.axis_size(axis)
    return lax.ppermute(v, axis, [(i, (i + by) % n) for i in range(n)])


def around(v, by):
    return lax.rem(v + by, 4)


def sigmoid(v):
    return 0.5 * jnp.tanh(0.5 * v) + 0.5


def lanes(q, width):
    return pl.ds(pl.multiple_of(q * width, width), width)


def three_parts(v):
    hi = v.astype(BF16).astype(F32)
    mid = (v - hi).astype(BF16).astype(F32)
    return hi, mid, (v - hi - mid).astype(BF16).astype(F32)


def first_finder(lengths):
    s1 = lengths[0]
    s2 = s1 + lengths[1]
    s3 = s2 + lengths[2]
    return lambda t: jnp.where(t >= s3, s3, jnp.where(t >= s2, s2, jnp.where(t >= s1, s1, 0)))


def pack_kernel(x_any, bc_any, dt_any, own, to_next, to_prev, to_far, h0, h1, h2, h3, turned, sems):
    x = lax.axis_index("x")
    get_dt = pltpu.make_async_copy(dt_any, turned, sems.at[0])
    get_dt.start()
    copies = []

    def start(src, dst):
        copy = pltpu.make_async_copy(src, dst, sems.at[len(copies) + 1])
        copy.start()
        copies.append(copy)

    outs = ((1, to_next), (3, to_prev), (2, to_far), (0, own))
    for by, out in outs:
        q = around(x, by)
        start(x_any.at[:, lanes(q, WIDTH)], out.at[:SPAN, :WIDTH])
        start(bc_any, out.at[:SPAN, WIDTH:])
    for q, out in enumerate((h0, h1, h2, h3)):
        start(x_any.at[SPAN - 16 :, q * WIDTH : (q + 1) * WIDTH], out.at[:, :WIDTH])
        start(bc_any.at[SPAN - 16 :, :], out.at[:, WIDTH:])
    get_dt.wait()
    for by, out in outs:
        q = around(x, by)
        rows = turned[pl.ds(pl.multiple_of(q * HEADS, HEADS), HEADS), :]
        hi, mid, low = three_parts(rows)
        line = jnp.concatenate([hi, mid, low, jnp.zeros_like(low)], axis=1)
        out[SPAN:, :] = jnp.concatenate([line, jnp.zeros_like(line)], axis=0).astype(BF16)
    for copy in copies:
        copy.wait()


def split_kernel(g_any, after, own, to_next, to_prev, to_far, sems):
    x = lax.axis_index("x")
    copies = []
    for k, (by, out) in enumerate(((0, own), (1, to_next), (3, to_prev), (2, to_far))):
        copies.append(pltpu.make_async_copy(g_any.at[:, lanes(around(x, by), WIDTH)], out, sems.at[k]))
        copies[-1].start()
    for copy in copies:
        copy.wait()


def state_kernel(
    lengths, decay, own, prev, nxt, far, h0, h1, h2, h3, cw_ref, cb_ref,
    conv_hbm, cols_hbm, rows_hbm, carry_hbm, re_hbm, t_out,
    pay, ext, carry, weighted, conv_out, cols_out, rows_out, carry_out, re_out, sems,
):
    def outgoing(j):
        pairs = (
            (conv_out, conv_hbm),
            (cols_out, cols_hbm),
            (rows_out, rows_hbm),
            (carry_out, carry_hbm),
            (re_out, re_hbm),
        )
        return [
            pltpu.make_async_copy(src.at[j], dst.at[j], sems.at[k, j])
            for k, (src, dst) in enumerate(pairs)
        ]

    x = lax.axis_index("x")
    base = lax.axis_index("z") * (NX * SPAN)
    first_of = first_finder(lengths)
    pay[x] = own[...]
    pay[around(x, 3)] = prev[...]
    pay[around(x, 1)] = nxt[...]
    pay[around(x, 2)] = far[...]
    ext[0:8] = (
        h0[8:16].astype(F32) + h1[8:16].astype(F32) + h2[8:16].astype(F32) + h3[8:16].astype(F32)
    )
    carry[...] = jnp.zeros_like(carry)
    taps_x = cw_ref[:, lanes(x, WIDTH)]
    head = lax.broadcasted_iota(jnp.int32, (HEADS, SPAN), 0)
    rates = jnp.zeros((HEADS, SPAN), F32)
    for h in range(HEADS):
        rates = jnp.where(head == h, decay[x * HEADS + h], rates)

    def turn(j, before):
        start = base + j * SPAN

        @pl.when(j > 0)
        def _():
            ext[0:8] = ext[SPAN : SPAN + 8]

        ext[8:] = pay[j, :SPAN, :].astype(F32)
        row = lax.broadcasted_iota(jnp.int32, (SPAN, 128), 0)
        lane = lax.broadcasted_iota(jnp.int32, (SPAN, 128), 1)
        lane1 = lax.broadcasted_iota(jnp.int32, (1, 128), 1)
        place = start + row
        first = first_of(place)
        pos = place - first
        for part in range(WIDE // 128):
            at = part * 128
            cols = slice(at, at + 128)

            def tap(k):
                if at < WIDTH:
                    return taps_x[k : k + 1, cols]
                return cb_ref[k][:, at - WIDTH : at - WIDTH + 128]

            acc = tap(3) * ext[8 : 8 + SPAN, cols]
            for back in (1, 2, 3):
                term = tap(3 - back) * ext[8 - back : 8 - back + SPAN, cols]
                acc = acc + jnp.where(pos >= back, term, 0.0)
            conv_out[j, :, cols] = (acc * sigmoid(acc)).astype(BF16)
        packed = pay[j, SPAN:, :][:HEADS].astype(F32)
        raw = packed[:, :SPAN] + packed[:, SPAN : 2 * SPAN] + packed[:, 2 * SPAN : 3 * SPAN]
        step = jnp.maximum(raw, 0.0) + jnp.log1p(jnp.exp(-jnp.abs(raw)))
        parts = jnp.concatenate(
            [*three_parts(-rates * step), jnp.zeros((HEADS, SPAN), F32)], axis=0
        ).astype(BF16)
        wide_s = lax.broadcasted_iota(jnp.int32, (SPAN, SPAN), 0)
        wide_t = lax.broadcasted_iota(jnp.int32, (SPAN, SPAN), 1)
        upper = jnp.where(wide_s <= wide_t, 1.0, 0.0).astype(BF16)
        sums = jnp.dot(parts, upper, preferred_element_type=F32)
        logd = sums[:HEADS] + sums[HEADS : 2 * HEADS] + sums[2 * HEADS : 3 * HEADS]
        both = jnp.concatenate([logd, step], axis=0)
        rows_out[j] = both
        cols = jnp.transpose(
            jnp.concatenate([both, jnp.zeros((128 - 2 * HEADS, SPAN), F32)], axis=0)
        )
        cols_out[j] = cols
        first_end = first_of(start + SPAN - 1)
        keep = place >= first_end
        carried = jnp.where(first_end < start, 1.0, 0.0)
        end = cols[SPAN - 1 : SPAN, :]
        re_out[j] = jnp.where(first < base, jnp.exp(jnp.minimum(cols + before, 0.0)), 0.0)
        left = lane < HEAD_DIM
        left1 = lane1 < HEAD_DIM
        decays = []
        for pair in range(HEADS // 2):
            at = slice(pair * 128, pair * 128 + 128)
            h = 2 * pair
            log2 = jnp.where(left, cols[:, h : h + 1], cols[:, h + 1 : h + 2])
            s = HEADS + h
            step2 = jnp.where(left, cols[:, s : s + 1], cols[:, s + 1 : s + 2])
            end2 = jnp.where(left1, end[:, h : h + 1], end[:, h + 1 : h + 2])
            inputs = jnp.where(keep, jnp.exp(end2 - log2) * step2, 0.0) * conv_out[j, :, at].astype(F32)
            weighted[:, at] = inputs.astype(BF16)
            decays.append(jnp.exp(end2) * carried)
        keys = conv_out[j, :, WIDTH : WIDTH + STATE]
        states = lax.dot_general(
            keys, weighted[...], (((0,), (0,)), ((), ())), preferred_element_type=F32
        )
        state = carry[...]
        carry_out[j] = state.astype(BF16)
        carry[...] = jnp.concatenate(decays, axis=1) * state + states
        for copy in outgoing(j):
            copy.start()
        return before + jnp.where(lane1 < HEADS, end, 0.0)

    total = lax.fori_loop(0, NX, turn, jnp.zeros((1, 128), F32))
    last = first_of(base + NX * SPAN - 1)
    lane1 = lax.broadcasted_iota(jnp.int32, (1, 128), 1)
    whole = jnp.where(last < base, jnp.exp(total), 0.0)
    spread = jnp.concatenate(
        [
            jnp.where(lane1 < HEAD_DIM, whole[:, h : h + 1], whole[:, h + 1 : h + 2])
            for h in range(0, HEADS, 2)
        ],
        axis=1,
    )
    hi = spread.astype(BF16).astype(F32)
    which = lax.broadcasted_iota(jnp.int32, (16, WIDTH), 0)
    marks = jnp.where(which == 0, hi, jnp.where(which == 1, spread - hi, 0.0)).astype(BF16)
    parts = t_out.shape[0]
    rows = STATE // parts
    for k in range(parts):
        t_out[k, :rows] = carry[k * rows : (k + 1) * rows].astype(BF16)
        t_out[k, rows:] = marks

    def finish(j, token):
        for copy in outgoing(j):
            copy.wait()
        return token

    lax.fori_loop(0, NX, finish, 0)


def within_kernel(
    lengths, skip, conv_hbm, cols_hbm, rows_hbm, carry_hbm, after, y_hbm,
    gram, conv_ref, cols_ref, rows_ref, carry_ref, y_out, sems,
):
    def incoming(j):
        pairs = (
            (conv_hbm, conv_ref),
            (cols_hbm, cols_ref),
            (rows_hbm, rows_ref),
            (carry_hbm, carry_ref),
        )
        return [
            pltpu.make_async_copy(src.at[j], dst.at[j], sems.at[k, j])
            for k, (src, dst) in enumerate(pairs)
        ]

    def result(j):
        return pltpu.make_async_copy(y_out.at[j], y_hbm.at[j], sems.at[4, j])

    def begin(j, token):
        for copy in incoming(j):
            copy.start()
        return token

    lax.fori_loop(0, NX, begin, 0)
    x = lax.axis_index("x")
    base = lax.axis_index("z") * (NX * SPAN)
    first_of = first_finder(lengths)
    half = SPAN // 2

    def turn(j, token):
        for copy in incoming(j):
            copy.wait()
        start = base + j * SPAN
        row = lax.broadcasted_iota(jnp.int32, (SPAN, 128), 0)
        lane = lax.broadcasted_iota(jnp.int32, (SPAN, 128), 1)
        left = lane < HEAD_DIM
        left1 = lax.broadcasted_iota(jnp.int32, (1, 128), 1) < HEAD_DIM
        entered = first_of(start + row) < start
        keys = conv_ref[j, :, WIDTH : WIDTH + STATE]
        query = conv_ref[j, :, WIDTH + STATE :]
        dots = lax.dot_general(query, keys, (((1,), (1,)), ((), ())), preferred_element_type=F32)
        wide_t = lax.broadcasted_iota(jnp.int32, (SPAN, SPAN), 0)
        wide_s = lax.broadcasted_iota(jnp.int32, (SPAN, SPAN), 1)
        wide_first = first_of(start + wide_t)
        gram[...] = jnp.where((wide_s <= wide_t) & (start + wide_s >= wide_first), dots, 0.0)
        across = jnp.dot(query, carry_ref[j], preferred_element_type=F32)
        cols = cols_ref[j]
        rows = rows_ref[j]
        for pair in range(HEADS // 2):
            at = slice(pair * 128, pair * 128 + 128)
            xs = conv_ref[j, :, at]
            tops, bottoms = [], []
            for h in (2 * pair, 2 * pair + 1):
                column = cols[:, h : h + 1]
                log_row = rows[h : h + 1, :]
                weight = rows[HEADS + h : HEADS + h + 1, :]
                top = jnp.exp(jnp.minimum(column[:half] - log_row[:, :half], 0.0)) * (
                    gram[:half, :half] * weight[:, :half]
                )
                bottom = jnp.exp(jnp.minimum(column[half:] - log_row, 0.0)) * (
                    gram[half:, :] * weight
                )
                tops.append(jnp.dot(top.astype(BF16), xs[:half], preferred_element_type=F32))
                bottoms.append(jnp.dot(bottom.astype(BF16), xs, preferred_element_type=F32))
            within = jnp.concatenate(
                [
                    jnp.where(left[:half], tops[0], tops[1]),
                    jnp.where(left[half:], bottoms[0], bottoms[1]),
                ],
                axis=0,
            )
            h = 2 * pair
            log2 = jnp.where(left, cols[:, h : h + 1], cols[:, h + 1 : h + 2])
            reach = jnp.where(entered, jnp.exp(log2), 0.0)
            direct = jnp.where(left1, skip[x * HEADS + h], skip[x * HEADS + h + 1])
            y_out[j, :, at] = within + reach * across[:, at] + direct * xs.astype(F32)
        result(j).start()
        return token

    lax.fori_loop(0, NX, turn, 0)

    def finish(j, token):
        result(j).wait()
        return token

    lax.fori_loop(0, NX, finish, 0)


def scan_kernel(t_ref, *refs):
    e_out = refs[-1]
    parts, rows, _ = e_out.shape
    state = jnp.zeros(e_out.shape[1:], F32)
    for k in range(parts):
        e_out[k] = state.astype(BF16)
        if k < parts - 1:
            marks = t_ref[k, rows:].astype(F32)
            state = (marks[0:1] + marks[1:2]) * state + t_ref[k, :rows].astype(F32)


def gate_kernel(own, prev, nxt, far, y_hbm, conv_hbm, re_hbm, e_ref, gain_ref, *refs):
    *outs, gate, y_ref, query, re_ref, sems = refs[1:]
    x = lax.axis_index("x")
    copies = []
    for j in range(NX):
        b = j
        for src, dst in (
            (y_hbm.at[j], y_ref.at[b]),
            (conv_hbm.at[j, :, WIDTH + STATE :], query.at[b]),
            (re_hbm.at[j], re_ref.at[b]),
        ):
            copies.append(pltpu.make_async_copy(src, dst, sems.at[len(copies)]))
            copies[-1].start()
    gets = []
    for k, (by, src) in enumerate(((0, own), (3, prev), (1, nxt), (2, far))):
        gets.append(pltpu.make_async_copy(src, gate.at[around(x, by)], sems.at[12 + k]))
        gets[-1].start()
    for get in gets:
        get.wait()
    gain = gain_ref[:, lanes(x, WIDTH)]
    left = lax.broadcasted_iota(jnp.int32, (SPAN, 128), 1) < HEAD_DIM
    for b, out in enumerate(outs):
        for copy in copies[3 * b : 3 * b + 3]:
            copy.wait()
        across = jnp.dot(query[b], e_ref[...], preferred_element_type=F32)
        reach = re_ref[b]
        for pair in range(HEADS // 2):
            cols = slice(pair * 128, pair * 128 + 128)
            h = 2 * pair
            reach2 = jnp.where(left, reach[:, h : h + 1], reach[:, h + 1 : h + 2])
            g = gate[b, :, cols].astype(F32)
            v = (y_ref[b, :, cols] + reach2 * across[:, cols]) * (g * sigmoid(g))
            out[:, cols] = (v * gain[:, cols]).astype(BF16)


def product_kernel(*refs):
    gain_ref, w_ref = refs[8:10]
    send, kept, left = refs[-3:]
    x, c = lax.axis_index("x"), lax.axis_index("c")
    order = (x, around(x, 3), around(x, 1), around(x, 2))
    for k, ref in enumerate(refs[:8]):
        left[k // 4 * SPAN : k // 4 * SPAN + SPAN, lanes(order[k % 4], WIDTH)] = ref[...]
    plain = left[...] * (1.0 / gain_ref[...]).astype(BF16)
    ones = jnp.ones((NX * WIDTH, 128), BF16)
    mean = jnp.dot(plain * plain, ones, preferred_element_type=F32) * (1.0 / (NX * WIDTH))
    scale = lax.rsqrt(mean + 1e-05)
    scale = jnp.concatenate([scale, scale], axis=1)
    for core, out in ((1 - c, send), (c, kept)):
        for yy in range(0, NY, 2):
            w = jnp.concatenate([w_ref[2 * yy + core], w_ref[2 * yy + 2 + core]], axis=1)
            acc = jnp.dot(left[...], w, preferred_element_type=F32)
            acc = (acc * scale).astype(out.dtype)
            out[yy] = acc[:, :128]
            out[yy + 1] = acc[:, 128:]


def hold_kernel(w_any, after, out, sem):
    copy = pltpu.make_async_copy(w_any, out, sem)
    copy.start()
    copy.wait()


def cores_kernel(kept, got, to_next, to_prev, to_far, mine):
    y = lax.axis_index("y")
    for by, out in ((1, to_next), (3, to_prev), (2, to_far), (0, mine)):
        q = around(y, by)
        out[...] = (kept[q] + got[q].astype(F32)).astype(out.dtype)


def rows_kernel(a0, a1, a2, a3, b0, b1, b2, b3, own, to_next, to_prev, to_far, whole):
    x = lax.axis_index("x")
    first = a0[...] + a1[...].astype(F32) + a2[...].astype(F32) + a3[...].astype(F32)
    second = b0[...] + b1[...].astype(F32) + b2[...].astype(F32) + b3[...].astype(F32)
    whole[0] = first[:SPAN]
    whole[1] = first[SPAN:]
    whole[2] = second[:SPAN]
    whole[3] = second[SPAN:]
    for by, out in ((0, own), (1, to_next), (3, to_prev), (2, to_far)):
        out[...] = whole[around(x, by)].astype(BF16)


def place_kernel(own, prev, nxt, far, out):
    x = lax.axis_index("x")
    for by, got in ((0, own), (3, prev), (1, nxt), (2, far)):
        out[:, lanes(around(x, by), 128)] = got[...]


def on_device(
    x_in, bc_in, gate_in, dt_raw, decay_rate, skip_gain, conv_x, conv_bc, norm_gain, out_weight, lengths
):
    nz = lax.axis_size("z")
    bc = bc_in.reshape(SPAN, BC)
    w_all = lax.all_gather(out_weight, "z", axis=0)

    piece = ((SPAN + 16, WIDE), BF16)
    edge = ((16, WIDE), BF16)
    own, to_next, to_prev, to_far, *edges = call(
        pack_kernel, "hhh", (x_in, bc, dt_raw.T), [piece] * 4 + [edge] * 4,
        [
            pltpu.VMEM((4 * HEADS, SPAN), F32),
            pltpu.SemaphoreType.DMA((17,)),
        ],
        nbytes=6 << 20,
    )
    far = shift(to_far, "x", 2)
    prev, nxt = shift(to_next, "x", 1), shift(to_prev, "x", -1)
    halo = [
        lax.ppermute(e, ("z", "x"), [((z - 1) * NX + NX - 1, z * NX + k) for z in range(1, nz)])
        for k, e in enumerate(edges)
    ]
    quarter = ((SPAN, WIDTH), BF16)
    g_own, g_next, g_prev, g_far = call(
        split_kernel, "ha", (gate_in, far), [quarter] * 4, [pltpu.SemaphoreType.DMA((4,))],
        nbytes=2 << 20,
    )
    gates = (g_own, shift(g_next, "x", 1), shift(g_prev, "x", -1), shift(g_far, "x", 2))

    gain = norm_gain[None, :]
    rows = STATE // nz
    kept_specs = [
        pltpu.VMEM((NX, SPAN, WIDE), BF16),
        pltpu.VMEM((NX, SPAN, 128), F32),
        pltpu.VMEM((NX, 2 * HEADS, SPAN), F32),
        pltpu.VMEM((NX, STATE, WIDTH), BF16),
        pltpu.VMEM((NX, SPAN, 128), F32),
    ]
    conv, cols, lines, carry, reach, sums = call(
        state_kernel, "ss" + "v" * 10,
        (lengths, decay_rate, own, prev, nxt, far, *halo, conv_x, conv_bc),
        [
            ((NX, SPAN, WIDE), BF16),
            ((NX, SPAN, 128), F32),
            ((NX, 2 * HEADS, SPAN), F32),
            ((NX, STATE, WIDTH), BF16),
            ((NX, SPAN, 128), F32),
            ((nz, rows + 16, WIDTH), BF16),
        ],
        [
            pltpu.VMEM((NX, SPAN + 16, WIDE), BF16),
            pltpu.VMEM((SPAN + 8, WIDE), F32),
            pltpu.VMEM((STATE, WIDTH), F32),
            pltpu.VMEM((SPAN, WIDTH), BF16),
            *kept_specs,
            pltpu.SemaphoreType.DMA((5, NX)),
        ],
        flops=4 << 30, nbytes=16 << 20, places="hhhhhv",
    )
    spread = lax.all_to_all(sums, "z", 0, 0, tiled=True)
    (y_loc,) = call(
        within_kernel, "sshhhha", (lengths, skip_gain, conv, cols, lines, carry, g_own),
        [((NX, SPAN, WIDTH), F32)],
        [
            pltpu.VMEM((SPAN, SPAN), F32),
            *kept_specs[:4],
            pltpu.VMEM((NX, SPAN, WIDTH), F32),
            pltpu.SemaphoreType.DMA((5, NX)),
        ],
        flops=6 << 30, nbytes=16 << 20, places="h",
    )
    (enter,) = call(
        scan_kernel, "vhaaa", (spread, y_loc, *gates[1:]), [((nz, rows, WIDTH), BF16)], nbytes=1 << 20
    )
    enter = lax.all_to_all(enter, "z", 0, 0, tiled=True).reshape(STATE, WIDTH)

    halves = []
    v = call(
        gate_kernel, "aaaahhhvva", (*gates, y_loc, conv, reach, enter, gain, w_all),
        [quarter] * NX,
        [
            pltpu.VMEM((NX, SPAN, WIDTH), BF16),
            pltpu.VMEM((NX, SPAN, WIDTH), F32),
            pltpu.VMEM((NX, SPAN, STATE), BF16),
            pltpu.VMEM((NX, SPAN, 128), F32),
            pltpu.SemaphoreType.DMA((16,)),
        ],
        flops=2 << 30, nbytes=6 << 20,
    )
    parts = []
    for k, o in enumerate(v):
        a, b = shift(o, "x", 1), shift(o, "x", -1)
        parts += [o, a, b, shift(a, "x", 1) if k % 2 == 0 else shift(b, "x", -1)]
    gathered = (parts[:8], parts[8:])
    (w_near,) = call(
        hold_kernel, "aa", (w_all, v[-1]), [((nz, NX * WIDTH, 128), BF16)],
        [pltpu.SemaphoreType.DMA(())], nbytes=1 << 20, vmem=SMALL,
    )
    after = tuple(parts[k] for k in (9, 10, 11, 13, 14, 15))
    for parts in gathered:
        send, kept = call(
            product_kernel, "v" * 10 + "a" * len(after), (*parts, gain, w_near, *after),
            [((NY, 2 * SPAN, 128), BF16), ((NY, 2 * SPAN, 128), F32)],
            [
                pltpu.VMEM((2 * SPAN, NX * WIDTH), BF16),
            ],
            flops=3 << 30, nbytes=8 << 20, vmem=SMALL,
        )
        got = shift(send, "c", 1)
        part = ((2 * SPAN, 128), BF16)
        y_next, y_prev, y_far, mine = call(
            cores_kernel, "vv", (kept, got), [part] * 3 + [((2 * SPAN, 128), F32)], nbytes=2 << 20, vmem=SMALL
        )
        after = ()
        halves += [mine, shift(y_next, "y", 1), shift(y_prev, "y", -1), shift(y_far, "y", 2)]
    tile = ((SPAN, 128), BF16)
    own, to_next, to_prev, to_far = call(
        rows_kernel, "v" * 8, halves, [tile] * 4, [pltpu.VMEM((NX, SPAN, 128), F32)], nbytes=2 << 20, vmem=SMALL
    )
    (mixed,) = call(
        place_kernel, "vvvv",
        (own, shift(to_next, "x", 1), shift(to_prev, "x", -1), shift(to_far, "x", 2)),
        [((SPAN, NX * 128), BF16)], nbytes=1 << 20, vmem=SMALL,
    )
    return mixed


def solution(mesh):
    seq, tp = ("z", "x"), ("y", "c")
    fine = Mesh(mesh.devices.reshape(mesh.devices.shape[0] // NX, NX, NY, 2), seq + tp)
    in_specs = (
        P(seq, tp),
        P(seq, tp, None),
        P(seq, tp),
        P(seq, tp),
        P(tp),
        P(tp),
        P(None, tp),
        P(None, tp, None),
        P(tp),
        P(tp, seq),
        P(),
    )
    return jax.shard_map(
        on_device, mesh=fine, in_specs=in_specs, out_specs=P(seq, tp), check_vma=False
    )
```

time: 193 us -> 174 us (0.902)
  waiting for transfers between devices: 59 us -> 51.2 us
  blocking collectives: 22.1 us -> 17.4 us
  local copies, waits for them, and re-layouts: 19.3 us -> 14.7 us
  Pallas kernels: 30.5 us -> 27.5 us
    ppermute x32 -> x29, waiting for transfers between devices: 58.3 us -> 50.5 us  [shift(): return lax.ppermute(v, axis, [(i, (i + by) % n) for i in range(n)])]
    all_to_all x1, starting transfers between devices: 3.41 us -> 9.04 us  [on_device(): spread = lax.all_to_all(sums, 'z', 0, 0, tiled=True)]
    all_to_all x1, blocking collectives: 22.1 us -> 17.4 us  [on_device(): enter = lax.all_to_all(enter, 'z', 0, 0, tiled=True).reshape(STATE, WIDTH)]
    ppermute x32 -> x29, starting transfers between devices: 41.1 us -> 37.3 us  [shift(): return lax.ppermute(v, axis, [(i, (i + by) % n) for i in range(n)])]
    pallas_call x11 -> x13, Pallas kernels: 30.5 us -> 27.5 us  [call(): pl.pallas_call(kernel, in_specs=[SPECS[s] for s in spaces], out_specs=tup...]
    another operation x2 -> x0, local copies, waits for them, and re-layouts: 2.68 us -> none  [the longest x1 2.6 us: on_device(): jnp.stack([xi, zi, lax.axis_index('y'), lax.axis_index('c'), ends[0], end...]
    dynamic_slice x3 -> x0, local copies, waits for them, and re-layouts: 2.23 us -> none  [the longest x1 0.76 us: on_device(): gain = lax.dynamic_slice(norm_gain, (xi * WIDTH,), (WIDTH,))[None, :]]
    unnamed x30 -> x42, local copies, waits for them, and re-layouts: 13.6 us -> 14.7 us
  transfers between devices with their start and end apart: 38 -> 35, of which waited for: 17 -> 16; matrix products, arithmetic and copies ran while one was open for 4% -> 0% of each run, Pallas kernels for 15% -> 14%
where the time goes in v2:
time: 174 us
  waiting for transfers between devices  51.2 us (29%)
  starting transfers between devices  49 us (28%)
  Pallas kernels  27.5 us (16%)
  blocking collectives  17.4 us (10%)
  local copies, waits for them, and re-layouts  14.7 us (8%)
  between operations  13.7 us (8%)
    ppermute x29, waiting for transfers between devices, shift(): return lax.ppermute(v, axis, [(i, (i + by) % n) for i in range(n)])  50.5 us
    ppermute x29, starting transfers between devices, shift(): return lax.ppermute(v, axis, [(i, (i + by) % n) for i in range(n)])  37.3 us
    pallas_call x13, Pallas kernels, call(): pl.pallas_call(kernel, in_specs=[SPECS[s] for s in spaces], out_specs=tup...  27.5 us
    all_to_all x1, blocking collectives, on_device(): enter = lax.all_to_all(enter, 'z', 0, 0, tiled=True).reshape(STATE, WIDTH)  17.4 us
    unnamed x42, local copies, waits for them, and re-layouts  14.7 us
    all_to_all x1, starting transfers between devices, on_device(): spread = lax.all_to_all(sums, 'z', 0, 0, tiled=True)  9.04 us
  transfers between devices with their start and end apart: 35, of which 16 were waited for; matrix products, arithmetic and copies ran while one was open for 0% of the time, Pallas kernels for 14%

profile of v2, /device:TPU:8, one launch (start us, length us, event | category | flops | bytes accessed | tf_op | source)
XLA Modules:
  0.0 173.5 jit_solution(1633842170379166592)
XLA Ops:
  7.3 1.2 copy-done.2
  8.5 0.9 copy-done.6
  10.7 3.1 %collective-permute-start = (bf16[272,1024]{1,0:T(8,128)(2,1)S(1)}, bf16[272,1024]{1,0:T(8,128)(2,1)S(1)}, u32[]{:S(2)}, u32[]{:S(2)}) collective-permute-start(bf16[272,1024]{1,0:T(8,128)(2,1)S(1)} %get-tuple-element.43), channel_id=1, source_target_pairs={{0,16},{8,24},{16,0},{24,8},{1,17},{9,25},{17,1},{25,9},{2,18},{10... | collective-permute-start | bytes 1671176 | tf_op jit(solution)/shard_map/ppermute | solution.py:43
  14.4 2.6 %collective-permute-start.5 = (bf16[272,1024]{1,0:T(8,128)(2,1)S(1)}, bf16[272,1024]{1,0:T(8,128)(2,1)S(1)}, u32[]{:S(2)}, u32[]{:S(2)}) collective-permute-start(bf16[272,1024]{1,0:T(8,128)(2,1)S(1)} %get-tuple-element.50), channel_id=1, source_target_pairs={{0,24},{8,0},{16,8},{24,16},{1,25},{9,1},{17,9},{25,17},{2,26},{10... | collective-permute-start | bytes 1671176 | tf_op jit(solution)/shard_map/ppermute | solution.py:43
  19.7 8.1 %collective-permute-done.after.far = bf16[272,1024]{1,0:T(8,128)(2,1)S(1)} collective-permute-done((bf16[272,1024]{1,0:T(8,128)(2,1)S(1)}, bf16[272,1024]{1,0:T(8,128)(2,1)S(1)}, u32[]{:S(2)}, u32[]{:S(2)}) %collective-permute-start) | collective-permute-done | bytes 557088 | tf_op jit(solution)/shard_map/ppermute | solution.py:43
  27.8 10.7 %collective-permute-done.4.prev = bf16[272,1024]{1,0:T(8,128)(2,1)S(1)} collective-permute-done((bf16[272,1024]{1,0:T(8,128)(2,1)S(1)}, bf16[272,1024]{1,0:T(8,128)(2,1)S(1)}, u32[]{:S(2)}, u32[]{:S(2)}) %collective-permute-start.4) | collective-permute-done | bytes 557088 | tf_op jit(solution)/shard_map/ppermute | solution.py:43
  41.5 11.0 %shard_map.111 = (bf16[4,256,1024]{2,1,0:T(8,128)(2,1)}, f32[4,256,128]{2,1,0:T(8,128)S(1)}, f32[4,16,256]{2,1,0:T(8,128)S(1)}, bf16[4,256,512]{2,1,0:T(8,128)(2...) custom-call(s32[4]{0:T(128)S(1)} %copy-done.12, f32[32]{0:T(128)S(1)} %copy-done.11, ...), custom_call_target="tpu_custom_call" | custom-call | flops 4294967296 | bytes 16777216 | tf_op jit(solution)/shard_map/pallas_call | solution.py:30
  52.5 0.8 copy-done.4
  53.3 1.0 copy-done.15
  54.3 0.8 copy-done.17
  55.8 9.0 %all-to-all-start = ((bf16[8,48,512]{2,1,0:T(8,128)(2,1)}), bf16[8,48,512]{2,1,0:T(8,128)(2,1)S(1)}, u32[]{:S(2)}, u32[]{:S(2)}) async-start(bf16[8,48,512]{2,1,0:T(8,128)(2,1)} %get-tuple-element.60), calls=%async_computation | async-start | bytes 786432 | tf_op jit(solution)/shard_map/all_to_all | solution.py:495
  65.0 1.6 collective-permute-start.1
  66.6 1.7 %collective-permute-start.2 = (bf16[256,512]{1,0:T(8,128)(2,1)S(1)}, bf16[256,512]{1,0:T(8,128)(2,1)S(1)}, u32[]{:S(2)}, u32[]{:S(2)}) collective-permute-start(bf16[256,512]{1,0:T(8,128)(2,1)S(1)} %get-tuple-element.46), channel_id=1, source_target_pairs={{0,24},{8,0},{16,8},{24,16},{1,25},{9,1},{17,9},{25,17},{2,26},{10... | collective-permute-start | bytes 786440 | tf_op jit(solution)/shard_map/ppermute | solution.py:43
  68.3 1.6 collective-permute-start.3
  69.9 1.6 copy-done.1
  71.5 1.2 copy-done.16
  72.8 1.0 copy-done.18
  73.8 0.8 copy-done.20
  74.6 5.1 %shard_map.112.refs_0_.y_hbm = f32[4,256,512]{2,1,0:T(8,128)S(1)} custom-call(s32[4]{0:T(128)S(1)} %copy-done.13, f32[32]{0:T(128)S(1)} %copy-done.14, bf16[4,256,1024]{2,1,0:T(8,128)(2,1)S(1)} %copy-done.1, f32[4,256,128]{2,1,0:T(8,128)S(1)} %copy-done.18, f32[4,16,256]{2,1,0:T(8,128)S(1)} %copy-done.20, bf16[4,256,512]{2,1,0:T(8,128)(2,1)S(1)} %copy-done.16, ...), custom_call_target="tpu_custom_call" | custom-call | flops 6442450944 | bytes 16777216 | tf_op jit(solution)/shard_map/pallas_call | solution.py:30
  80.3 17.4 %all_to_all.10 = bf16[8,32,512]{2,1,0:T(8,128)(2,1)S(1)} all-to-all(bf16[8,32,512]{2,1,0:T(8,128)(2,1)S(1)} %shard_map.113), channel_id=1, replica_groups=mesh['z'=8,'x'=4,'y'=4,'c'=2] {'z'}, dimensions={0} | all-to-all | bytes 524288 | tf_op jit(solution)/shard_map/all_to_all | solution.py:510
  97.7 1.0 copy-done.5
  98.7 2.8 %shard_map.114 = (bf16[256,512]{1,0:T(8,128)(2,1)S(1)}, bf16[256,512]{1,0:T(8,128)(2,1)S(1)}, bf16[256,512]{1,0:T(8,128)(2,1)S(1)}, bf16[256,512]{1,0:T(8,128)(2,1)S(1)}) custom-call(bf16[256,512]{1,0:T(8,128)(2,1)S(1)} %get-tuple-element.44.after.own, bf16[256,512]{1,0:T(8,128)(2,1)S(1)} %collective-permute-done.1.refs_1_.prev, ...), custom_call_target="tpu_custom_call" | custom-call | flops 2147483648 | bytes 6291456 | tf_op jit(solution)/shard_map/pallas_call | solution.py:30
  101.5 1.0 collective-permute-start.16
  102.5 2.3 %collective-permute-start.20 = (bf16[256,512]{1,0:T(8,128)(2,1)S(1)}, bf16[256,512]{1,0:T(8,128)(2,1)S(1)}, u32[]{:S(2)}, u32[]{:S(2)}) collective-permute-start(bf16[256,512]{1,0:T(8,128)(2,1)S(1)} %get-tuple-element.63.after.refs_4_), channel_id=1, source_target_pairs={{0,24},{8,0},{16,8},{24,16},{1,25},{9,1},{17,9},{25,17},{2,26},{10... | collective-permute-start | bytes 786440 | tf_op jit(solution)/shard_map/ppermute | solution.py:43
  104.8 1.3 collective-permute-start.17
  106.1 0.8 collective-permute-start.19
  106.9 5.0 %collective-permute-done.16.refs_10_.refs_1_ = bf16[256,512]{1,0:T(8,128)(2,1)S(1)} collective-permute-done((bf16[256,512]{1,0:T(8,128)(2,1)S(1)}, bf16[256,512]{1,0:T(8,128)(2,1)S(1)}, u32[]{:S(2)}, u32[]{:S(2)}) %collective-permute-start.16) | collective-permute-done | bytes 262176 | tf_op jit(solution)/shard_map/ppermute | solution.py:43
  111.9 1.4 collective-permute-start.14
  114.0 3.4 %collective-permute-done.17.refs_11_.refs_2_ = bf16[256,512]{1,0:T(8,128)(2,1)S(1)} collective-permute-done((bf16[256,512]{1,0:T(8,128)(2,1)S(1)}, bf16[256,512]{1,0:T(8,128)(2,1)S(1)}, u32[]{:S(2)}, u32[]{:S(2)}) %collective-permute-start.17) | collective-permute-done | bytes 262176 | tf_op jit(solution)/shard_map/ppermute | solution.py:43
  117.4 3.5 %collective-permute-start.21 = (bf16[256,512]{1,0:T(8,128)(2,1)S(1)}, bf16[256,512]{1,0:T(8,128)(2,1)S(1)}, u32[]{:S(2)}, u32[]{:S(2)}) collective-permute-start(bf16[256,512]{1,0:T(8,128)(2,1)S(1)} %collective-permute-done.20.refs_14_.refs_6_), channel_id=1, source_target_pairs={{0,24},{8,0},{16,8},{24,16},{1,25},{9,1},{17,9},{25,17},{2,26},{10... | collective-permute-start | bytes 786440 | tf_op jit(solution)/shard_map/ppermute | solution.py:43
  121.3 1.8 %collective-permute-done.10.refs_1_ = bf16[256,512]{1,0:T(8,128)(2,1)S(1)} collective-permute-done((bf16[256,512]{1,0:T(8,128)(2,1)S(1)}, bf16[256,512]{1,0:T(8,128)(2,1)S(1)}, u32[]{:S(2)}, u32[]{:S(2)}) %collective-permute-start.10) | collective-permute-done | bytes 262176 | tf_op jit(solution)/shard_map/ppermute | solution.py:43
  123.9 4.8 %collective-permute-done.18.refs_12_.refs_3_ = bf16[256,512]{1,0:T(8,128)(2,1)S(1)} collective-permute-done((bf16[256,512]{1,0:T(8,128)(2,1)S(1)}, bf16[256,512]{1,0:T(8,128)(2,1)S(1)}, u32[]{:S(2)}, u32[]{:S(2)}) %collective-permute-start.18) | collective-permute-done | bytes 262176 | tf_op jit(solution)/shard_map/ppermute | solution.py:43
  128.8 1.4 collective-permute-start.15
  130.2 3.2 %shard_map.118 = (bf16[4,512,128]{2,1,0:T(8,128)(2,1)S(1)}, f32[4,512,128]{2,1,0:T(8,128)S(1)}) custom-call(bf16[256,512]{1,0:T(8,128)(2,1)S(1)} %get-tuple-element.64.refs_0_, bf16[256,512]{1,0:T(8,128)(2,1)S(1)} %collective-permute-done.16.refs_10_.refs_1_, bf16[256,512]{1,0:T(8,128)(2,1)S(1)} %collective-permute-done.17.refs_11_.refs_2_, ...), custom_call_target="tpu_custom_call" | custom-call | flops 3221225472 | bytes 8388608 | tf_op jit(solution)/shard_map/pallas_call | solution.py:30
  133.9 2.8 %collective-permute-done.12.refs_3_ = bf16[256,512]{1,0:T(8,128)(2,1)S(1)} collective-permute-done((bf16[256,512]{1,0:T(8,128)(2,1)S(1)}, bf16[256,512]{1,0:T(8,128)(2,1)S(1)}, u32[]{:S(2)}, u32[]{:S(2)}) %collective-permute-start.12) | collective-permute-done | bytes 262176 | tf_op jit(solution)/shard_map/ppermute | solution.py:43
  136.7 3.2 %shard_map.116 = (bf16[4,512,128]{2,1,0:T(8,128)(2,1)S(1)}, f32[4,512,128]{2,1,0:T(8,128)S(1)}) custom-call(bf16[256,512]{1,0:T(8,128)(2,1)S(1)} %get-tuple-element.61.refs_0_, bf16[256,512]{1,0:T(8,128)(2,1)S(1)} %collective-permute-done.10.refs_1_, bf16[256,512]{1,0:T(8,128)(2,1)S(1)} %collective-permute-done.11.refs_2_, ...), custom_call_target="tpu_custom_call" | custom-call | flops 3221225472 | bytes 8388608 | tf_op jit(solution)/shard_map/pallas_call | solution.py:30
  140.2 1.7 collective-permute-start.27
  142.3 2.3 %collective-permute-start.29 = (bf16[512,128]{1,0:T(8,128)(2,1)S(1)}, bf16[512,128]{1,0:T(8,128)(2,1)S(1)}, u32[]{:S(2)}, u32[]{:S(2)}) collective-permute-start(bf16[512,128]{1,0:T(8,128)(2,1)S(1)} %get-tuple-element.76), channel_id=1, source_target_pairs={{0,4},{2,6},{4,0},{6,2},{1,5},{3,7},{5,1},{7,3},{8,12},{10,14},{12... | collective-permute-start | bytes 393224 | tf_op jit(solution)/shard_map/ppermute | solution.py:43
  144.7 0.9 collective-permute-start.23
  145.6 1.2 collective-permute-start.24
  146.8 2.1 %collective-permute-start.25 = (bf16[512,128]{1,0:T(8,128)(2,1)S(1)}, bf16[512,128]{1,0:T(8,128)(2,1)S(1)}, u32[]{:S(2)}, u32[]{:S(2)}) collective-permute-start(bf16[512,128]{1,0:T(8,128)(2,1)S(1)} %get-tuple-element.70), channel_id=1, source_target_pairs={{0,4},{2,6},{4,0},{6,2},{1,5},{3,7},{5,1},{7,3},{8,12},{10,14},{12... | collective-permute-start | bytes 393224 | tf_op jit(solution)/shard_map/ppermute | solution.py:43
  148.9 2.9 %collective-permute-done.29.b3 = bf16[512,128]{1,0:T(8,128)(2,1)S(1)} collective-permute-done((bf16[512,128]{1,0:T(8,128)(2,1)S(1)}, bf16[512,128]{1,0:T(8,128)(2,1)S(1)}, u32[]{:S(2)}, u32[]{:S(2)}) %collective-permute-start.29) | collective-permute-done | bytes 131104 | tf_op jit(solution)/shard_map/ppermute | solution.py:43
  151.8 1.4 collective-permute-done.23.a1
  153.3 3.4 %collective-permute-done.25.a3 = bf16[512,128]{1,0:T(8,128)(2,1)S(1)} collective-permute-done((bf16[512,128]{1,0:T(8,128)(2,1)S(1)}, bf16[512,128]{1,0:T(8,128)(2,1)S(1)}, u32[]{:S(2)}, u32[]{:S(2)}) %collective-permute-start.25) | collective-permute-done | bytes 131104 | tf_op jit(solution)/shard_map/ppermute | solution.py:43
  156.9 3.2 %collective-permute-start.31 = (bf16[256,128]{1,0:T(8,128)(2,1)S(1)}, bf16[256,128]{1,0:T(8,128)(2,1)S(1)}, u32[]{:S(2)}, u32[]{:S(2)}) collective-permute-start(bf16[256,128]{1,0:T(8,128)(2,1)S(1)} %get-tuple-element.79), channel_id=1, source_target_pairs={{0,24},{8,0},{16,8},{24,16},{1,25},{9,1},{17,9},{25,17},{2,26},{10... | collective-permute-start | bytes 196616 | tf_op jit(solution)/shard_map/ppermute | solution.py:43
  160.6 1.7 collective-permute-done.30.prev
  162.3 3.5 %collective-permute-done.32.far = bf16[256,128]{1,0:T(8,128)(2,1)S(1)} collective-permute-done((bf16[256,128]{1,0:T(8,128)(2,1)S(1)}, bf16[256,128]{1,0:T(8,128)(2,1)S(1)}, u32[]{:S(2)}, u32[]{:S(2)}) %collective-permute-start.32) | collective-permute-done | bytes 65568 | tf_op jit(solution)/shard_map/ppermute | solution.py:43
  165.9 0.8 shard_map.121
  (79 shorter events, 13.5 us)
Async XLA Ops:
  6.5 91.2 %all-gather.3.cloned.1.call-start = ((), (), s32[]{:S(2)}) async-start(), calls=%async_computation.2 | async-start | bytes 4718592 | tf_op jit(solution)/shard_map/all_gather | solution.py:440
  7.3 1.2 copy-start.2
  8.5 0.9 copy-start.6
  10.7 17.1 %collective-permute-start = (bf16[272,1024]{1,0:T(8,128)(2,1)S(1)}, bf16[272,1024]{1,0:T(8,128)(2,1)S(1)}, u32[]{:S(2)}, u32[]{:S(2)}) collective-permute-start(bf16[272,1024]{1,0:T(8,128)(2,1)S(1)} %get-tuple-element.43), channel_id=1, source_target_pairs={{0,16},{8,24},{16,0},{24,8},{1,17},{9,25},{17,1},{25,9},{2,18},{10... | collective-permute-start | bytes 1671176 | tf_op jit(solution)/shard_map/ppermute | solution.py:43
  13.8 24.8 %collective-permute-start.4 = (bf16[272,1024]{1,0:T(8,128)(2,1)S(1)}, bf16[272,1024]{1,0:T(8,128)(2,1)S(1)}, u32[]{:S(2)}, u32[]{:S(2)}) collective-permute-start(bf16[272,1024]{1,0:T(8,128)(2,1)S(1)} %get-tuple-element.49), channel_id=1, source_target_pairs={{0,8},{8,16},{16,24},{24,0},{1,9},{9,17},{17,25},{25,1},{2,10},{10... | collective-permute-start | bytes 1671176 | tf_op jit(solution)/shard_map/ppermute | solution.py:43
  14.4 24.3 %collective-permute-start.5 = (bf16[272,1024]{1,0:T(8,128)(2,1)S(1)}, bf16[272,1024]{1,0:T(8,128)(2,1)S(1)}, u32[]{:S(2)}, u32[]{:S(2)}) collective-permute-start(bf16[272,1024]{1,0:T(8,128)(2,1)S(1)} %get-tuple-element.50), channel_id=1, source_target_pairs={{0,24},{8,0},{16,8},{24,16},{1,25},{9,1},{17,9},{25,17},{2,26},{10... | collective-permute-start | bytes 1671176 | tf_op jit(solution)/shard_map/ppermute | solution.py:43
  17.0 1.3 collective-permute-start.6
  17.7 1.4 collective-permute-start.7
  18.3 1.4 collective-permute-start.8
  19.0 0.7 collective-permute-start.9
  41.5 23.4 %copy-start.3 = (bf16[256,2048]{1,0:T(8,128)(2,1)S(1)}, bf16[256,2048]{1,0:T(8,128)(2,1)}, u32[]{:S(2)}) copy-start(bf16[256,2048]{1,0:T(8,128)(2,1)} %g_any.1) | copy-start | bytes 3145732
  41.5 28.5 %copy-start.13 = (s32[4]{0:T(128)S(1)}, s32[4]{0:T(128)}, u32[]{:S(2)}) copy-start(s32[4]{0:T(128)} %lengths.3) | copy-start | bytes 52
  41.5 28.5 %copy-start.14 = (f32[32]{0:T(128)S(1)}, f32[32]{0:T(128)}, u32[]{:S(2)}) copy-start(f32[32]{0:T(128)} %skip.1) | copy-start | bytes 388
  53.3 1.0 copy-start.15
  54.3 0.8 copy-start.17
  55.8 24.4 %all-to-all-start = ((bf16[8,48,512]{2,1,0:T(8,128)(2,1)}), bf16[8,48,512]{2,1,0:T(8,128)(2,1)S(1)}, u32[]{:S(2)}, u32[]{:S(2)}) async-start(bf16[8,48,512]{2,1,0:T(8,128)(2,1)} %get-tuple-element.60), calls=%async_computation | async-start | bytes 786432 | tf_op jit(solution)/shard_map/all_to_all | solution.py:495
  65.0 14.8 %collective-permute-start.1 = (bf16[256,512]{1,0:T(8,128)(2,1)S(1)}, bf16[256,512]{1,0:T(8,128)(2,1)S(1)}, u32[]{:S(2)}, u32[]{:S(2)}) collective-permute-start(bf16[256,512]{1,0:T(8,128)(2,1)S(1)} %get-tuple-element.45), channel_id=1, source_target_pairs={{0,8},{8,16},{16,24},{24,0},{1,9},{9,17},{17,25},{25,1},{2,10},{10... | collective-permute-start | bytes 786440 | tf_op jit(solution)/shard_map/ppermute | solution.py:43
  66.6 13.2 %collective-permute-start.2 = (bf16[256,512]{1,0:T(8,128)(2,1)S(1)}, bf16[256,512]{1,0:T(8,128)(2,1)S(1)}, u32[]{:S(2)}, u32[]{:S(2)}) collective-permute-start(bf16[256,512]{1,0:T(8,128)(2,1)S(1)} %get-tuple-element.46), channel_id=1, source_target_pairs={{0,24},{8,0},{16,8},{24,16},{1,25},{9,1},{17,9},{25,17},{2,26},{10... | collective-permute-start | bytes 786440 | tf_op jit(solution)/shard_map/ppermute | solution.py:43
  68.3 11.9 %collective-permute-start.3 = (bf16[256,512]{1,0:T(8,128)(2,1)S(1)}, bf16[256,512]{1,0:T(8,128)(2,1)S(1)}, u32[]{:S(2)}, u32[]{:S(2)}) collective-permute-start(bf16[256,512]{1,0:T(8,128)(2,1)S(1)} %get-tuple-element.47), channel_id=1, source_target_pairs={{0,16},{8,24},{16,0},{24,8},{1,17},{9,25},{17,1},{25,9},{2,18},{10... | collective-permute-start | bytes 786440 | tf_op jit(solution)/shard_map/ppermute | solution.py:43
  69.9 1.6 copy-start.1
  71.5 1.2 copy-start.16
  72.7 1.0 copy-start.18
  74.6 23.1 %copy-start.8 = (f32[2048]{0:T(1024)S(1)}, f32[2048]{0:T(1024)}, u32[]{:S(2)}) copy-start(f32[2048]{0:T(1024)} %param.19) | copy-start | bytes 24580
  97.7 1.0 copy-start.5
  98.7 22.2 %copy-start = (bf16[16384,128]{1,0:T(8,128)(2,1)S(1)}, bf16[16384,128]{1,0:T(8,128)(2,1)}, u32[]{:S(2)}) copy-start(bf16[16384,128]{1,0:T(8,128)(2,1)} %all-gather.3.cloned.1.call-done) | copy-start | bytes 12582916
  101.5 10.4 %collective-permute-start.16 = (bf16[256,512]{1,0:T(8,128)(2,1)S(1)}, bf16[256,512]{1,0:T(8,128)(2,1)S(1)}, u32[]{:S(2)}, u32[]{:S(2)}) collective-permute-start(bf16[256,512]{1,0:T(8,128)(2,1)S(1)} %get-tuple-element.64.refs_0_), channel_id=1, source_target_pairs={{0,8},{8,16},{16,24},{24,0},{1,9},{9,17},{17,25},{25,1},{2,10},{10... | collective-permute-start | bytes 786440 | tf_op jit(solution)/shard_map/ppermute | solution.py:43
  102.5 10.8 %collective-permute-start.20 = (bf16[256,512]{1,0:T(8,128)(2,1)S(1)}, bf16[256,512]{1,0:T(8,128)(2,1)S(1)}, u32[]{:S(2)}, u32[]{:S(2)}) collective-permute-start(bf16[256,512]{1,0:T(8,128)(2,1)S(1)} %get-tuple-element.63.after.refs_4_), channel_id=1, source_target_pairs={{0,24},{8,0},{16,8},{24,16},{1,25},{9,1},{17,9},{25,17},{2,26},{10... | collective-permute-start | bytes 786440 | tf_op jit(solution)/shard_map/ppermute | solution.py:43
  104.8 12.6 %collective-permute-start.17 = (bf16[256,512]{1,0:T(8,128)(2,1)S(1)}, bf16[256,512]{1,0:T(8,128)(2,1)S(1)}, u32[]{:S(2)}, u32[]{:S(2)}) collective-permute-start(bf16[256,512]{1,0:T(8,128)(2,1)S(1)} %get-tuple-element.64.refs_0_), channel_id=1, source_target_pairs={{0,24},{8,0},{16,8},{24,16},{1,25},{9,1},{17,9},{25,17},{2,26},{10... | collective-permute-start | bytes 786440 | tf_op jit(solution)/shard_map/ppermute | solution.py:43
  106.1 15.1 %collective-permute-start.19 = (bf16[256,512]{1,0:T(8,128)(2,1)S(1)}, bf16[256,512]{1,0:T(8,128)(2,1)S(1)}, u32[]{:S(2)}, u32[]{:S(2)}) collective-permute-start(bf16[256,512]{1,0:T(8,128)(2,1)S(1)} %get-tuple-element.63.after.refs_4_), channel_id=1, source_target_pairs={{0,8},{8,16},{16,24},{24,0},{1,9},{9,17},{17,25},{25,1},{2,10},{10... | collective-permute-start | bytes 786440 | tf_op jit(solution)/shard_map/ppermute | solution.py:43
  106.9 16.3 %collective-permute-start.10 = (bf16[256,512]{1,0:T(8,128)(2,1)S(1)}, bf16[256,512]{1,0:T(8,128)(2,1)S(1)}, u32[]{:S(2)}, u32[]{:S(2)}) collective-permute-start(bf16[256,512]{1,0:T(8,128)(2,1)S(1)} %get-tuple-element.61.refs_0_), channel_id=1, source_target_pairs={{0,8},{8,16},{16,24},{24,0},{1,9},{9,17},{17,25},{25,1},{2,10},{10... | collective-permute-start | bytes 786440 | tf_op jit(solution)/shard_map/ppermute | solution.py:43
  111.9 11.4 %collective-permute-start.14 = (bf16[256,512]{1,0:T(8,128)(2,1)S(1)}, bf16[256,512]{1,0:T(8,128)(2,1)S(1)}, u32[]{:S(2)}, u32[]{:S(2)}) collective-permute-start(bf16[256,512]{1,0:T(8,128)(2,1)S(1)} %get-tuple-element.62.refs_4_), channel_id=1, source_target_pairs={{0,24},{8,0},{16,8},{24,16},{1,25},{9,1},{17,9},{25,17},{2,26},{10... | collective-permute-start | bytes 786440 | tf_op jit(solution)/shard_map/ppermute | solution.py:43
  113.3 15.5 %collective-permute-start.18 = (bf16[256,512]{1,0:T(8,128)(2,1)S(1)}, bf16[256,512]{1,0:T(8,128)(2,1)S(1)}, u32[]{:S(2)}, u32[]{:S(2)}) collective-permute-start(bf16[256,512]{1,0:T(8,128)(2,1)S(1)} %collective-permute-done.16.refs_10_.refs_1_), channel_id=1, source_target_pairs={{0,8},{8,16},{16,24},{24,0},{1,9},{9,17},{17,25},{25,1},{2,10},{10... | collective-permute-start | bytes 786440 | tf_op jit(solution)/shard_map/ppermute | solution.py:43
  117.4 12.8 %collective-permute-start.21 = (bf16[256,512]{1,0:T(8,128)(2,1)S(1)}, bf16[256,512]{1,0:T(8,128)(2,1)S(1)}, u32[]{:S(2)}, u32[]{:S(2)}) collective-permute-start(bf16[256,512]{1,0:T(8,128)(2,1)S(1)} %collective-permute-done.20.refs_14_.refs_6_), channel_id=1, source_target_pairs={{0,24},{8,0},{16,8},{24,16},{1,25},{9,1},{17,9},{25,17},{2,26},{10... | collective-permute-start | bytes 786440 | tf_op jit(solution)/shard_map/ppermute | solution.py:43
  121.2 12.5 %collective-permute-start.11 = (bf16[256,512]{1,0:T(8,128)(2,1)S(1)}, bf16[256,512]{1,0:T(8,128)(2,1)S(1)}, u32[]{:S(2)}, u32[]{:S(2)}) collective-permute-start(bf16[256,512]{1,0:T(8,128)(2,1)S(1)} %get-tuple-element.61.refs_0_), channel_id=1, source_target_pairs={{0,24},{8,0},{16,8},{24,16},{1,25},{9,1},{17,9},{25,17},{2,26},{10... | collective-permute-start | bytes 786440 | tf_op jit(solution)/shard_map/ppermute | solution.py:43
  123.2 10.8 %collective-permute-start.13 = (bf16[256,512]{1,0:T(8,128)(2,1)S(1)}, bf16[256,512]{1,0:T(8,128)(2,1)S(1)}, u32[]{:S(2)}, u32[]{:S(2)}) collective-permute-start(bf16[256,512]{1,0:T(8,128)(2,1)S(1)} %get-tuple-element.62.refs_4_), channel_id=1, source_target_pairs={{0,8},{8,16},{16,24},{24,0},{1,9},{9,17},{17,25},{25,1},{2,10},{10... | collective-permute-start | bytes 786440 | tf_op jit(solution)/shard_map/ppermute | solution.py:43
  123.3 13.4 %collective-permute-start.12 = (bf16[256,512]{1,0:T(8,128)(2,1)S(1)}, bf16[256,512]{1,0:T(8,128)(2,1)S(1)}, u32[]{:S(2)}, u32[]{:S(2)}) collective-permute-start(bf16[256,512]{1,0:T(8,128)(2,1)S(1)} %collective-permute-done.10.refs_1_), channel_id=1, source_target_pairs={{0,8},{8,16},{16,24},{24,0},{1,9},{9,17},{17,25},{25,1},{2,10},{10... | collective-permute-start | bytes 786440 | tf_op jit(solution)/shard_map/ppermute | solution.py:43
  128.8 8.0 %collective-permute-start.15 = (bf16[256,512]{1,0:T(8,128)(2,1)S(1)}, bf16[256,512]{1,0:T(8,128)(2,1)S(1)}, u32[]{:S(2)}, u32[]{:S(2)}) collective-permute-start(bf16[256,512]{1,0:T(8,128)(2,1)S(1)} %collective-permute-done.14.refs_6_), channel_id=1, source_target_pairs={{0,24},{8,0},{16,8},{24,16},{1,25},{9,1},{17,9},{25,17},{2,26},{10... | collective-permute-start | bytes 786440 | tf_op jit(solution)/shard_map/ppermute | solution.py:43
  133.4 6.7 %collective-permute-start.26 = (bf16[4,512,128]{2,1,0:T(8,128)(2,1)S(1)}, bf16[4,512,128]{2,1,0:T(8,128)(2,1)S(1)}, u32[]{:S(2)}, u32[]{:S(2)}) collective-permute-start(bf16[4,512,128]{2,1,0:T(8,128)(2,1)S(1)} %get-tuple-element.72), channel_id=1, source_target_pairs={{0,1},{1,0},{2,3},{3,2},{4,5},{5,4},{6,7},{7,6},{8,9},{9,8},{10,11... | collective-permute-start | bytes 1572872 | tf_op jit(solution)/shard_map/ppermute | solution.py:43
  140.0 4.6 %collective-permute-start.22 = (bf16[4,512,128]{2,1,0:T(8,128)(2,1)S(1)}, bf16[4,512,128]{2,1,0:T(8,128)(2,1)S(1)}, u32[]{:S(2)}, u32[]{:S(2)}) collective-permute-start(bf16[4,512,128]{2,1,0:T(8,128)(2,1)S(1)} %get-tuple-element.66), channel_id=1, source_target_pairs={{0,1},{1,0},{2,3},{3,2},{4,5},{5,4},{6,7},{7,6},{8,9},{9,8},{10,11... | collective-permute-start | bytes 1572872 | tf_op jit(solution)/shard_map/ppermute | solution.py:43
  140.2 6.6 %collective-permute-start.27 = (bf16[512,128]{1,0:T(8,128)(2,1)S(1)}, bf16[512,128]{1,0:T(8,128)(2,1)S(1)}, u32[]{:S(2)}, u32[]{:S(2)}) collective-permute-start(bf16[512,128]{1,0:T(8,128)(2,1)S(1)} %get-tuple-element.74), channel_id=1, source_target_pairs={{0,2},{2,4},{4,6},{6,0},{1,3},{3,5},{5,7},{7,1},{8,10},{10,12},{12... | collective-permute-start | bytes 393224 | tf_op jit(solution)/shard_map/ppermute | solution.py:43
  141.8 7.0 %collective-permute-start.28 = (bf16[512,128]{1,0:T(8,128)(2,1)S(1)}, bf16[512,128]{1,0:T(8,128)(2,1)S(1)}, u32[]{:S(2)}, u32[]{:S(2)}) collective-permute-start(bf16[512,128]{1,0:T(8,128)(2,1)S(1)} %get-tuple-element.75), channel_id=1, source_target_pairs={{0,6},{2,0},{4,2},{6,4},{1,7},{3,1},{5,3},{7,5},{8,14},{10,8},{12,... | collective-permute-start | bytes 393224 | tf_op jit(solution)/shard_map/ppermute | solution.py:43
  142.3 9.5 %collective-permute-start.29 = (bf16[512,128]{1,0:T(8,128)(2,1)S(1)}, bf16[512,128]{1,0:T(8,128)(2,1)S(1)}, u32[]{:S(2)}, u32[]{:S(2)}) collective-permute-start(bf16[512,128]{1,0:T(8,128)(2,1)S(1)} %get-tuple-element.76), channel_id=1, source_target_pairs={{0,4},{2,6},{4,0},{6,2},{1,5},{3,7},{5,1},{7,3},{8,12},{10,14},{12... | collective-permute-start | bytes 393224 | tf_op jit(solution)/shard_map/ppermute | solution.py:43
  144.7 8.4 %collective-permute-start.23 = (bf16[512,128]{1,0:T(8,128)(2,1)S(1)}, bf16[512,128]{1,0:T(8,128)(2,1)S(1)}, u32[]{:S(2)}, u32[]{:S(2)}) collective-permute-start(bf16[512,128]{1,0:T(8,128)(2,1)S(1)} %get-tuple-element.68), channel_id=1, source_target_pairs={{0,2},{2,4},{4,6},{6,0},{1,3},{3,5},{5,7},{7,1},{8,10},{10,12},{12... | collective-permute-start | bytes 393224 | tf_op jit(solution)/shard_map/ppermute | solution.py:43
  145.6 7.7 %collective-permute-start.24 = (bf16[512,128]{1,0:T(8,128)(2,1)S(1)}, bf16[512,128]{1,0:T(8,128)(2,1)S(1)}, u32[]{:S(2)}, u32[]{:S(2)}) collective-permute-start(bf16[512,128]{1,0:T(8,128)(2,1)S(1)} %get-tuple-element.69), channel_id=1, source_target_pairs={{0,6},{2,0},{4,2},{6,4},{1,7},{3,1},{5,3},{7,5},{8,14},{10,8},{12,... | collective-permute-start | bytes 393224 | tf_op jit(solution)/shard_map/ppermute | solution.py:43
  146.8 9.8 %collective-permute-start.25 = (bf16[512,128]{1,0:T(8,128)(2,1)S(1)}, bf16[512,128]{1,0:T(8,128)(2,1)S(1)}, u32[]{:S(2)}, u32[]{:S(2)}) collective-permute-start(bf16[512,128]{1,0:T(8,128)(2,1)S(1)} %get-tuple-element.70), channel_id=1, source_target_pairs={{0,4},{2,6},{4,0},{6,2},{1,5},{3,7},{5,1},{7,3},{8,12},{10,14},{12... | collective-permute-start | bytes 393224 | tf_op jit(solution)/shard_map/ppermute | solution.py:43
  156.8 5.6 %collective-permute-start.30 = (bf16[256,128]{1,0:T(8,128)(2,1)S(1)}, bf16[256,128]{1,0:T(8,128)(2,1)S(1)}, u32[]{:S(2)}, u32[]{:S(2)}) collective-permute-start(bf16[256,128]{1,0:T(8,128)(2,1)S(1)} %get-tuple-element.78), channel_id=1, source_target_pairs={{0,8},{8,16},{16,24},{24,0},{1,9},{9,17},{17,25},{25,1},{2,10},{10... | collective-permute-start | bytes 196616 | tf_op jit(solution)/shard_map/ppermute | solution.py:43
  156.9 5.5 %collective-permute-start.31 = (bf16[256,128]{1,0:T(8,128)(2,1)S(1)}, bf16[256,128]{1,0:T(8,128)(2,1)S(1)}, u32[]{:S(2)}, u32[]{:S(2)}) collective-permute-start(bf16[256,128]{1,0:T(8,128)(2,1)S(1)} %get-tuple-element.79), channel_id=1, source_target_pairs={{0,24},{8,0},{16,8},{24,16},{1,25},{9,1},{17,9},{25,17},{2,26},{10... | collective-permute-start | bytes 196616 | tf_op jit(solution)/shard_map/ppermute | solution.py:43
  160.1 5.8 %collective-permute-start.32 = (bf16[256,128]{1,0:T(8,128)(2,1)S(1)}, bf16[256,128]{1,0:T(8,128)(2,1)S(1)}, u32[]{:S(2)}, u32[]{:S(2)}) collective-permute-start(bf16[256,128]{1,0:T(8,128)(2,1)S(1)} %get-tuple-element.80), channel_id=1, source_target_pairs={{0,16},{8,24},{16,0},{24,8},{1,17},{9,25},{17,1},{25,9},{2,18},{10... | collective-permute-start | bytes 196616 | tf_op jit(solution)/shard_map/ppermute | solution.py:43
  (8 other events, 5.8 us)
Sparse Core Ops, SparseCore 0:
  9.1 57.6 all-gather.2

commit v3 on v2

--- a/solution.py
+++ b/solution.py
@@ -16,7 +16,7 @@
 WIDE = WIDTH + BC
 F32 = jnp.float32
 BF16 = jnp.bfloat16
-LARGE = 48 * 1024 * 1024
+LARGE = 60 * 1024 * 1024
 SMALL = 20 * 1024 * 1024
 SPECS = {
     "v": pl.BlockSpec(memory_space=pltpu.VMEM),
@@ -68,7 +68,9 @@
     return lambda t: jnp.where(t >= s3, s3, jnp.where(t >= s2, s2, jnp.where(t >= s1, s1, 0)))
 
 
-def pack_kernel(x_any, bc_any, dt_any, own, to_next, to_prev, to_far, h0, h1, h2, h3, turned, sems):
+def pack_kernel(x_any, bc_any, dt_any, *refs):
+    bcs, xs, edges = refs[0:4], refs[4:8], refs[8:12]
+    turned, sems = refs[12:]
     x = lax.axis_index("x")
     get_dt = pltpu.make_async_copy(dt_any, turned, sems.at[0])
     get_dt.start()
@@ -79,21 +81,21 @@
         copy.start()
         copies.append(copy)
 
-    outs = ((1, to_next), (3, to_prev), (2, to_far), (0, own))
-    for by, out in outs:
-        q = around(x, by)
-        start(x_any.at[:, lanes(q, WIDTH)], out.at[:SPAN, :WIDTH])
-        start(bc_any, out.at[:SPAN, WIDTH:])
-    for q, out in enumerate((h0, h1, h2, h3)):
+    order = (1, 3, 2, 0)
+    for out in bcs:
+        start(bc_any, out.at[:SPAN, :])
+    for by, out in zip(order, xs):
+        start(x_any.at[:, lanes(around(x, by), WIDTH)], out)
+    for q, out in enumerate(edges):
         start(x_any.at[SPAN - 16 :, q * WIDTH : (q + 1) * WIDTH], out.at[:, :WIDTH])
         start(bc_any.at[SPAN - 16 :, :], out.at[:, WIDTH:])
     get_dt.wait()
-    for by, out in outs:
-        q = around(x, by)
-        rows = turned[pl.ds(pl.multiple_of(q * HEADS, HEADS), HEADS), :]
+    for by, out in zip(order, bcs):
+        rows = turned[pl.ds(pl.multiple_of(around(x, by) * HEADS, HEADS), HEADS), :]
         hi, mid, low = three_parts(rows)
-        line = jnp.concatenate([hi, mid, low, jnp.zeros_like(low)], axis=1)
-        out[SPAN:, :] = jnp.concatenate([line, jnp.zeros_like(line)], axis=0).astype(BF16)
+        upper = jnp.concatenate([hi, mid], axis=1)
+        lower = jnp.concatenate([low, jnp.zeros_like(low)], axis=1)
+        out[SPAN:, :] = jnp.concatenate([upper, lower], axis=0).astype(BF16)
     for copy in copies:
         copy.wait()
 
@@ -108,19 +110,22 @@
         copy.wait()
 
 
-def state_kernel(
-    lengths, decay, own, prev, nxt, far, h0, h1, h2, h3, cw_ref, cb_ref,
-    conv_hbm, cols_hbm, rows_hbm, carry_hbm, re_hbm, t_out,
-    pay, ext, carry, weighted, conv_out, cols_out, rows_out, carry_out, re_out, sems,
+def convolve(ext, tap, pos, at):
+    cols = slice(at, at + 128)
+    acc = tap(3, at) * ext[8 : 8 + SPAN, cols]
+    for back in (1, 2, 3):
+        term = tap(3 - back, at) * ext[8 - back : 8 - back + SPAN, cols]
+        acc = acc + jnp.where(pos >= back, term, 0.0)
+    return (acc * sigmoid(acc)).astype(BF16)
+
+
+def step_kernel(
+    lengths, decay, h0, h1, h2, h3, own, prev, nxt, far, cb_ref,
+    bc_hbm, cols_hbm, rows_hbm, re_hbm, total_out,
+    pay, ext, bc_out, cols_out, rows_out, re_out, sems,
 ):
     def outgoing(j):
-        pairs = (
-            (conv_out, conv_hbm),
-            (cols_out, cols_hbm),
-            (rows_out, rows_hbm),
-            (carry_out, carry_hbm),
-            (re_out, re_hbm),
-        )
+        pairs = ((bc_out, bc_hbm), (cols_out, cols_hbm), (rows_out, rows_hbm), (re_out, re_hbm))
         return [
             pltpu.make_async_copy(src.at[j], dst.at[j], sems.at[k, j])
             for k, (src, dst) in enumerate(pairs)
@@ -129,101 +134,149 @@
     x = lax.axis_index("x")
     base = lax.axis_index("z") * (NX * SPAN)
     first_of = first_finder(lengths)
-    pay[x] = own[...]
-    pay[around(x, 3)] = prev[...]
-    pay[around(x, 1)] = nxt[...]
-    pay[around(x, 2)] = far[...]
+    for by, src in ((0, own), (3, prev), (1, nxt), (2, far)):
+        pay[around(x, by)] = src[...]
+    cut = slice(WIDTH, WIDTH + BC)
     ext[0:8] = (
-        h0[8:16].astype(F32) + h1[8:16].astype(F32) + h2[8:16].astype(F32) + h3[8:16].astype(F32)
-    )
-    carry[...] = jnp.zeros_like(carry)
-    taps_x = cw_ref[:, lanes(x, WIDTH)]
+        h0[8:16, cut].astype(F32)
+        + h1[8:16, cut].astype(F32)
+        + h2[8:16, cut].astype(F32)
+        + h3[8:16, cut].astype(F32)
+    )
     head = lax.broadcasted_iota(jnp.int32, (HEADS, SPAN), 0)
     rates = jnp.zeros((HEADS, SPAN), F32)
     for h in range(HEADS):
         rates = jnp.where(head == h, decay[x * HEADS + h], rates)
-
-    def turn(j, before):
-        start = base + j * SPAN
-
-        @pl.when(j > 0)
-        def _():
-            ext[0:8] = ext[SPAN : SPAN + 8]
-
-        ext[8:] = pay[j, :SPAN, :].astype(F32)
-        row = lax.broadcasted_iota(jnp.int32, (SPAN, 128), 0)
-        lane = lax.broadcasted_iota(jnp.int32, (SPAN, 128), 1)
-        lane1 = lax.broadcasted_iota(jnp.int32, (1, 128), 1)
-        place = start + row
-        first = first_of(place)
-        pos = place - first
-        for part in range(WIDE // 128):
-            at = part * 128
-            cols = slice(at, at + 128)
-
-            def tap(k):
-                if at < WIDTH:
-                    return taps_x[k : k + 1, cols]
-                return cb_ref[k][:, at - WIDTH : at - WIDTH + 128]
-
-            acc = tap(3) * ext[8 : 8 + SPAN, cols]
-            for back in (1, 2, 3):
-                term = tap(3 - back) * ext[8 - back : 8 - back + SPAN, cols]
-                acc = acc + jnp.where(pos >= back, term, 0.0)
-            conv_out[j, :, cols] = (acc * sigmoid(acc)).astype(BF16)
-        packed = pay[j, SPAN:, :][:HEADS].astype(F32)
-        raw = packed[:, :SPAN] + packed[:, SPAN : 2 * SPAN] + packed[:, 2 * SPAN : 3 * SPAN]
-        step = jnp.maximum(raw, 0.0) + jnp.log1p(jnp.exp(-jnp.abs(raw)))
-        parts = jnp.concatenate(
-            [*three_parts(-rates * step), jnp.zeros((HEADS, SPAN), F32)], axis=0
-        ).astype(BF16)
-        wide_s = lax.broadcasted_iota(jnp.int32, (SPAN, SPAN), 0)
-        wide_t = lax.broadcasted_iota(jnp.int32, (SPAN, SPAN), 1)
-        upper = jnp.where(wide_s <= wide_t, 1.0, 0.0).astype(BF16)
-        sums = jnp.dot(parts, upper, preferred_element_type=F32)
-        logd = sums[:HEADS] + sums[HEADS : 2 * HEADS] + sums[2 * HEADS : 3 * HEADS]
-        both = jnp.concatenate([logd, step], axis=0)
+    raw = []
+    for j in range(NX):
+        packed = pay[j, SPAN:, :].astype(F32)
+        raw.append(packed[:HEADS, :SPAN] + packed[:HEADS, SPAN:] + packed[HEADS:, :SPAN])
+    raw = jnp.concatenate(raw, axis=0)
+    step = jnp.maximum(raw, 0.0) + jnp.log1p(jnp.exp(-jnp.abs(raw)))
+    rate = -jnp.concatenate([rates] * NX, axis=0) * step
+    parts = jnp.concatenate([*three_parts(rate), jnp.zeros_like(rate)], axis=0).astype(BF16)
+    wide_s = lax.broadcasted_iota(jnp.int32, (SPAN, SPAN), 0)
+    wide_t = lax.broadcasted_iota(jnp.int32, (SPAN, SPAN), 1)
+    upper = jnp.where(wide_s <= wide_t, 1.0, 0.0).astype(BF16)
+    sums = jnp.dot(parts, upper, preferred_element_type=F32)
+    n = NX * HEADS
+    logd = sums[:n] + sums[n : 2 * n] + sums[2 * n : 3 * n]
+    row = lax.broadcasted_iota(jnp.int32, (SPAN, 128), 0)
+    lane1 = lax.broadcasted_iota(jnp.int32, (1, 128), 1)
+    before = jnp.zeros((1, 128), F32)
+    for j in range(NX):
+        at = slice(j * HEADS, (j + 1) * HEADS)
+        both = jnp.concatenate([logd[at], step[at]], axis=0)
         rows_out[j] = both
         cols = jnp.transpose(
             jnp.concatenate([both, jnp.zeros((128 - 2 * HEADS, SPAN), F32)], axis=0)
         )
         cols_out[j] = cols
+        first = first_of(base + j * SPAN + row)
+        re_out[j] = jnp.where(first < base, jnp.exp(jnp.minimum(cols + before, 0.0)), 0.0)
+        before = before + jnp.where(lane1 < HEADS, cols[SPAN - 1 : SPAN, :], 0.0)
+    total_out[...] = jnp.broadcast_to(before, total_out.shape)
+
+    def turn(j, token):
+        @pl.when(j > 0)
+        def _():
+            ext[0:8] = ext[SPAN : SPAN + 8]
+
+        ext[8:] = pay[j, :SPAN, :].astype(F32)
+        place = base + j * SPAN + row
+        pos = place - first_of(place)
+        for part in range(BC // 128):
+            at = part * 128
+            bc_out[j, :, at : at + 128] = convolve(
+                ext, lambda k, at: cb_ref[k][:, at : at + 128], pos, at
+            )
+        for copy in outgoing(j):
+            copy.start()
+        return token
+
+    lax.fori_loop(0, NX, turn, 0)
+
+    def finish(j, token):
+        for copy in outgoing(j):
+            copy.wait()
+        return token
+
+    lax.fori_loop(0, NX, finish, 0)
+
+
+def state_kernel(
+    lengths, own, prev, nxt, far, h0, h1, h2, h3, cw_ref, bc_ref, cols_ref, total_ref,
+    xs_hbm, carry_hbm, t_out,
+    pay, ext, carry, weighted, xs_out, carry_out, sems,
+):
+    def outgoing(j):
+        pairs = ((xs_out, xs_hbm), (carry_out, carry_hbm))
+        return [
+            pltpu.make_async_copy(src.at[j], dst.at[j], sems.at[k, j])
+            for k, (src, dst) in enumerate(pairs)
+        ]
+
+    x = lax.axis_index("x")
+    base = lax.axis_index("z") * (NX * SPAN)
+    first_of = first_finder(lengths)
+    for by, src in ((0, own), (3, prev), (1, nxt), (2, far)):
+        pay[around(x, by)] = src[...]
+    ext[0:8] = (
+        h0[8:16, :WIDTH].astype(F32)
+        + h1[8:16, :WIDTH].astype(F32)
+        + h2[8:16, :WIDTH].astype(F32)
+        + h3[8:16, :WIDTH].astype(F32)
+    )
+    carry[...] = jnp.zeros_like(carry)
+    taps = cw_ref[:, lanes(x, WIDTH)]
+    row = lax.broadcasted_iota(jnp.int32, (SPAN, 128), 0)
+    left = lax.broadcasted_iota(jnp.int32, (SPAN, 128), 1) < HEAD_DIM
+    left1 = lax.broadcasted_iota(jnp.int32, (1, 128), 1) < HEAD_DIM
+
+    def turn(j, token):
+        start = base + j * SPAN
+
+        @pl.when(j > 0)
+        def _():
+            ext[0:8] = ext[SPAN : SPAN + 8]
+
+        ext[8:] = pay[j].astype(F32)
+        place = start + row
+        pos = place - first_of(place)
         first_end = first_of(start + SPAN - 1)
         keep = place >= first_end
         carried = jnp.where(first_end < start, 1.0, 0.0)
+        cols = cols_ref[j]
         end = cols[SPAN - 1 : SPAN, :]
-        re_out[j] = jnp.where(first < base, jnp.exp(jnp.minimum(cols + before, 0.0)), 0.0)
-        left = lane < HEAD_DIM
-        left1 = lane1 < HEAD_DIM
         decays = []
         for pair in range(HEADS // 2):
             at = slice(pair * 128, pair * 128 + 128)
             h = 2 * pair
+            xs = convolve(ext, lambda k, at: taps[k : k + 1, at : at + 128], pos, pair * 128)
+            xs_out[j, :, at] = xs
             log2 = jnp.where(left, cols[:, h : h + 1], cols[:, h + 1 : h + 2])
             s = HEADS + h
             step2 = jnp.where(left, cols[:, s : s + 1], cols[:, s + 1 : s + 2])
             end2 = jnp.where(left1, end[:, h : h + 1], end[:, h + 1 : h + 2])
-            inputs = jnp.where(keep, jnp.exp(end2 - log2) * step2, 0.0) * conv_out[j, :, at].astype(F32)
+            inputs = jnp.where(keep, jnp.exp(end2 - log2) * step2, 0.0) * xs.astype(F32)
             weighted[:, at] = inputs.astype(BF16)
             decays.append(jnp.exp(end2) * carried)
-        keys = conv_out[j, :, WIDTH : WIDTH + STATE]
         states = lax.dot_general(
-            keys, weighted[...], (((0,), (0,)), ((), ())), preferred_element_type=F32
+            bc_ref[j, :, :STATE], weighted[...], (((0,), (0,)), ((), ())), preferred_element_type=F32
         )
         state = carry[...]
         carry_out[j] = state.astype(BF16)
         carry[...] = jnp.concatenate(decays, axis=1) * state + states
         for copy in outgoing(j):
             copy.start()
-        return before + jnp.where(lane1 < HEADS, end, 0.0)
-
-    total = lax.fori_loop(0, NX, turn, jnp.zeros((1, 128), F32))
+        return token
+
+    lax.fori_loop(0, NX, turn, 0)
     last = first_of(base + NX * SPAN - 1)
-    lane1 = lax.broadcasted_iota(jnp.int32, (1, 128), 1)
-    whole = jnp.where(last < base, jnp.exp(total), 0.0)
+    whole = jnp.where(last < base, jnp.exp(total_ref[0:1, :]), 0.0)
     spread = jnp.concatenate(
         [
-            jnp.where(lane1 < HEAD_DIM, whole[:, h : h + 1], whole[:, h + 1 : h + 2])
+            jnp.where(left1, whole[:, h : h + 1], whole[:, h + 1 : h + 2])
             for h in range(0, HEADS, 2)
         ],
         axis=1,
@@ -246,12 +299,14 @@
 
 
 def within_kernel(
-    lengths, skip, conv_hbm, cols_hbm, rows_hbm, carry_hbm, after, y_hbm,
-    gram, conv_ref, cols_ref, rows_ref, carry_ref, y_out, sems,
+    lengths, skip, xs_hbm, bc_hbm, cols_hbm, rows_hbm, carry_hbm, *refs
 ):
+    y_hbm, gram, xs_ref, bc_ref, cols_ref, rows_ref, carry_ref, y_out, sems = refs[-9:]
+
     def incoming(j):
         pairs = (
-            (conv_hbm, conv_ref),
+            (xs_hbm, xs_ref),
+            (bc_hbm, bc_ref),
             (cols_hbm, cols_ref),
             (rows_hbm, rows_ref),
             (carry_hbm, carry_ref),
@@ -262,7 +317,7 @@
         ]
 
     def result(j):
-        return pltpu.make_async_copy(y_out.at[j], y_hbm.at[j], sems.at[4, j])
+        return pltpu.make_async_copy(y_out.at[j], y_hbm.at[j], sems.at[5, j])
 
     def begin(j, token):
         for copy in incoming(j):
@@ -284,8 +339,8 @@
         left = lane < HEAD_DIM
         left1 = lax.broadcasted_iota(jnp.int32, (1, 128), 1) < HEAD_DIM
         entered = first_of(start + row) < start
-        keys = conv_ref[j, :, WIDTH : WIDTH + STATE]
-        query = conv_ref[j, :, WIDTH + STATE :]
+        keys = bc_ref[j, :, :STATE]
+        query = bc_ref[j, :, STATE:]
         dots = lax.dot_general(query, keys, (((1,), (1,)), ((), ())), preferred_element_type=F32)
         wide_t = lax.broadcasted_iota(jnp.int32, (SPAN, SPAN), 0)
         wide_s = lax.broadcasted_iota(jnp.int32, (SPAN, SPAN), 1)
@@ -296,7 +351,7 @@
         rows = rows_ref[j]
         for pair in range(HEADS // 2):
             at = slice(pair * 128, pair * 128 + 128)
-            xs = conv_ref[j, :, at]
+            xs = xs_ref[j, :, at]
             tops, bottoms = [], []
             for h in (2 * pair, 2 * pair + 1):
                 column = cols[:, h : h + 1]
@@ -345,7 +400,7 @@
             state = (marks[0:1] + marks[1:2]) * state + t_ref[k, :rows].astype(F32)
 
 
-def gate_kernel(own, prev, nxt, far, y_hbm, conv_hbm, re_hbm, e_ref, gain_ref, *refs):
+def gate_kernel(own, prev, nxt, far, y_hbm, bc_hbm, re_hbm, e_ref, gain_ref, *refs):
     *outs, gate, y_ref, query, re_ref, sems = refs[1:]
     x = lax.axis_index("x")
     copies = []
@@ -353,7 +408,7 @@
         b = j
         for src, dst in (
             (y_hbm.at[j], y_ref.at[b]),
-            (conv_hbm.at[j, :, WIDTH + STATE :], query.at[b]),
+            (bc_hbm.at[j, :, STATE:], query.at[b]),
             (re_hbm.at[j], re_ref.at[b]),
         ):
             copies.append(pltpu.make_async_copy(src, dst, sems.at[len(copies)]))
@@ -439,23 +494,25 @@
     bc = bc_in.reshape(SPAN, BC)
     w_all = lax.all_gather(out_weight, "z", axis=0)
 
-    piece = ((SPAN + 16, WIDE), BF16)
+    piece = ((SPAN + 16, BC), BF16)
+    quarter = ((SPAN, WIDTH), BF16)
     edge = ((16, WIDE), BF16)
-    own, to_next, to_prev, to_far, *edges = call(
-        pack_kernel, "hhh", (x_in, bc, dt_raw.T), [piece] * 4 + [edge] * 4,
-        [
-            pltpu.VMEM((4 * HEADS, SPAN), F32),
-            pltpu.SemaphoreType.DMA((17,)),
-        ],
+    packed = call(
+        pack_kernel, "hhh", (x_in, bc, dt_raw.T), [piece] * 4 + [quarter] * 4 + [edge] * 4,
+        [pltpu.VMEM((4 * HEADS, SPAN), F32), pltpu.SemaphoreType.DMA((17,))],
         nbytes=6 << 20,
     )
-    far = shift(to_far, "x", 2)
-    prev, nxt = shift(to_next, "x", 1), shift(to_prev, "x", -1)
-    halo = [
-        lax.ppermute(e, ("z", "x"), [((z - 1) * NX + NX - 1, z * NX + k) for z in range(1, nz)])
-        for k, e in enumerate(edges)
-    ]
-    quarter = ((SPAN, WIDTH), BF16)
+
+    def spread_out(to_next, to_prev, to_far, own):
+        return own, shift(to_next, "x", 1), shift(to_prev, "x", -1), shift(to_far, "x", 2)
+
+    def behind(v, k):
+        return lax.ppermute(v, ("z", "x"), [((z - 1) * NX + NX - 1, z * NX + k) for z in range(1, nz)])
+
+    bcs = spread_out(*packed[0:4])
+    xs_in = spread_out(*packed[4:8])
+    halo = [behind(e, k) for k, e in enumerate(packed[8:12])]
+    far = xs_in[3]
     g_own, g_next, g_prev, g_far = call(
         split_kernel, "ha", (gate_in, far), [quarter] * 4, [pltpu.SemaphoreType.DMA((4,))],
         nbytes=2 << 20,
@@ -464,54 +521,64 @@
 
     gain = norm_gain[None, :]
     rows = STATE // nz
-    kept_specs = [
-        pltpu.VMEM((NX, SPAN, WIDE), BF16),
-        pltpu.VMEM((NX, SPAN, 128), F32),
-        pltpu.VMEM((NX, 2 * HEADS, SPAN), F32),
-        pltpu.VMEM((NX, STATE, WIDTH), BF16),
-        pltpu.VMEM((NX, SPAN, 128), F32),
-    ]
-    conv, cols, lines, carry, reach, sums = call(
-        state_kernel, "ss" + "v" * 10,
-        (lengths, decay_rate, own, prev, nxt, far, *halo, conv_x, conv_bc),
+    blocks_bc = pltpu.VMEM((NX, SPAN, BC), BF16)
+    blocks_cols = pltpu.VMEM((NX, SPAN, 128), F32)
+    blocks_rows = pltpu.VMEM((NX, 2 * HEADS, SPAN), F32)
+    bcv, cols, lines, reach, total = call(
+        step_kernel, "ss" + "v" * 9,
+        (lengths, decay_rate, *halo, *bcs, conv_bc),
         [
-            ((NX, SPAN, WIDE), BF16),
+            ((NX, SPAN, BC), BF16),
             ((NX, SPAN, 128), F32),
             ((NX, 2 * HEADS, SPAN), F32),
+            ((NX, SPAN, 128), F32),
+            ((8, 128), F32),
+        ],
+        [
+            pltpu.VMEM((NX, SPAN + 16, BC), BF16),
+            pltpu.VMEM((SPAN + 8, BC), F32),
+            blocks_bc, blocks_cols, blocks_rows, blocks_cols,
+            pltpu.SemaphoreType.DMA((4, NX)),
+        ],
+        flops=2 << 30, nbytes=8 << 20, places="hhhhv",
+    )
+    xs, carry, sums = call(
+        state_kernel, "s" + "v" * 12,
+        (lengths, *xs_in, *halo, conv_x, bcv, cols, total),
+        [
+            ((NX, SPAN, WIDTH), BF16),
             ((NX, STATE, WIDTH), BF16),
-            ((NX, SPAN, 128), F32),
             ((nz, rows + 16, WIDTH), BF16),
         ],
         [
-            pltpu.VMEM((NX, SPAN + 16, WIDE), BF16),
-            pltpu.VMEM((SPAN + 8, WIDE), F32),
+            pltpu.VMEM((NX, SPAN, WIDTH), BF16),
+            pltpu.VMEM((SPAN + 8, WIDTH), F32),
             pltpu.VMEM((STATE, WIDTH), F32),
             pltpu.VMEM((SPAN, WIDTH), BF16),
-            *kept_specs,
-            pltpu.SemaphoreType.DMA((5, NX)),
+            blocks_bc,
+            blocks_bc,
+            pltpu.SemaphoreType.DMA((2, NX)),
         ],
-        flops=4 << 30, nbytes=16 << 20, places="hhhhhv",
+        flops=3 << 30, nbytes=10 << 20, places="hhv",
     )
     spread = lax.all_to_all(sums, "z", 0, 0, tiled=True)
+    (mine,) = call(scan_kernel, "v", (spread,), [((nz, rows, WIDTH), BF16)], nbytes=1 << 20)
     (y_loc,) = call(
-        within_kernel, "sshhhha", (lengths, skip_gain, conv, cols, lines, carry, g_own),
+        within_kernel, "sshhhhhaaaa", (lengths, skip_gain, xs, bcv, cols, lines, carry, mine, *gates[1:]),
         [((NX, SPAN, WIDTH), F32)],
         [
             pltpu.VMEM((SPAN, SPAN), F32),
-            *kept_specs[:4],
+            blocks_bc, blocks_bc, blocks_cols, blocks_rows, blocks_bc,
             pltpu.VMEM((NX, SPAN, WIDTH), F32),
-            pltpu.SemaphoreType.DMA((5, NX)),
+            pltpu.SemaphoreType.DMA((6, NX)),
         ],
         flops=6 << 30, nbytes=16 << 20, places="h",
     )
-    (enter,) = call(
-        scan_kernel, "vhaaa", (spread, y_loc, *gates[1:]), [((nz, rows, WIDTH), BF16)], nbytes=1 << 20
-    )
-    enter = lax.all_to_all(enter, "z", 0, 0, tiled=True).reshape(STATE, WIDTH)
+    enter = lax.all_to_all(mine, "z", 0, 0, tiled=True).reshape(STATE, WIDTH)
 
     halves = []
     v = call(
-        gate_kernel, "aaaahhhvva", (*gates, y_loc, conv, reach, enter, gain, w_all),
+        gate_kernel, "aaaahhhvva", (*gates, y_loc, bcv, reach, enter, gain, w_all),
         [quarter] * NX,
         [
             pltpu.VMEM((NX, SPAN, WIDTH), BF16),

time: 174 us -> 171 us (0.983)
  blocking collectives: 17.4 us -> 0 us
  starting transfers between devices: 49 us -> 63.3 us
  Pallas kernels: 27.5 us -> 40.2 us
  local copies, waits for them, and re-layouts: 14.7 us -> 7.68 us
  waiting for transfers between devices: 51.2 us -> 45 us
    ppermute x29 -> x32, waiting for transfers between devices: 50.5 us -> 29 us  [shift(): return lax.ppermute(v, axis, [(i, (i + by) % n) for i in range(n)])]
    all_to_all x1 -> x0, blocking collectives: 17.4 us -> none  [on_device(): enter = lax.all_to_all(enter, 'z', 0, 0, tiled=True).reshape(STATE, WIDTH)]
    pallas_call x13 -> x14, Pallas kernels: 27.5 us -> 40.2 us  [call(): pl.pallas_call(kernel, in_specs=[SPECS[s] for s in spaces], out_specs=tup...]
    all_to_all x1, waiting for transfers between devices: 0.01 us -> 12 us  [on_device(): spread = lax.all_to_all(sums, 'z', 0, 0, tiled=True)]
    ppermute x29 -> x32, starting transfers between devices: 37.3 us -> 47.7 us  [shift(): return lax.ppermute(v, axis, [(i, (i + by) % n) for i in range(n)])]
    unnamed x42, local copies, waits for them, and re-layouts: 14.7 us -> 7.68 us
    all_to_all x0 -> x1, starting transfers between devices: none -> 3.59 us  [on_device(): enter = lax.all_to_all(mine, 'z', 0, 0, tiled=True).reshape(STATE, WIDTH)]
    all_to_all x0 -> x1, waiting for transfers between devices: none -> 3.27 us  [on_device(): enter = lax.all_to_all(mine, 'z', 0, 0, tiled=True).reshape(STATE, WIDTH)]
  transfers between devices with their start and end apart: 35 -> 39, of which waited for: 16 -> 16; matrix products, arithmetic and copies ran while one was open for 0% -> 0% of each run, Pallas kernels for 14% -> 20%
where the time goes in v3:
time: 171 us; the launch traced here: 170 us
  starting transfers between devices  63.3 us (37%)
  waiting for transfers between devices  45 us (26%)
  Pallas kernels  40.2 us (24%)
  between operations  13.8 us (8%)
  local copies, waits for them, and re-layouts  7.68 us (4%)
    ppermute x32, starting transfers between devices, shift(): return lax.ppermute(v, axis, [(i, (i + by) % n) for i in range(n)])  47.7 us
    pallas_call x14, Pallas kernels, call(): pl.pallas_call(kernel, in_specs=[SPECS[s] for s in spaces], out_specs=tup...  40.2 us
    ppermute x32, waiting for transfers between devices, shift(): return lax.ppermute(v, axis, [(i, (i + by) % n) for i in range(n)])  29 us
    all_to_all x1, waiting for transfers between devices, on_device(): spread = lax.all_to_all(sums, 'z', 0, 0, tiled=True)  12 us
    all_to_all x1, starting transfers between devices, on_device(): spread = lax.all_to_all(sums, 'z', 0, 0, tiled=True)  9.31 us
    unnamed x42, local copies, waits for them, and re-layouts  7.68 us
    all_to_all x1, starting transfers between devices, on_device(): enter = lax.all_to_all(mine, 'z', 0, 0, tiled=True).reshape(STATE, WIDTH)  3.59 us
  transfers between devices with their start and end apart: 39, of which 16 were waited for; matrix products, arithmetic and copies ran while one was open for 0% of the time, Pallas kernels for 20%

profile of v3, /device:TPU:8, one launch (start us, length us, event | category | flops | bytes accessed | tf_op | source)
XLA Modules:
  0.0 169.9 jit_solution(14159845278430232875)
XLA Ops:
  7.3 3.2 %shard_map.109 = (bf16[272,512]{1,0:T(8,128)(2,1)}, bf16[272,512]{1,0:T(8,128)(2,1)}, bf16[272,512]{1,0:T(8,128)(2,1)}, bf16[272,512]{1,0:T(8,128)(2,1)}, bf16[2...) custom-call(bf16[256,2048]{1,0:T(8,128)(2,1)} %x_any.1, ...), custom_call_target="tpu_custom_call" | custom-call | bytes 6291456 | tf_op jit(solution)/shard_map/pallas_call | solution.py:30
  10.5 1.6 collective-permute-start.10
  12.1 1.7 %collective-permute-start.11 = (bf16[272,512]{1,0:T(8,128)(2,1)}, bf16[272,512]{1,0:T(8,128)(2,1)S(1)}, u32[]{:S(2)}, u32[]{:S(2)}) collective-permute-start(bf16[272,512]{1,0:T(8,128)(2,1)} %get-tuple-element.63), channel_id=1, source_target_pairs={{0,24},{8,0},{16,8},{24,16},{1,25},{9,1},{17,9},{25,17},{2,26},{10... | collective-permute-start | bytes 835592 | tf_op jit(solution)/shard_map/ppermute | solution.py:43
  13.8 1.8 %collective-permute-start.12 = (bf16[272,512]{1,0:T(8,128)(2,1)}, bf16[272,512]{1,0:T(8,128)(2,1)S(1)}, u32[]{:S(2)}, u32[]{:S(2)}) collective-permute-start(bf16[272,512]{1,0:T(8,128)(2,1)} %get-tuple-element.64), channel_id=1, source_target_pairs={{0,16},{8,24},{16,0},{24,8},{1,17},{9,25},{17,1},{25,9},{2,18},{10... | collective-permute-start | bytes 835592 | tf_op jit(solution)/shard_map/ppermute | solution.py:43
  18.4 1.8 %collective-permute-start = (bf16[256,512]{1,0:T(8,128)(2,1)}, bf16[256,512]{1,0:T(8,128)(2,1)S(1)}, u32[]{:S(2)}, u32[]{:S(2)}) collective-permute-start(bf16[256,512]{1,0:T(8,128)(2,1)} %get-tuple-element.49), channel_id=1, source_target_pairs={{0,16},{8,24},{16,0},{24,8},{1,17},{9,25},{17,1},{25,9},{2,18},{10... | collective-permute-start | bytes 786440 | tf_op jit(solution)/shard_map/ppermute | solution.py:43
  20.2 10.0 %collective-permute-start.4 = (bf16[256,512]{1,0:T(8,128)(2,1)}, bf16[256,512]{1,0:T(8,128)(2,1)S(1)}, u32[]{:S(2)}, u32[]{:S(2)}) collective-permute-start(bf16[256,512]{1,0:T(8,128)(2,1)} %get-tuple-element.55), channel_id=1, source_target_pairs={{0,8},{8,16},{16,24},{24,0},{1,9},{9,17},{17,25},{25,1},{2,10},{10... | collective-permute-start | bytes 786440 | tf_op jit(solution)/shard_map/ppermute | solution.py:43
  30.1 1.5 collective-permute-start.5
  32.5 5.9 %shard_map.111 = (bf16[4,256,512]{2,1,0:T(8,128)(2,1)}, f32[4,256,128]{2,1,0:T(8,128)}, f32[4,16,256]{2,1,0:T(8,128)}, f32[4,256,128]{2,1,0:T(8,128)}, f32[8,128]{1,0:T(8,128)}) custom-call(s32[4]{0:T(128)} %lengths.5, f32[32]{0:T(128)} %decay.1, bf16[16,1024]{1,0:T(8,128)(2,1)} %copy-done.17, bf16[16,1024]{1,0:T(8,128)(2,1)} %copy-done.18, ...), custom_call_target="tpu_custom_call" | custom-call | flops 2147483648 | bytes 8388608 | tf_op jit(solution)/shard_map/pallas_call | solution.py:30
  38.6 1.4 collective-permute-done.5.nxt
  40.7 7.8 %shard_map.112 = (bf16[4,256,512]{2,1,0:T(8,128)(2,1)}, bf16[4,256,512]{2,1,0:T(8,128)(2,1)}, bf16[8,48,512]{2,1,0:T(8,128)(2,1)}) custom-call(s32[4]{0:T(128)} %lengths.5, bf16[256,512]{1,0:T(8,128)(2,1)} %get-tuple-element.54.own, bf16[256,512]{1,0:T(8,128)(2,1)} %copy-done.15, bf16[256,512]{1,0:T(8,128)(2,1)} %copy-done.16, bf16[256,512]{1,0:T(8,128)(2,1)} %copy-done.8, ...), custom_call_target="tpu_custom_call" | custom-call | flops 3221225472 | bytes 10485760 | tf_op jit(solution)/shard_map/pallas_call | solution.py:30
  48.5 9.3 %all-to-all-start = ((bf16[8,48,512]{2,1,0:T(8,128)(2,1)}), bf16[8,48,512]{2,1,0:T(8,128)(2,1)S(1)}, u32[]{:S(2)}, u32[]{:S(2)}) async-start(bf16[8,48,512]{2,1,0:T(8,128)(2,1)} %get-tuple-element.71), calls=%async_computation | async-start | bytes 786432 | tf_op jit(solution)/shard_map/all_to_all | solution.py:564
  57.8 2.2 %shard_map.110 = (bf16[256,512]{1,0:T(8,128)(2,1)}, bf16[256,512]{1,0:T(8,128)(2,1)}, bf16[256,512]{1,0:T(8,128)(2,1)}, bf16[256,512]{1,0:T(8,128)(2,1)}) custom-call(bf16[256,2048]{1,0:T(8,128)(2,1)} %g_any.1, bf16[256,512]{1,0:T(8,128)(2,1)} %copy-done.8), custom_call_target="tpu_custom_call" | custom-call | bytes 2097152 | tf_op jit(solution)/shard_map/pallas_call | solution.py:30
  60.0 1.0 collective-permute-start.1
  61.0 2.3 %collective-permute-start.2 = (bf16[256,512]{1,0:T(8,128)(2,1)}, bf16[256,512]{1,0:T(8,128)(2,1)S(1)}, u32[]{:S(2)}, u32[]{:S(2)}) collective-permute-start(bf16[256,512]{1,0:T(8,128)(2,1)} %get-tuple-element.52), channel_id=1, source_target_pairs={{0,24},{8,0},{16,8},{24,16},{1,25},{9,1},{17,9},{25,17},{2,26},{10... | collective-permute-start | bytes 786440 | tf_op jit(solution)/shard_map/ppermute | solution.py:43
  63.8 12.0 %all-to-all-done.t_ref = bf16[8,48,512]{2,1,0:T(8,128)(2,1)S(1)} async-done(((bf16[8,48,512]{2,1,0:T(8,128)(2,1)}), bf16[8,48,512]{2,1,0:T(8,128)(2,1)S(1)}, u32[]{:S(2)}, u32[]{:S(2)}) %all-to-all-start) | async-done | bytes 393248 | tf_op jit(solution)/shard_map/all_to_all | solution.py:564
  76.6 1.8 %shard_map.113.refs_0_ = bf16[8,32,512]{2,1,0:T(8,128)(2,1)} custom-call(bf16[8,48,512]{2,1,0:T(8,128)(2,1)} %copy-done.6), custom_call_target="tpu_custom_call" | custom-call | bytes 1048576 | tf_op jit(solution)/shard_map/pallas_call | solution.py:30
  78.3 3.6 %all-to-all-start.1 = ((bf16[8,32,512]{2,1,0:T(8,128)(2,1)}), bf16[8,32,512]{2,1,0:T(8,128)(2,1)S(1)}, u32[]{:S(2)}, u32[]{:S(2)}) async-start(bf16[8,32,512]{2,1,0:T(8,128)(2,1)} %shard_map.113.refs_0_), calls=%async_computation.1 | async-start | bytes 524288 | tf_op jit(solution)/shard_map/all_to_all | solution.py:577
  82.8 6.0 %shard_map.114.y_hbm = f32[4,256,512]{2,1,0:T(8,128)} custom-call(s32[4]{0:T(128)} %lengths.5, f32[32]{0:T(128)} %skip.1, bf16[4,256,512]{2,1,0:T(8,128)(2,1)} %get-tuple-element.68.xs_hbm, bf16[4,256,512]{2,1,0:T(8,128)(2,1)} %get-tuple-element.65.bc_ref.bc_hbm, f32[4,256,128]{2,1,0:T(8,128)} %get-tuple-element.66.cols_ref.cols_hbm, ...), custom_call_target="tpu_custom_call" | custom-call | flops 6442450944 | bytes 16777216 | tf_op jit(solution)/shard_map/pallas_call | solution.py:30
  88.9 3.3 %all-to-all-done.1 = bf16[8,32,512]{2,1,0:T(8,128)(2,1)S(1)} async-done(((bf16[8,32,512]{2,1,0:T(8,128)(2,1)}), bf16[8,32,512]{2,1,0:T(8,128)(2,1)S(1)}, u32[]{:S(2)}, u32[]{:S(2)}) %all-to-all-start.1) | async-done | bytes 262176 | tf_op jit(solution)/shard_map/all_to_all | solution.py:577
  92.9 5.5 %shard_map.115 = (bf16[256,512]{1,0:T(8,128)(2,1)}, bf16[256,512]{1,0:T(8,128)(2,1)}, bf16[256,512]{1,0:T(8,128)(2,1)}, bf16[256,512]{1,0:T(8,128)(2,1)}) custom-call(bf16[256,512]{1,0:T(8,128)(2,1)} %get-tuple-element.50.own, bf16[256,512]{1,0:T(8,128)(2,1)} %copy-done.9, bf16[256,512]{1,0:T(8,128)(2,1)} %copy-done.10, bf16[256,512]{1,0:T(8,128)(2,1)} %copy-done.11, ...), custom_call_target="tpu_custom_call" | custom-call | flops 2147483648 | bytes 6291456 | tf_op jit(solution)/shard_map/pallas_call | solution.py:30
  98.4 1.7 %collective-permute-start.19 = (bf16[256,512]{1,0:T(8,128)(2,1)}, bf16[256,512]{1,0:T(8,128)(2,1)S(1)}, u32[]{:S(2)}, u32[]{:S(2)}) collective-permute-start(bf16[256,512]{1,0:T(8,128)(2,1)} %get-tuple-element.76.refs_0_), channel_id=1, source_target_pairs={{0,8},{8,16},{16,24},{24,0},{1,9},{9,17},{17,25},{25,1},{2,10},{10... | collective-permute-start | bytes 786440 | tf_op jit(solution)/shard_map/ppermute | solution.py:43
  100.1 1.6 collective-permute-start.23
  101.8 1.9 %collective-permute-start.22 = (bf16[256,512]{1,0:T(8,128)(2,1)}, bf16[256,512]{1,0:T(8,128)(2,1)S(1)}, u32[]{:S(2)}, u32[]{:S(2)}) collective-permute-start(bf16[256,512]{1,0:T(8,128)(2,1)} %get-tuple-element.75.after.refs_4_), channel_id=1, source_target_pairs={{0,8},{8,16},{16,24},{24,0},{1,9},{9,17},{17,25},{25,1},{2,10},{10... | collective-permute-start | bytes 786440 | tf_op jit(solution)/shard_map/ppermute | solution.py:43
  104.1 4.9 %collective-permute-done.19.refs_10_.refs_1_ = bf16[256,512]{1,0:T(8,128)(2,1)S(1)} collective-permute-done((bf16[256,512]{1,0:T(8,128)(2,1)}, bf16[256,512]{1,0:T(8,128)(2,1)S(1)}, u32[]{:S(2)}, u32[]{:S(2)}) %collective-permute-start.19) | collective-permute-done | bytes 262176 | tf_op jit(solution)/shard_map/ppermute | solution.py:43
  109.5 1.6 collective-permute-start.21
  111.1 4.0 %collective-permute-done.20.refs_11_.refs_2_ = bf16[256,512]{1,0:T(8,128)(2,1)S(1)} collective-permute-done((bf16[256,512]{1,0:T(8,128)(2,1)}, bf16[256,512]{1,0:T(8,128)(2,1)S(1)}, u32[]{:S(2)}, u32[]{:S(2)}) %collective-permute-start.20) | collective-permute-done | bytes 262176 | tf_op jit(solution)/shard_map/ppermute | solution.py:43
  115.2 2.8 %collective-permute-start.24 = (bf16[256,512]{1,0:T(8,128)(2,1)S(1)}, bf16[256,512]{1,0:T(8,128)(2,1)S(1)}, u32[]{:S(2)}, u32[]{:S(2)}) collective-permute-start(bf16[256,512]{1,0:T(8,128)(2,1)S(1)} %collective-permute-done.23.refs_14_.refs_6_), channel_id=1, source_target_pairs={{0,24},{8,0},{16,8},{24,16},{1,25},{9,1},{17,9},{25,17},{2,26},{10... | collective-permute-start | bytes 786440 | tf_op jit(solution)/shard_map/ppermute | solution.py:43
  118.0 2.2 %copy-done = bf16[16384,128]{1,0:T(8,128)(2,1)S(1)} copy-done((bf16[16384,128]{1,0:T(8,128)(2,1)S(1)}, bf16[16384,128]{1,0:T(8,128)(2,1)}, u32[]{:S(2)}) %copy-start) | copy-done | bytes 4194328
  120.1 0.9 copy-done.1
  122.1 2.0 %collective-permute-start.16 = (bf16[256,512]{1,0:T(8,128)(2,1)S(1)}, bf16[256,512]{1,0:T(8,128)(2,1)S(1)}, u32[]{:S(2)}, u32[]{:S(2)}) collective-permute-start(bf16[256,512]{1,0:T(8,128)(2,1)S(1)} %copy-done.4), channel_id=1, source_target_pairs={{0,8},{8,16},{16,24},{24,0},{1,9},{9,17},{17,25},{25,1},{2,10},{10... | collective-permute-start | bytes 786440 | tf_op jit(solution)/shard_map/ppermute | solution.py:43
  124.2 1.8 %collective-permute-done.21.refs_12_.refs_3_ = bf16[256,512]{1,0:T(8,128)(2,1)S(1)} collective-permute-done((bf16[256,512]{1,0:T(8,128)(2,1)S(1)}, bf16[256,512]{1,0:T(8,128)(2,1)S(1)}, u32[]{:S(2)}, u32[]{:S(2)}) %collective-permute-start.21) | collective-permute-done | bytes 262176 | tf_op jit(solution)/shard_map/ppermute | solution.py:43
  125.9 1.4 collective-permute-start.18
  127.3 3.2 %shard_map.119 = (bf16[4,512,128]{2,1,0:T(8,128)(2,1)S(1)}, f32[4,512,128]{2,1,0:T(8,128)S(1)}) custom-call(bf16[256,512]{1,0:T(8,128)(2,1)S(1)} %copy-done.5, bf16[256,512]{1,0:T(8,128)(2,1)S(1)} %collective-permute-done.19.refs_10_.refs_1_, bf16[256,512]{1,0:T(8,128)(2,1)S(1)} %collective-permute-done.20.refs_11_.refs_2_, ...), custom_call_target="tpu_custom_call" | custom-call | flops 3221225472 | bytes 8388608 | tf_op jit(solution)/shard_map/pallas_call | solution.py:30
  130.7 1.9 %collective-permute-done.15.refs_3_ = bf16[256,512]{1,0:T(8,128)(2,1)S(1)} collective-permute-done((bf16[256,512]{1,0:T(8,128)(2,1)S(1)}, bf16[256,512]{1,0:T(8,128)(2,1)S(1)}, u32[]{:S(2)}, u32[]{:S(2)}) %collective-permute-start.15) | collective-permute-done | bytes 262176 | tf_op jit(solution)/shard_map/ppermute | solution.py:43
  132.5 0.8 collective-permute-done.18.refs_7_
  133.3 3.2 %shard_map.117 = (bf16[4,512,128]{2,1,0:T(8,128)(2,1)S(1)}, f32[4,512,128]{2,1,0:T(8,128)S(1)}) custom-call(bf16[256,512]{1,0:T(8,128)(2,1)S(1)} %copy-done.3, bf16[256,512]{1,0:T(8,128)(2,1)S(1)} %collective-permute-done.13.refs_1_, bf16[256,512]{1,0:T(8,128)(2,1)S(1)} %collective-permute-done.14.refs_2_, ...), custom_call_target="tpu_custom_call" | custom-call | flops 3221225472 | bytes 8388608 | tf_op jit(solution)/shard_map/pallas_call | solution.py:30
  136.8 1.6 collective-permute-start.30
  138.9 2.1 %collective-permute-start.32 = (bf16[512,128]{1,0:T(8,128)(2,1)S(1)}, bf16[512,128]{1,0:T(8,128)(2,1)S(1)}, u32[]{:S(2)}, u32[]{:S(2)}) collective-permute-start(bf16[512,128]{1,0:T(8,128)(2,1)S(1)} %get-tuple-element.88), channel_id=1, source_target_pairs={{0,4},{2,6},{4,0},{6,2},{1,5},{3,7},{5,1},{7,3},{8,12},{10,14},{12... | collective-permute-start | bytes 393224 | tf_op jit(solution)/shard_map/ppermute | solution.py:43
  141.1 0.8 collective-permute-start.26
  141.9 1.3 collective-permute-start.27
  143.2 2.1 %collective-permute-start.28 = (bf16[512,128]{1,0:T(8,128)(2,1)S(1)}, bf16[512,128]{1,0:T(8,128)(2,1)S(1)}, u32[]{:S(2)}, u32[]{:S(2)}) collective-permute-start(bf16[512,128]{1,0:T(8,128)(2,1)S(1)} %get-tuple-element.82), channel_id=1, source_target_pairs={{0,4},{2,6},{4,0},{6,2},{1,5},{3,7},{5,1},{7,3},{8,12},{10,14},{12... | collective-permute-start | bytes 393224 | tf_op jit(solution)/shard_map/ppermute | solution.py:43
  145.3 2.9 %collective-permute-done.32.b3 = bf16[512,128]{1,0:T(8,128)(2,1)S(1)} collective-permute-done((bf16[512,128]{1,0:T(8,128)(2,1)S(1)}, bf16[512,128]{1,0:T(8,128)(2,1)S(1)}, u32[]{:S(2)}, u32[]{:S(2)}) %collective-permute-start.32) | collective-permute-done | bytes 131104 | tf_op jit(solution)/shard_map/ppermute | solution.py:43
  148.2 1.5 collective-permute-done.26.a1
  149.8 3.3 %collective-permute-done.28.a3 = bf16[512,128]{1,0:T(8,128)(2,1)S(1)} collective-permute-done((bf16[512,128]{1,0:T(8,128)(2,1)S(1)}, bf16[512,128]{1,0:T(8,128)(2,1)S(1)}, u32[]{:S(2)}, u32[]{:S(2)}) %collective-permute-start.28) | collective-permute-done | bytes 131104 | tf_op jit(solution)/shard_map/ppermute | solution.py:43
  153.6 2.9 %collective-permute-start.34 = (bf16[256,128]{1,0:T(8,128)(2,1)S(1)}, bf16[256,128]{1,0:T(8,128)(2,1)S(1)}, u32[]{:S(2)}, u32[]{:S(2)}) collective-permute-start(bf16[256,128]{1,0:T(8,128)(2,1)S(1)} %get-tuple-element.91), channel_id=1, source_target_pairs={{0,24},{8,0},{16,8},{24,16},{1,25},{9,1},{17,9},{25,17},{2,26},{10... | collective-permute-start | bytes 196616 | tf_op jit(solution)/shard_map/ppermute | solution.py:43
  156.5 2.2 %collective-permute-done.33.prev = bf16[256,128]{1,0:T(8,128)(2,1)S(1)} collective-permute-done((bf16[256,128]{1,0:T(8,128)(2,1)S(1)}, bf16[256,128]{1,0:T(8,128)(2,1)S(1)}, u32[]{:S(2)}, u32[]{:S(2)}) %collective-permute-start.33) | collective-permute-done | bytes 65568 | tf_op jit(solution)/shard_map/ppermute | solution.py:43
  158.8 3.5 %collective-permute-done.35.far = bf16[256,128]{1,0:T(8,128)(2,1)S(1)} collective-permute-done((bf16[256,128]{1,0:T(8,128)(2,1)S(1)}, bf16[256,128]{1,0:T(8,128)(2,1)S(1)}, u32[]{:S(2)}, u32[]{:S(2)}) %collective-permute-start.35) | collective-permute-done | bytes 65568 | tf_op jit(solution)/shard_map/ppermute | solution.py:43
  162.3 0.8 shard_map.122
  (87 shorter events, 11.5 us)
Async XLA Ops:
  6.5 85.6 %all-gather.3.cloned.1.call-start = ((), (), s32[]{:S(2)}) async-start(), calls=%async_computation.2 | async-start | bytes 4718592 | tf_op jit(solution)/shard_map/all_gather | solution.py:495
  10.5 19.6 %collective-permute-start.10 = (bf16[272,512]{1,0:T(8,128)(2,1)}, bf16[272,512]{1,0:T(8,128)(2,1)S(1)}, u32[]{:S(2)}, u32[]{:S(2)}) collective-permute-start(bf16[272,512]{1,0:T(8,128)(2,1)} %get-tuple-element.62), channel_id=1, source_target_pairs={{0,8},{8,16},{16,24},{24,0},{1,9},{9,17},{17,25},{25,1},{2,10},{10... | collective-permute-start | bytes 835592 | tf_op jit(solution)/shard_map/ppermute | solution.py:43
  12.1 19.6 %collective-permute-start.11 = (bf16[272,512]{1,0:T(8,128)(2,1)}, bf16[272,512]{1,0:T(8,128)(2,1)S(1)}, u32[]{:S(2)}, u32[]{:S(2)}) collective-permute-start(bf16[272,512]{1,0:T(8,128)(2,1)} %get-tuple-element.63), channel_id=1, source_target_pairs={{0,24},{8,0},{16,8},{24,16},{1,25},{9,1},{17,9},{25,17},{2,26},{10... | collective-permute-start | bytes 835592 | tf_op jit(solution)/shard_map/ppermute | solution.py:43
  13.8 17.8 %collective-permute-start.12 = (bf16[272,512]{1,0:T(8,128)(2,1)}, bf16[272,512]{1,0:T(8,128)(2,1)S(1)}, u32[]{:S(2)}, u32[]{:S(2)}) collective-permute-start(bf16[272,512]{1,0:T(8,128)(2,1)} %get-tuple-element.64), channel_id=1, source_target_pairs={{0,16},{8,24},{16,0},{24,8},{1,17},{9,25},{17,1},{25,9},{2,18},{10... | collective-permute-start | bytes 835592 | tf_op jit(solution)/shard_map/ppermute | solution.py:43
  15.6 1.3 collective-permute-start.6
  16.3 1.4 collective-permute-start.7
  17.0 14.7 %copy-start.17 = (bf16[16,1024]{1,0:T(8,128)(2,1)}, bf16[16,1024]{1,0:T(8,128)(2,1)S(1)}, u32[]{:S(2)}) copy-start(bf16[16,1024]{1,0:T(8,128)(2,1)S(1)} %collective-permute-done.6.h0) | copy-start | bytes 98308
  17.0 1.4 collective-permute-start.8
  17.7 14.0 %copy-start.18 = (bf16[16,1024]{1,0:T(8,128)(2,1)}, bf16[16,1024]{1,0:T(8,128)(2,1)S(1)}, u32[]{:S(2)}) copy-start(bf16[16,1024]{1,0:T(8,128)(2,1)S(1)} %collective-permute-done.7.h1) | copy-start | bytes 98308
  17.7 2.5 %collective-permute-start.9 = (bf16[16,1024]{1,0:T(8,128)(2,1)}, bf16[16,1024]{1,0:T(8,128)(2,1)S(1)}, u32[]{:S(2)}, u32[]{:S(2)}) collective-permute-start(bf16[16,1024]{1,0:T(8,128)(2,1)} %get-tuple-element.60), channel_id=1, source_target_pairs={{24,56},{56,88},{88,120},{120,152},{152,184},{184,216},{216,248},{... | collective-permute-start | bytes 98312 | tf_op jit(solution)/shard_map/ppermute | solution.py:510
  18.3 13.3 %copy-start.19 = (bf16[16,1024]{1,0:T(8,128)(2,1)}, bf16[16,1024]{1,0:T(8,128)(2,1)S(1)}, u32[]{:S(2)}) copy-start(bf16[16,1024]{1,0:T(8,128)(2,1)S(1)} %collective-permute-done.8.h2) | copy-start | bytes 98308
  18.4 20.0 %collective-permute-start = (bf16[256,512]{1,0:T(8,128)(2,1)}, bf16[256,512]{1,0:T(8,128)(2,1)S(1)}, u32[]{:S(2)}, u32[]{:S(2)}) collective-permute-start(bf16[256,512]{1,0:T(8,128)(2,1)} %get-tuple-element.49), channel_id=1, source_target_pairs={{0,16},{8,24},{16,0},{24,8},{1,17},{9,25},{17,1},{25,9},{2,18},{10... | collective-permute-start | bytes 786440 | tf_op jit(solution)/shard_map/ppermute | solution.py:43
  20.2 11.5 %copy-start.20 = (bf16[16,1024]{1,0:T(8,128)(2,1)}, bf16[16,1024]{1,0:T(8,128)(2,1)S(1)}, u32[]{:S(2)}) copy-start(bf16[16,1024]{1,0:T(8,128)(2,1)S(1)} %collective-permute-done.9.h3) | copy-start | bytes 98308
  20.2 18.4 %collective-permute-start.4 = (bf16[256,512]{1,0:T(8,128)(2,1)}, bf16[256,512]{1,0:T(8,128)(2,1)S(1)}, u32[]{:S(2)}, u32[]{:S(2)}) collective-permute-start(bf16[256,512]{1,0:T(8,128)(2,1)} %get-tuple-element.55), channel_id=1, source_target_pairs={{0,8},{8,16},{16,24},{24,0},{1,9},{9,17},{17,25},{25,1},{2,10},{10... | collective-permute-start | bytes 786440 | tf_op jit(solution)/shard_map/ppermute | solution.py:43
  30.1 1.6 copy-start.12
  30.1 9.9 %collective-permute-start.5 = (bf16[256,512]{1,0:T(8,128)(2,1)}, bf16[256,512]{1,0:T(8,128)(2,1)S(1)}, u32[]{:S(2)}, u32[]{:S(2)}) collective-permute-start(bf16[256,512]{1,0:T(8,128)(2,1)} %get-tuple-element.56), channel_id=1, source_target_pairs={{0,24},{8,0},{16,8},{24,16},{1,25},{9,1},{17,9},{25,17},{2,26},{10... | collective-permute-start | bytes 786440 | tf_op jit(solution)/shard_map/ppermute | solution.py:43
  38.4 1.6 copy-start.8
  48.5 27.3 %all-to-all-start = ((bf16[8,48,512]{2,1,0:T(8,128)(2,1)}), bf16[8,48,512]{2,1,0:T(8,128)(2,1)S(1)}, u32[]{:S(2)}, u32[]{:S(2)}) async-start(bf16[8,48,512]{2,1,0:T(8,128)(2,1)} %get-tuple-element.71), calls=%async_computation | async-start | bytes 786432 | tf_op jit(solution)/shard_map/all_to_all | solution.py:564
  60.0 21.9 %collective-permute-start.1 = (bf16[256,512]{1,0:T(8,128)(2,1)}, bf16[256,512]{1,0:T(8,128)(2,1)S(1)}, u32[]{:S(2)}, u32[]{:S(2)}) collective-permute-start(bf16[256,512]{1,0:T(8,128)(2,1)} %get-tuple-element.51), channel_id=1, source_target_pairs={{0,8},{8,16},{16,24},{24,0},{1,9},{9,17},{17,25},{25,1},{2,10},{10... | collective-permute-start | bytes 786440 | tf_op jit(solution)/shard_map/ppermute | solution.py:43
  61.0 20.9 %collective-permute-start.2 = (bf16[256,512]{1,0:T(8,128)(2,1)}, bf16[256,512]{1,0:T(8,128)(2,1)S(1)}, u32[]{:S(2)}, u32[]{:S(2)}) collective-permute-start(bf16[256,512]{1,0:T(8,128)(2,1)} %get-tuple-element.52), channel_id=1, source_target_pairs={{0,24},{8,0},{16,8},{24,16},{1,25},{9,1},{17,9},{25,17},{2,26},{10... | collective-permute-start | bytes 786440 | tf_op jit(solution)/shard_map/ppermute | solution.py:43
  63.3 18.6 %collective-permute-start.3 = (bf16[256,512]{1,0:T(8,128)(2,1)}, bf16[256,512]{1,0:T(8,128)(2,1)S(1)}, u32[]{:S(2)}, u32[]{:S(2)}) collective-permute-start(bf16[256,512]{1,0:T(8,128)(2,1)} %get-tuple-element.53), channel_id=1, source_target_pairs={{0,16},{8,24},{16,0},{24,8},{1,17},{9,25},{17,1},{25,9},{2,18},{10... | collective-permute-start | bytes 786440 | tf_op jit(solution)/shard_map/ppermute | solution.py:43
  78.3 13.8 %all-to-all-start.1 = ((bf16[8,32,512]{2,1,0:T(8,128)(2,1)}), bf16[8,32,512]{2,1,0:T(8,128)(2,1)S(1)}, u32[]{:S(2)}, u32[]{:S(2)}) async-start(bf16[8,32,512]{2,1,0:T(8,128)(2,1)} %shard_map.113.refs_0_), calls=%async_computation.1 | async-start | bytes 524288 | tf_op jit(solution)/shard_map/all_to_all | solution.py:577
  98.4 10.7 %collective-permute-start.19 = (bf16[256,512]{1,0:T(8,128)(2,1)}, bf16[256,512]{1,0:T(8,128)(2,1)S(1)}, u32[]{:S(2)}, u32[]{:S(2)}) collective-permute-start(bf16[256,512]{1,0:T(8,128)(2,1)} %get-tuple-element.76.refs_0_), channel_id=1, source_target_pairs={{0,8},{8,16},{16,24},{24,0},{1,9},{9,17},{17,25},{25,1},{2,10},{10... | collective-permute-start | bytes 786440 | tf_op jit(solution)/shard_map/ppermute | solution.py:43
  100.1 9.5 %collective-permute-start.23 = (bf16[256,512]{1,0:T(8,128)(2,1)}, bf16[256,512]{1,0:T(8,128)(2,1)S(1)}, u32[]{:S(2)}, u32[]{:S(2)}) collective-permute-start(bf16[256,512]{1,0:T(8,128)(2,1)} %get-tuple-element.75.after.refs_4_), channel_id=1, source_target_pairs={{0,24},{8,0},{16,8},{24,16},{1,25},{9,1},{17,9},{25,17},{2,26},{10... | collective-permute-start | bytes 786440 | tf_op jit(solution)/shard_map/ppermute | solution.py:43
  101.7 13.5 %collective-permute-start.20 = (bf16[256,512]{1,0:T(8,128)(2,1)}, bf16[256,512]{1,0:T(8,128)(2,1)S(1)}, u32[]{:S(2)}, u32[]{:S(2)}) collective-permute-start(bf16[256,512]{1,0:T(8,128)(2,1)} %get-tuple-element.76.refs_0_), channel_id=1, source_target_pairs={{0,24},{8,0},{16,8},{24,16},{1,25},{9,1},{17,9},{25,17},{2,26},{10... | collective-permute-start | bytes 786440 | tf_op jit(solution)/shard_map/ppermute | solution.py:43
  101.8 19.6 %collective-permute-start.22 = (bf16[256,512]{1,0:T(8,128)(2,1)}, bf16[256,512]{1,0:T(8,128)(2,1)S(1)}, u32[]{:S(2)}, u32[]{:S(2)}) collective-permute-start(bf16[256,512]{1,0:T(8,128)(2,1)} %get-tuple-element.75.after.refs_4_), channel_id=1, source_target_pairs={{0,8},{8,16},{16,24},{24,0},{1,9},{9,17},{17,25},{25,1},{2,10},{10... | collective-permute-start | bytes 786440 | tf_op jit(solution)/shard_map/ppermute | solution.py:43
  103.7 18.4 %collective-permute-start.13 = (bf16[256,512]{1,0:T(8,128)(2,1)}, bf16[256,512]{1,0:T(8,128)(2,1)S(1)}, u32[]{:S(2)}, u32[]{:S(2)}) collective-permute-start(bf16[256,512]{1,0:T(8,128)(2,1)} %get-tuple-element.73.refs_0_), channel_id=1, source_target_pairs={{0,8},{8,16},{16,24},{24,0},{1,9},{9,17},{17,25},{25,1},{2,10},{10... | collective-permute-start | bytes 786440 | tf_op jit(solution)/shard_map/ppermute | solution.py:43
  109.1 15.0 %collective-permute-start.17 = (bf16[256,512]{1,0:T(8,128)(2,1)}, bf16[256,512]{1,0:T(8,128)(2,1)S(1)}, u32[]{:S(2)}, u32[]{:S(2)}) collective-permute-start(bf16[256,512]{1,0:T(8,128)(2,1)} %get-tuple-element.74.refs_4_), channel_id=1, source_target_pairs={{0,24},{8,0},{16,8},{24,16},{1,25},{9,1},{17,9},{25,17},{2,26},{10... | collective-permute-start | bytes 786440 | tf_op jit(solution)/shard_map/ppermute | solution.py:43
  109.5 16.4 %collective-permute-start.21 = (bf16[256,512]{1,0:T(8,128)(2,1)S(1)}, bf16[256,512]{1,0:T(8,128)(2,1)S(1)}, u32[]{:S(2)}, u32[]{:S(2)}) collective-permute-start(bf16[256,512]{1,0:T(8,128)(2,1)S(1)} %collective-permute-done.19.refs_10_.refs_1_), channel_id=1, source_target_pairs={{0,8},{8,16},{16,24},{24,0},{1,9},{9,17},{17,25},{25,1},{2,10},{10... | collective-permute-start | bytes 786440 | tf_op jit(solution)/shard_map/ppermute | solution.py:43
  115.2 12.2 %collective-permute-start.24 = (bf16[256,512]{1,0:T(8,128)(2,1)S(1)}, bf16[256,512]{1,0:T(8,128)(2,1)S(1)}, u32[]{:S(2)}, u32[]{:S(2)}) collective-permute-start(bf16[256,512]{1,0:T(8,128)(2,1)S(1)} %collective-permute-done.23.refs_14_.refs_6_), channel_id=1, source_target_pairs={{0,24},{8,0},{16,8},{24,16},{1,25},{9,1},{17,9},{25,17},{2,26},{10... | collective-permute-start | bytes 786440 | tf_op jit(solution)/shard_map/ppermute | solution.py:43
  118.0 2.2 %copy-start = (bf16[16384,128]{1,0:T(8,128)(2,1)S(1)}, bf16[16384,128]{1,0:T(8,128)(2,1)}, u32[]{:S(2)}) copy-start(bf16[16384,128]{1,0:T(8,128)(2,1)} %all-gather.3.cloned.1.call-done) | copy-start | bytes 12582916
  121.1 6.2 %copy-start.2 = (f32[2048]{0:T(1024)S(1)}, f32[2048]{0:T(1024)}, u32[]{:S(2)}) copy-start(f32[2048]{0:T(1024)} %param.19) | copy-start | bytes 24580
  121.1 6.2 %copy-start.5 = (bf16[256,512]{1,0:T(8,128)(2,1)S(1)}, bf16[256,512]{1,0:T(8,128)(2,1)}, u32[]{:S(2)}) copy-start(bf16[256,512]{1,0:T(8,128)(2,1)} %get-tuple-element.76.refs_0_) | copy-start | bytes 786436
  122.0 8.6 %collective-permute-start.14 = (bf16[256,512]{1,0:T(8,128)(2,1)S(1)}, bf16[256,512]{1,0:T(8,128)(2,1)S(1)}, u32[]{:S(2)}, u32[]{:S(2)}) collective-permute-start(bf16[256,512]{1,0:T(8,128)(2,1)S(1)} %copy-done.3), channel_id=1, source_target_pairs={{0,24},{8,0},{16,8},{24,16},{1,25},{9,1},{17,9},{25,17},{2,26},{10... | collective-permute-start | bytes 786440 | tf_op jit(solution)/shard_map/ppermute | solution.py:43
  122.1 8.5 %collective-permute-start.16 = (bf16[256,512]{1,0:T(8,128)(2,1)S(1)}, bf16[256,512]{1,0:T(8,128)(2,1)S(1)}, u32[]{:S(2)}, u32[]{:S(2)}) collective-permute-start(bf16[256,512]{1,0:T(8,128)(2,1)S(1)} %copy-done.4), channel_id=1, source_target_pairs={{0,8},{8,16},{16,24},{24,0},{1,9},{9,17},{17,25},{25,1},{2,10},{10... | collective-permute-start | bytes 786440 | tf_op jit(solution)/shard_map/ppermute | solution.py:43
  124.1 8.4 %collective-permute-start.15 = (bf16[256,512]{1,0:T(8,128)(2,1)S(1)}, bf16[256,512]{1,0:T(8,128)(2,1)S(1)}, u32[]{:S(2)}, u32[]{:S(2)}) collective-permute-start(bf16[256,512]{1,0:T(8,128)(2,1)S(1)} %collective-permute-done.13.refs_1_), channel_id=1, source_target_pairs={{0,8},{8,16},{16,24},{24,0},{1,9},{9,17},{17,25},{25,1},{2,10},{10... | collective-permute-start | bytes 786440 | tf_op jit(solution)/shard_map/ppermute | solution.py:43
  125.9 7.4 %collective-permute-start.18 = (bf16[256,512]{1,0:T(8,128)(2,1)S(1)}, bf16[256,512]{1,0:T(8,128)(2,1)S(1)}, u32[]{:S(2)}, u32[]{:S(2)}) collective-permute-start(bf16[256,512]{1,0:T(8,128)(2,1)S(1)} %collective-permute-done.17.refs_6_), channel_id=1, source_target_pairs={{0,24},{8,0},{16,8},{24,16},{1,25},{9,1},{17,9},{25,17},{2,26},{10... | collective-permute-start | bytes 786440 | tf_op jit(solution)/shard_map/ppermute | solution.py:43
  130.6 6.1 %collective-permute-start.29 = (bf16[4,512,128]{2,1,0:T(8,128)(2,1)S(1)}, bf16[4,512,128]{2,1,0:T(8,128)(2,1)S(1)}, u32[]{:S(2)}, u32[]{:S(2)}) collective-permute-start(bf16[4,512,128]{2,1,0:T(8,128)(2,1)S(1)} %get-tuple-element.84), channel_id=1, source_target_pairs={{0,1},{1,0},{2,3},{3,2},{4,5},{5,4},{6,7},{7,6},{8,9},{9,8},{10,11... | collective-permute-start | bytes 1572872 | tf_op jit(solution)/shard_map/ppermute | solution.py:43
  136.6 4.4 %collective-permute-start.25 = (bf16[4,512,128]{2,1,0:T(8,128)(2,1)S(1)}, bf16[4,512,128]{2,1,0:T(8,128)(2,1)S(1)}, u32[]{:S(2)}, u32[]{:S(2)}) collective-permute-start(bf16[4,512,128]{2,1,0:T(8,128)(2,1)S(1)} %get-tuple-element.78), channel_id=1, source_target_pairs={{0,1},{1,0},{2,3},{3,2},{4,5},{5,4},{6,7},{7,6},{8,9},{9,8},{10,11... | collective-permute-start | bytes 1572872 | tf_op jit(solution)/shard_map/ppermute | solution.py:43
  136.8 6.4 %collective-permute-start.30 = (bf16[512,128]{1,0:T(8,128)(2,1)S(1)}, bf16[512,128]{1,0:T(8,128)(2,1)S(1)}, u32[]{:S(2)}, u32[]{:S(2)}) collective-permute-start(bf16[512,128]{1,0:T(8,128)(2,1)S(1)} %get-tuple-element.86), channel_id=1, source_target_pairs={{0,2},{2,4},{4,6},{6,0},{1,3},{3,5},{5,7},{7,1},{8,10},{10,12},{12... | collective-permute-start | bytes 393224 | tf_op jit(solution)/shard_map/ppermute | solution.py:43
  138.4 6.9 %collective-permute-start.31 = (bf16[512,128]{1,0:T(8,128)(2,1)S(1)}, bf16[512,128]{1,0:T(8,128)(2,1)S(1)}, u32[]{:S(2)}, u32[]{:S(2)}) collective-permute-start(bf16[512,128]{1,0:T(8,128)(2,1)S(1)} %get-tuple-element.87), channel_id=1, source_target_pairs={{0,6},{2,0},{4,2},{6,4},{1,7},{3,1},{5,3},{7,5},{8,14},{10,8},{12,... | collective-permute-start | bytes 393224 | tf_op jit(solution)/shard_map/ppermute | solution.py:43
  138.9 9.3 %collective-permute-start.32 = (bf16[512,128]{1,0:T(8,128)(2,1)S(1)}, bf16[512,128]{1,0:T(8,128)(2,1)S(1)}, u32[]{:S(2)}, u32[]{:S(2)}) collective-permute-start(bf16[512,128]{1,0:T(8,128)(2,1)S(1)} %get-tuple-element.88), channel_id=1, source_target_pairs={{0,4},{2,6},{4,0},{6,2},{1,5},{3,7},{5,1},{7,3},{8,12},{10,14},{12... | collective-permute-start | bytes 393224 | tf_op jit(solution)/shard_map/ppermute | solution.py:43
  141.1 8.6 %collective-permute-start.26 = (bf16[512,128]{1,0:T(8,128)(2,1)S(1)}, bf16[512,128]{1,0:T(8,128)(2,1)S(1)}, u32[]{:S(2)}, u32[]{:S(2)}) collective-permute-start(bf16[512,128]{1,0:T(8,128)(2,1)S(1)} %get-tuple-element.80), channel_id=1, source_target_pairs={{0,2},{2,4},{4,6},{6,0},{1,3},{3,5},{5,7},{7,1},{8,10},{10,12},{12... | collective-permute-start | bytes 393224 | tf_op jit(solution)/shard_map/ppermute | solution.py:43
  141.9 7.9 %collective-permute-start.27 = (bf16[512,128]{1,0:T(8,128)(2,1)S(1)}, bf16[512,128]{1,0:T(8,128)(2,1)S(1)}, u32[]{:S(2)}, u32[]{:S(2)}) collective-permute-start(bf16[512,128]{1,0:T(8,128)(2,1)S(1)} %get-tuple-element.81), channel_id=1, source_target_pairs={{0,6},{2,0},{4,2},{6,4},{1,7},{3,1},{5,3},{7,5},{8,14},{10,8},{12,... | collective-permute-start | bytes 393224 | tf_op jit(solution)/shard_map/ppermute | solution.py:43
  143.2 9.8 %collective-permute-start.28 = (bf16[512,128]{1,0:T(8,128)(2,1)S(1)}, bf16[512,128]{1,0:T(8,128)(2,1)S(1)}, u32[]{:S(2)}, u32[]{:S(2)}) collective-permute-start(bf16[512,128]{1,0:T(8,128)(2,1)S(1)} %get-tuple-element.82), channel_id=1, source_target_pairs={{0,4},{2,6},{4,0},{6,2},{1,5},{3,7},{5,1},{7,3},{8,12},{10,14},{12... | collective-permute-start | bytes 393224 | tf_op jit(solution)/shard_map/ppermute | solution.py:43
  153.2 5.6 %collective-permute-start.33 = (bf16[256,128]{1,0:T(8,128)(2,1)S(1)}, bf16[256,128]{1,0:T(8,128)(2,1)S(1)}, u32[]{:S(2)}, u32[]{:S(2)}) collective-permute-start(bf16[256,128]{1,0:T(8,128)(2,1)S(1)} %get-tuple-element.90), channel_id=1, source_target_pairs={{0,8},{8,16},{16,24},{24,0},{1,9},{9,17},{17,25},{25,1},{2,10},{10... | collective-permute-start | bytes 196616 | tf_op jit(solution)/shard_map/ppermute | solution.py:43
  153.6 5.1 %collective-permute-start.34 = (bf16[256,128]{1,0:T(8,128)(2,1)S(1)}, bf16[256,128]{1,0:T(8,128)(2,1)S(1)}, u32[]{:S(2)}, u32[]{:S(2)}) collective-permute-start(bf16[256,128]{1,0:T(8,128)(2,1)S(1)} %get-tuple-element.91), channel_id=1, source_target_pairs={{0,24},{8,0},{16,8},{24,16},{1,25},{9,1},{17,9},{25,17},{2,26},{10... | collective-permute-start | bytes 196616 | tf_op jit(solution)/shard_map/ppermute | solution.py:43
  156.5 5.8 %collective-permute-start.35 = (bf16[256,128]{1,0:T(8,128)(2,1)S(1)}, bf16[256,128]{1,0:T(8,128)(2,1)S(1)}, u32[]{:S(2)}, u32[]{:S(2)}) collective-permute-start(bf16[256,128]{1,0:T(8,128)(2,1)S(1)} %get-tuple-element.92), channel_id=1, source_target_pairs={{0,16},{8,24},{16,0},{24,8},{1,17},{9,25},{17,1},{25,9},{2,18},{10... | collective-permute-start | bytes 196616 | tf_op jit(solution)/shard_map/ppermute | solution.py:43
  (12 other events, 10.4 us)
Sparse Core Ops, SparseCore 0:
  9.1 65.6 all-gather.2
